TPU v7x, 128 devices: a whole 4x4x4 slice. The times are simulated.
128 devices in a mesh: gx: 32 (over x, z, core), gz: 4 (over y).
Axes of the slice: x: 4, y: 4, z: 4, core: 2. Of those that a mesh axis runs over, the one named last changes fastest.
Arguments:
- vorticity: float32 [3, 128, 16384], P(None, None, ('gx', 'gz')), may hold values from -6 to 6
- position: float32 [3, 128, 16384], P(None, None, ('gx', 'gz')), may hold values from 1 to 6, as said below
- counts: int32 [4, 16384], P(None, ('gx', 'gz')), may hold values from 0 to 32
- owner_ids: int32 [32768, 1], P(('gx', 'gz')), may hold values from 0 to 127; in each aligned block of 256 rows (0 to 255, 256 to 511, ...) at most 4 rows name the same one
- slot_ids: int32 [32768], P(('gx', 'gz')), may hold values from 0 to 1023
- velocity: float32 [128, 16, 64, 3, 128], P('gx', None, 'gz'), may hold values from -6 to 6
Outputs:
- mesh_vorticity: float32 [128, 16, 64, 3, 128], P('gx', None, 'gz')
- stretching: float32 [2, 3, 128, 16384], P(None, None, None, ('gx', 'gz'))
Inputs may be any that keep to these rules, and one draw needn't show every extreme that they name: `owner_ids`: among the routed tiles of one domain no owner is named more than 4 times, a bound that some block reaches. `position`: coordinates 0 and 1 lie in [1, 2), coordinate 2 in [1, 6).
All inputs are finite; a program needn't handle non-finite values.
Results may differ from a plain program's by a relative error of at most 0.0003.
Values sent between devices are 32-bit elements; how exact they have to be, the bound alone decides.
No kernel may reach another device: no remote copies, remote signals or barrier semaphores. Data moves between devices by JAX's collectives and lax.ppermute only.
A program may use at most 256 MiB of HBM per device.

v0:
```python
import jax
import jax.numpy as jnp
from jax import lax
from jax.sharding import PartitionSpec as P


def extended(x, sides, width):
    for axis, dim in sides:
        peers, length = (lax.axis_size(axis), x.shape[dim])
        up = [(i, (i + 1) % peers) for i in range(peers - 1)]
        down = [(j, i) for i, j in up]
        last = lax.slice_in_dim(x, length - width, length, axis=dim)
        initial = lax.slice_in_dim(x, 0, width, axis=dim)
        before = lax.ppermute(last, axis, up)
        after = lax.ppermute(initial, axis, down)
        x = jnp.concatenate([before, x, after], axis=dim)
    return x


def passed_along(value, axis, steps):
    count = lax.axis_size(axis)
    initial, last = (max(0, -steps), min(count, count - steps))
    return lax.ppermute(value, axis, [(source, source + steps) for source in range(initial, last)])


def m4prime(offset):
    radius = jnp.abs(offset)
    inner_part = 1.0 - 2.5 * radius * radius + 1.5 * radius * radius * radius
    outer_part = 0.5 * (2.0 - radius) * (2.0 - radius) * (1.0 - radius)
    return jnp.where(
        radius < 1.0, inner_part, jnp.where(radius < 2.0, outer_part, jnp.zeros_like(radius))
    )


def kernel_table(coords):
    float_type = coords.dtype
    cells = jnp.arange(128, dtype=jnp.int32)
    cell_x = (cells // 32).astype(float_type)
    cell_y = (cells // 8 % 4).astype(float_type)
    cell_z = (cells % 8).astype(float_type)
    return (
        m4prime(cell_x[None, None, :] - coords[:, 0, :, None])
        * m4prime(cell_y[None, None, :] - coords[:, 1, :, None])
        * m4prime(cell_z[None, None, :] - coords[:, 2, :, None])
    )


def cell_offset(center, after, before, stride, per, offset):
    lanes = jnp.arange(128, dtype=jnp.int32)
    digit = lanes // stride % per + offset
    same = jnp.roll(center, -offset * stride, axis=-1)
    ahead = jnp.roll(after, -(offset - per) * stride, axis=-1)
    behind = jnp.roll(before, -(offset + per) * stride, axis=-1)
    return jnp.where(digit >= per, ahead, jnp.where(digit < 0, behind, same))


def sixth_order(getter):
    return (
        45.0 * (getter(1) - getter(-1)) - 9.0 * (getter(2) - getter(-2)) + (getter(3) - getter(-3))
    ) / 60.0


def velocity_gradient(padded):
    field_x = padded[:, :, 1:-1]
    field_z = padded[1:-1]
    inner = padded[1:-1, :, 1:-1]
    after_y = jnp.roll(inner, -1, axis=1)
    before_y = jnp.roll(inner, 1, axis=1)
    along_x = sixth_order(
        lambda offset: cell_offset(field_x[1:-1], field_x[2:], field_x[:-2], 32, 4, offset)
    )
    along_y = sixth_order(lambda offset: cell_offset(inner, after_y, before_y, 8, 4, offset))
    along_z = sixth_order(
        lambda offset: cell_offset(
            field_z[:, :, 1:-1], field_z[:, :, 2:], field_z[:, :, :-2], 1, 8, offset
        )
    )
    stacked = jnp.stack([along_x, along_y, along_z], axis=4)
    return stacked.reshape(stacked.shape[:3] + (9, 128))


def deposit(vortex, coords):
    total_rows = vortex.shape[0]
    block_size = min(64, total_rows)

    def deposit_block_step(operands):
        block_vortex, block_coords = operands
        return jnp.einsum(
            "bip,bpc->bic",
            block_vortex,
            kernel_table(block_coords),
            precision=lax.Precision.HIGHEST,
        )

    shaped = (
        vortex.reshape((total_rows // block_size, block_size) + vortex.shape[1:]),
        coords.reshape((total_rows // block_size, block_size) + coords.shape[1:]),
    )
    return lax.map(deposit_block_step, shaped).reshape(total_rows, 3, 128)


def interpolate(grads, vortex, coords):
    total_rows = vortex.shape[0]
    block_size = min(64, total_rows)

    def interpolate_block_step(operands):
        block_grads, block_vortex, block_coords = operands
        sampled = jnp.einsum(
            "bkc,bpc->bkp", block_grads, kernel_table(block_coords), precision=lax.Precision.HIGHEST
        )
        sampled = sampled.reshape(sampled.shape[0], 3, 3, sampled.shape[2])
        return jnp.sum(sampled * block_vortex[:, None, :, :], axis=2)

    shaped = (
        grads.reshape((total_rows // block_size, block_size) + grads.shape[1:]),
        vortex.reshape((total_rows // block_size, block_size) + vortex.shape[1:]),
        coords.reshape((total_rows // block_size, block_size) + coords.shape[1:]),
    )
    return lax.map(interpolate_block_step, shaped).reshape(total_rows, 3, vortex.shape[2])


def assemble(patches, slot_index, slots_x, slots_y, slots_z):
    slot_count = slots_x * slots_y * slots_z
    summed = jax.ops.segment_sum(patches, slot_index, num_segments=slot_count)
    return summed.reshape(slots_x, slots_y, slots_z, 3, 128)


def to_owners(shipment, slot_marks, grid_x, grid_z, capacity):
    received, received_marks = (
        lax.all_to_all(
            shipment.reshape((grid_x * grid_z, capacity) + shipment.shape[1:]),
            ("gx", "gz"),
            split_axis=0,
            concat_axis=0,
            tiled=True,
        ),
        lax.all_to_all(
            slot_marks.reshape(grid_x * grid_z, capacity),
            ("gx", "gz"),
            split_axis=0,
            concat_axis=0,
            tiled=True,
        ),
    )
    return (received.reshape((-1,) + shipment.shape[1:]), received_marks.reshape(-1))


def from_owners(answers, grid_x, grid_z, capacity):
    returned = lax.all_to_all(
        answers.reshape((grid_x * grid_z, capacity) + answers.shape[1:]),
        ("gx", "gz"),
        split_axis=0,
        concat_axis=0,
        tiled=True,
    )
    return returned.reshape((-1,) + answers.shape[1:])


def on_device(vorticity, position, counts, owner_ids, slot_ids, velocity):
    particles = vorticity.shape[1]
    quarter = particles // 4
    tiles_dev = vorticity.shape[2]
    slots_x = velocity.shape[0]
    slots_y = velocity.shape[1]
    slots_z = velocity.shape[2]
    padded = extended(velocity, (("gx", 0), ("gz", 2)), 1)
    slot_grads = velocity_gradient(padded).reshape(-1, 9, 128)
    lane_ids = jnp.arange(quarter, dtype=jnp.int32)
    leave_masks = [
        (lane_ids[:, None] < counts[heading][None, :]).astype(jnp.float32) for heading in range(4)
    ]
    departing = [
        jnp.concatenate(
            [
                vorticity[:, heading * quarter : (heading + 1) * quarter] * leave_masks[heading],
                position[:, heading * quarter : (heading + 1) * quarter] * leave_masks[heading],
            ],
            axis=0,
        )
        for heading in range(4)
    ]
    arrivals = [
        passed_along(departing[0], "gx", 1),
        passed_along(departing[1], "gx", -1),
        passed_along(departing[2], "gz", 1),
        passed_along(departing[3], "gz", -1),
    ]
    leaving = jnp.concatenate(leave_masks, axis=0)
    kept_vortex = vorticity * (1.0 - leaving)[None]
    arrived_vortex = jnp.concatenate([arrival[:3] for arrival in arrivals], axis=1)
    arrived_coords = jnp.concatenate([arrival[3:] for arrival in arrivals], axis=1)
    routed_vortex = jnp.transpose(jnp.concatenate([kept_vortex, arrived_vortex], axis=2), (2, 0, 1))
    routed_coords = jnp.transpose(jnp.concatenate([position, arrived_coords], axis=2), (2, 0, 1))
    grid_x = lax.axis_size("gx")
    grid_z = lax.axis_size("gz")
    devices = grid_x * grid_z
    row_count = 2 * tiles_dev
    capacity = 2 * row_count // devices
    buffer_rows = devices * capacity
    owners = owner_ids[:, 0]
    onehot = (owners[:, None] == jnp.arange(devices, dtype=jnp.int32)[None, :]).astype(jnp.int32)
    ranking = jnp.sum((jnp.cumsum(onehot, axis=0) - onehot) * onehot, axis=1)
    targets = owners * capacity + ranking
    slot_marks = (
        jnp.zeros((buffer_rows,), jnp.float32).at[targets].set(slot_ids.astype(jnp.float32))
    )
    patches = deposit(routed_vortex, routed_coords)
    shipment = jnp.zeros((buffer_rows, 3, 128), jnp.float32).at[targets].set(patches)
    received, received_marks = to_owners(shipment, slot_marks, grid_x, grid_z, capacity)
    slot_index = received_marks.astype(jnp.int32)
    mesh_vorticity = assemble(received, slot_index, slots_x, slots_y, slots_z)
    answers = from_owners(slot_grads[slot_index], grid_x, grid_z, capacity)
    stretch_rows = interpolate(answers[targets], routed_vortex, routed_coords)
    stretching = jnp.transpose(stretch_rows.reshape(2, tiles_dev, 3, particles), (0, 2, 3, 1))
    return (mesh_vorticity, stretching)


def solution(mesh):
    placed = (
        P(None, None, ("gx", "gz")),
        P(None, None, ("gx", "gz")),
        P(None, ("gx", "gz")),
        P(("gx", "gz"), None),
        P(("gx", "gz")),
        P("gx", None, "gz", None, None),
    )
    return jax.shard_map(
        on_device,
        mesh=mesh,
        in_specs=placed,
        out_specs=(P("gx", None, "gz", None, None), P(None, None, None, ("gx", "gz"))),
        check_vma=False,
    )
```

profile of v0, /device:TPU:1, one launch (start us, length us, event | category | flops | bytes accessed | tf_op | source)
XLA Modules:
  0.0 442.4 jit_solution(10370786704517384294)
XLA Ops:
  2.8 4.9 %collective-permute-start.5 = (f32[1,16,16,3,128]{4,2,1,0,3:T(8,128)}, f32[1,16,16,3,128]{4,2,1,0,3:T(8,128)}, u32[]{:S(2)}, u32[]{:S(2)}) collective-permute-start(f32[1,16,16,3,128]{4,2,1,0,3:T(8,128)} %get-tuple-element.347), channel_id=1, source_target_pairs={{0,4},{4,8},{8,12},{12,16},{16,20},{20,24},{24,28},{28,32},{32,36}... | collective-permute-start | bytes 1179656 | tf_op jit(solution)/shard_map/ppermute | solution.py:14
  12.5 10.7 %all-to-all-start = ((f32[128,1,4]{2,1,0:T(1,128)}), f32[128,1,4]{2,1,0:T(1,128)}, u32[]{:S(2)}, u32[]{:S(2)}) async-start(f32[128,1,4]{2,1,0:T(1,128)} %bitcast.21), calls=%async_computation | async-start | bytes 131072 | tf_op jit(solution)/shard_map/all_to_all | solution.py:137
  110.3 22.1 %fusion.221 = f32[4,16,16,3,1,128]{5,2,1,0,4,3:T(8,128)} fusion(f32[4,16,16,3,1,104]{5,2,1,0,3,4:T(8,128)} %get-tuple-element.397, f32[4,16,16,3,1,24]{5,2,1,0,3,4:T(8,128)} %get-tuple-element.399, f32[4,16,16,3,1,40]{5,2,1,0,3,4:T(8,128)} %get-tuple-element.394, f32[4,16,16,3,1,88]{5,2,1,0,3,4:T(8,128)} %get-tuple-element.392, ...), kind=kLoop, calls=%fused_computation.385 | loop fusion | flops 14942208 | bytes 29885952 | tf_op jit(solution)/shard_map/div | solution.py:58
  148.6 8.2 %collective-permute-done.3 = f32[6,32,128]{1,2,0:T(8,128)S(1)} collective-permute-done((f32[6,32,128]{1,2,0:T(8,128)}, f32[6,32,128]{1,2,0:T(8,128)S(1)}, u32[]{:S(2)}, u32[]{:S(2)}) %collective-permute-start.3) | collective-permute-done | bytes 98336 | tf_op jit(solution)/shard_map/ppermute | solution.py:23
  157.4 51.7 %while.26 = (s32[]{:T(128)}, f32[4,64,3,128]{3,2,1,0:T(4,128)}, f32[4,64,3,128]{3,1,0,2:T(8,128)S(1)}, f32[4,64,3,128]{3,1,2,0:T(8,128)S(1)}, s32[]{:T(128)}) while((s32[]{:T(128)}, f32[4,64,3,128]{3,2,1,0:T(4,128)}, f32[4,64,3,128]{3,1,0,2:T(8,128)S(1)}, f32[4,64,3,128]{3,1,2,0:T(8,128)S(1)}, s32[]{:T(128)}) %tuple.181), condition=%wide.region_5.6_spmd, body=%wide.region_4.5_spmd.sunk | while | flops 96473600 | bytes 921157 | solution.py:99
  157.5 12.8 %fusion.288 = f32[4,64,3,128]{3,2,1,0:T(4,128)} fusion(f32[4,64,3,128]{3,2,1,0:T(4,128)} %get-tuple-element.518, s32[]{:T(128)} %get-tuple-element.517, f32[64,128]{1,0:T(8,128)S(1)} %get-tuple-element.497, f32[128]{0:T(128)S(1)} %get-tuple-element.498, f32[64,128]{1,0:T(8,128)S(1)} %get-tuple-element.499, f32[128]{0:T(128)S(1)} %fusion.287, ...), kind=kOutput, calls=%fused_computation.54.clone.1 | convolution fusion | flops 96468992 | bytes 329728 | tf_op jit(solution)/shard_map/while/body/eval_jaxpr/bip,bpc->bic/dot_general | solution.py:88
  170.4 12.8 %fusion.288 = f32[4,64,3,128]{3,2,1,0:T(4,128)} fusion(f32[4,64,3,128]{3,2,1,0:T(4,128)} %get-tuple-element.518, s32[]{:T(128)} %get-tuple-element.517, f32[64,128]{1,0:T(8,128)S(1)} %get-tuple-element.497, f32[128]{0:T(128)S(1)} %get-tuple-element.498, f32[64,128]{1,0:T(8,128)S(1)} %get-tuple-element.499, f32[128]{0:T(128)S(1)} %fusion.287, ...), kind=kOutput, calls=%fused_computation.54.clone.1 | convolution fusion | flops 96468992 | bytes 329728 | tf_op jit(solution)/shard_map/while/body/eval_jaxpr/bip,bpc->bic/dot_general | solution.py:88
  183.3 12.8 %fusion.288 = f32[4,64,3,128]{3,2,1,0:T(4,128)} fusion(f32[4,64,3,128]{3,2,1,0:T(4,128)} %get-tuple-element.518, s32[]{:T(128)} %get-tuple-element.517, f32[64,128]{1,0:T(8,128)S(1)} %get-tuple-element.497, f32[128]{0:T(128)S(1)} %get-tuple-element.498, f32[64,128]{1,0:T(8,128)S(1)} %get-tuple-element.499, f32[128]{0:T(128)S(1)} %fusion.287, ...), kind=kOutput, calls=%fused_computation.54.clone.1 | convolution fusion | flops 96468992 | bytes 329728 | tf_op jit(solution)/shard_map/while/body/eval_jaxpr/bip,bpc->bic/dot_general | solution.py:88
  196.2 12.8 %fusion.288 = f32[4,64,3,128]{3,2,1,0:T(4,128)} fusion(f32[4,64,3,128]{3,2,1,0:T(4,128)} %get-tuple-element.518, s32[]{:T(128)} %get-tuple-element.517, f32[64,128]{1,0:T(8,128)S(1)} %get-tuple-element.497, f32[128]{0:T(128)S(1)} %get-tuple-element.498, f32[64,128]{1,0:T(8,128)S(1)} %get-tuple-element.499, f32[128]{0:T(128)S(1)} %fusion.287, ...), kind=kOutput, calls=%fused_computation.54.clone.1 | convolution fusion | flops 96468992 | bytes 329728 | tf_op jit(solution)/shard_map/while/body/eval_jaxpr/bip,bpc->bic/dot_general | solution.py:88
  210.0 16.3 %scatter_fusion = f32[512,3,128]{2,1,0:T(4,128)S(1)} fusion(f32[512,3,128]{2,1,0:T(4,128)S(1)} %broadcast_in_dim.161, s32[256]{0:T(256)S(1)} %bitcast.329, f32[256,3,128]{2,1,0:T(4,128)} %bitcast.320), kind=kCustom, calls=%fused_computation.3 | custom fusion | bytes 1180672 | tf_op jit(solution)/shard_map/scatter | solution.py:208
  227.3 9.7 %all-to-all-start.1 = ((f32[128,4,3,128]{3,1,2,0:T(4,128)}), f32[128,4,3,128]{3,1,2,0:T(4,128)}, u32[]{:S(2)}, u32[]{:S(2)}) async-start(f32[128,4,3,128]{3,1,2,0:T(4,128)} %copy.316), calls=%async_computation.1 | async-start | bytes 1572864 | tf_op jit(solution)/shard_map/all_to_all | solution.py:130
  252.1 5.8 %fusion.236 = f32[4,16,16,3,1,128]{5,2,1,0,4,3:T(8,128)S(1)} fusion(f32[4,16,16,3,1,64]{5,2,1,0,3,4:T(8,128)S(1)} %get-tuple-element.308, f32[4,16,16,3,1,64]{5,2,1,0,3,4:T(8,128)S(1)} %get-tuple-element.307, f32[4,16,16,3,1,64]{5,2,1,0,3,4:T(8,128)S(1)} %copy-done.6, f32[4,16,16,3,1,64]{5,2,1,0,3,4:T(8,128)S(1)} %copy-done.5, ...), kind=kLoop, calls=%fused_computation.424 | loop fusion | flops 11403264 | bytes 15730176 | tf_op jit(solution)/shard_map/div | solution.py:58
  288.9 18.0 %fusion.232 = f32[4,16,16,3,1,128]{5,2,1,0,4,3:T(8,128)S(1)} fusion(f32[4,16,16,3,1,121]{5,2,1,0,3,4:T(8,128)} %get-tuple-element.288, f32[4,16,16,3,1,7]{5,2,1,0,3,4:T(8,128)} %get-tuple-element.290, f32[4,16,16,3,1,9]{5,2,1,0,3,4:T(8,128)} %get-tuple-element.292, f32[4,16,16,3,1,119]{5,2,1,0,3,4:T(8,128)} %get-tuple-element.294, ...), kind=kLoop, calls=%fused_computation.408 | loop fusion | flops 14942208 | bytes 29885952 | tf_op jit(solution)/shard_map/div | solution.py:58
  307.3 6.3 %copy.368 = f32[1024,9,128]{2,1,0:T(8,128)} copy(f32[1024,9,128]{2,0,1:T(8,128)S(1)} %bitcast.309) | data formatting | bytes 9437184 | tf_op jit(solution)/shard_map/reshape;reshape | solution.py:167
  313.6 6.4 %gather_fusion = f32[512,9,128]{2,1,0:T(8,128)} fusion(f32[1024,9,128]{2,1,0:T(8,128)} %copy.368, s32[1024]{0:T(1024)S(1)} %copy-done.23), kind=kCustom, calls=%fused_computation | custom fusion | bytes 4720640 | tf_op jit(solution)/shard_map/gather | solution.py:212
  320.0 4.7 %copy.369 = f32[128,4,9,128]{3,1,2,0:T(4,128)} copy(f32[128,4,9,128]{3,2,1,0:T(8,128)} %bitcast.310) | data formatting | bytes 4718592 | tf_op jit(solution)/shard_map/reshape | solution.py:150
  324.8 10.7 %all-to-all-start.2 = ((f32[128,4,9,128]{3,1,2,0:T(4,128)}), f32[128,4,9,128]{3,1,2,0:T(4,128)}, u32[]{:S(2)}, u32[]{:S(2)}) async-start(f32[128,4,9,128]{3,1,2,0:T(4,128)} %copy.369), calls=%async_computation.2 | async-start | bytes 4718592 | tf_op jit(solution)/shard_map/all_to_all | solution.py:149
  339.7 34.7 %scatter_fusion.1 = f32[1024,3,128]{2,1,0:T(4,128)S(1)} fusion(f32[1024,3,128]{2,1,0:T(4,128)S(1)} %broadcast_in_dim.159, s32[512]{0:T(512)S(1)} %reshape.1949, f32[512,3,128]{2,1,0:T(4,128)} %copy.318), kind=kCustom, calls=%fused_computation.4 | custom fusion | flops 196608 | bytes 2361344 | tf_op jit(solution)/shard_map/scatter-add | solution.py:124
  375.7 4.2 copy.370
  382.9 58.5 %while.27 = (s32[]{:T(128)}, f32[4,64,3,128]{3,1,0,2:T(8,128)S(1)}, f32[4,64,9,128]{3,2,1,0:T(8,128)S(1)}, f32[4,64,3,128]{3,1,2,0:T(8,128)S(1)}, f32[4,64,3,128]{3,1,0,2:T(8,128)}, /*index=5*/s32[]{:T(128)}) while((s32[]{:T(128)}, f32[4,64,3,128]{3,1,0,2:T(8,128)S(1)}, f32[4,64,9,128]{3,2,1,0:T(8,128)S(1)}, ...), condition=%wide.region_10.11_spmd, body=%wide.region_8.10_spmd.sunk | while | flops 172093952 | bytes 2788437 | solution.py:119
  383.1 13.4 %fusion.293 = f32[64,9,128]{2,1,0:T(8,128)S(1)} fusion(f32[64,128]{1,0:T(8,128)S(1)} %get-tuple-element.507, f32[128]{0:T(128)S(1)} %get-tuple-element.508, f32[64,128]{1,0:T(8,128)S(1)} %get-tuple-element.509, f32[128]{0:T(128)S(1)} %fusion.292, f32[64,128]{1,0:T(8,128)S(1)} %get-tuple-element.510, f32[128]{0:T(128)S(1)} %get-tuple-element.511, ...), kind=kOutput, calls=%fused_computation.96.clone.1 | convolution fusion | flops 171966464 | bytes 919044 | tf_op jit(solution)/shard_map/while/body/eval_jaxpr/bkc,bpc->bkp/dot_general | solution.py:108
  397.7 13.4 %fusion.293 = f32[64,9,128]{2,1,0:T(8,128)S(1)} fusion(f32[64,128]{1,0:T(8,128)S(1)} %get-tuple-element.507, f32[128]{0:T(128)S(1)} %get-tuple-element.508, f32[64,128]{1,0:T(8,128)S(1)} %get-tuple-element.509, f32[128]{0:T(128)S(1)} %fusion.292, f32[64,128]{1,0:T(8,128)S(1)} %get-tuple-element.510, f32[128]{0:T(128)S(1)} %get-tuple-element.511, ...), kind=kOutput, calls=%fused_computation.96.clone.1 | convolution fusion | flops 171966464 | bytes 919044 | tf_op jit(solution)/shard_map/while/body/eval_jaxpr/bkc,bpc->bkp/dot_general | solution.py:108
  412.3 13.4 %fusion.293 = f32[64,9,128]{2,1,0:T(8,128)S(1)} fusion(f32[64,128]{1,0:T(8,128)S(1)} %get-tuple-element.507, f32[128]{0:T(128)S(1)} %get-tuple-element.508, f32[64,128]{1,0:T(8,128)S(1)} %get-tuple-element.509, f32[128]{0:T(128)S(1)} %fusion.292, f32[64,128]{1,0:T(8,128)S(1)} %get-tuple-element.510, f32[128]{0:T(128)S(1)} %get-tuple-element.511, ...), kind=kOutput, calls=%fused_computation.96.clone.1 | convolution fusion | flops 171966464 | bytes 919044 | tf_op jit(solution)/shard_map/while/body/eval_jaxpr/bkc,bpc->bkp/dot_general | solution.py:108
  426.8 13.4 %fusion.293 = f32[64,9,128]{2,1,0:T(8,128)S(1)} fusion(f32[64,128]{1,0:T(8,128)S(1)} %get-tuple-element.507, f32[128]{0:T(128)S(1)} %get-tuple-element.508, f32[64,128]{1,0:T(8,128)S(1)} %get-tuple-element.509, f32[128]{0:T(128)S(1)} %fusion.292, f32[64,128]{1,0:T(8,128)S(1)} %get-tuple-element.510, f32[128]{0:T(128)S(1)} %get-tuple-element.511, ...), kind=kOutput, calls=%fused_computation.96.clone.1 | convolution fusion | flops 171966464 | bytes 919044 | tf_op jit(solution)/shard_map/while/body/eval_jaxpr/bkc,bpc->bkp/dot_general | solution.py:108
  (296 shorter events, 172.3 us)
Async XLA Ops:
  0.6 9.0 %copy-start.22 = (s32[256,1]{0,1:T(1,128)S(1)}, s32[256,1]{0,1:T(1,128)}, u32[]{:S(2)}) copy-start(s32[256,1]{0,1:T(1,128)} %param.13) | copy-start | bytes 3076
  0.6 9.7 %copy-start.27 = (s32[256]{0:T(256)S(1)}, s32[256]{0:T(256)}, u32[]{:S(2)}) copy-start(s32[256]{0:T(256)} %param.14) | copy-start | bytes 3076
  0.7 22.5 %copy-start.26 = (s32[4,128]{1,0:T(4,128)S(1)}, s32[4,128]{1,0:T(4,128)}, u32[]{:S(2)}) copy-start(s32[4,128]{1,0:T(4,128)} %param.12) | copy-start | bytes 6148
  0.7 22.5 %copy-start.18 = (f32[3,128,128]{2,1,0:T(8,128)S(1)}, f32[3,128,128]{2,1,0:T(8,128)}, u32[]{:S(2)}) copy-start(f32[3,128,128]{2,1,0:T(8,128)} %param.10) | copy-start | bytes 589828
  0.7 22.5 %copy-start.19 = (f32[3,128,128]{2,1,0:T(8,128)S(1)}, f32[3,128,128]{2,1,0:T(8,128)}, u32[]{:S(2)}) copy-start(f32[3,128,128]{2,1,0:T(8,128)} %param.11) | copy-start | bytes 589828
  2.8 234.3 %collective-permute-start.5 = (f32[1,16,16,3,128]{4,2,1,0,3:T(8,128)}, f32[1,16,16,3,128]{4,2,1,0,3:T(8,128)}, u32[]{:S(2)}, u32[]{:S(2)}) collective-permute-start(f32[1,16,16,3,128]{4,2,1,0,3:T(8,128)} %get-tuple-element.347), channel_id=1, source_target_pairs={{0,4},{4,8},{8,12},{12,16},{16,20},{20,24},{24,28},{28,32},{32,36}... | collective-permute-start | bytes 1179656 | tf_op jit(solution)/shard_map/ppermute | solution.py:14
  7.7 230.8 %collective-permute-start.4 = (f32[1,16,16,3,128]{4,2,1,0,3:T(8,128)}, f32[1,16,16,3,128]{4,2,1,0,3:T(8,128)}, u32[]{:S(2)}, u32[]{:S(2)}) collective-permute-start(f32[1,16,16,3,128]{4,2,1,0,3:T(8,128)} %get-tuple-element.346), channel_id=1, source_target_pairs={{4,0},{8,4},{12,8},{16,12},{20,16},{24,20},{28,24},{32,28},{36,32}... | collective-permute-start | bytes 1179656 | tf_op jit(solution)/shard_map/ppermute | solution.py:15
  12.5 23.9 %copy-start = (f32[4,16,16,3,128]{4,2,3,1,0:T(8,128)S(1)}, f32[4,16,16,3,128]{4,2,3,1,0:T(8,128)}, u32[]{:S(2)}) copy-start(f32[4,16,16,3,128]{4,2,3,1,0:T(8,128)} %param.15) | copy-start | bytes 4718596
  12.5 130.1 %all-to-all-start = ((f32[128,1,4]{2,1,0:T(1,128)}), f32[128,1,4]{2,1,0:T(1,128)}, u32[]{:S(2)}, u32[]{:S(2)}) async-start(f32[128,1,4]{2,1,0:T(1,128)} %bitcast.21), calls=%async_computation | async-start | bytes 131072 | tf_op jit(solution)/shard_map/all_to_all | solution.py:137
  24.8 119.3 %collective-permute-start = (f32[6,32,128]{1,2,0:T(8,128)}, f32[6,32,128]{1,2,0:T(8,128)}, u32[]{:S(2)}, u32[]{:S(2)}) collective-permute-start(f32[6,32,128]{1,2,0:T(8,128)} %copy.308), channel_id=1, source_target_pairs={{0,4},{4,8},{8,12},{12,16},{16,20},{20,24},{24,28},{28,32},{32,36}... | collective-permute-start | bytes 294920 | tf_op jit(solution)/shard_map/ppermute | solution.py:23
  29.5 117.1 %collective-permute-start.1 = (f32[6,32,128]{1,2,0:T(8,128)}, f32[6,32,128]{1,2,0:T(8,128)}, u32[]{:S(2)}, u32[]{:S(2)}) collective-permute-start(f32[6,32,128]{1,2,0:T(8,128)} %copy.309), channel_id=1, source_target_pairs={{4,0},{8,4},{12,8},{16,12},{20,16},{24,20},{28,24},{32,28},{36,32}... | collective-permute-start | bytes 294920 | tf_op jit(solution)/shard_map/ppermute | solution.py:23
  32.3 115.3 %collective-permute-start.2 = (f32[6,32,128]{1,2,0:T(8,128)}, f32[6,32,128]{1,2,0:T(8,128)}, u32[]{:S(2)}, u32[]{:S(2)}) collective-permute-start(f32[6,32,128]{1,2,0:T(8,128)} %copy.310), channel_id=1, source_target_pairs={{0,1},{1,2},{2,3},{4,5},{5,6},{6,7},{8,9},{9,10},{10,11},{12,13},{... | collective-permute-start | bytes 294920 | tf_op jit(solution)/shard_map/ppermute | solution.py:23
  110.3 22.6 %copy-start.20 = (f32[3,128,128]{2,1,0:T(8,128)S(1)}, f32[3,128,128]{2,1,0:T(8,128)}, u32[]{:S(2)}) copy-start(f32[3,128,128]{2,1,0:T(8,128)} %param.11) | copy-start | bytes 589828
  144.2 12.7 %collective-permute-start.3 = (f32[6,32,128]{1,2,0:T(8,128)}, f32[6,32,128]{1,2,0:T(8,128)S(1)}, u32[]{:S(2)}, u32[]{:S(2)}) collective-permute-start(f32[6,32,128]{1,2,0:T(8,128)} %copy.311), channel_id=1, source_target_pairs={{1,0},{2,1},{3,2},{5,4},{6,5},{7,6},{9,8},{10,9},{11,10},{13,12},{... | collective-permute-start | bytes 294920 | tf_op jit(solution)/shard_map/ppermute | solution.py:23
  148.6 8.5 %copy-start.17 = (f32[3,128,128]{1,2,0:T(8,128)S(1)}, f32[3,128,128]{1,2,0:T(8,128)}, u32[]{:S(2)}) copy-start(f32[3,128,128]{1,2,0:T(8,128)} %broadcast_multiply_fusion) | copy-start | bytes 589828
  157.4 52.6 %copy-start.25 = (s32[256,1]{0,1:T(1,128)S(1)}, s32[256,1]{0,1:T(1,128)}, u32[]{:S(2)}) copy-start(s32[256,1]{0,1:T(1,128)} %copy-done.24) | copy-start | bytes 3076
  227.3 97.4 %all-to-all-start.1 = ((f32[128,4,3,128]{3,1,2,0:T(4,128)}), f32[128,4,3,128]{3,1,2,0:T(4,128)}, u32[]{:S(2)}, u32[]{:S(2)}) async-start(f32[128,4,3,128]{3,1,2,0:T(4,128)} %copy.316), calls=%async_computation.1 | async-start | bytes 1572864 | tf_op jit(solution)/shard_map/all_to_all | solution.py:130
  241.8 10.2 %copy-start.5 = (f32[4,16,16,3,1,64]{5,2,1,0,3,4:T(8,128)S(1)}, f32[4,16,16,3,1,64]{5,2,1,0,3,4:T(8,128)}, u32[]{:S(2)}) copy-start(f32[4,16,16,3,1,64]{5,2,1,0,3,4:T(8,128)} %get-tuple-element.316) | copy-start | bytes 2359300
  241.8 10.2 %copy-start.6 = (f32[4,16,16,3,1,64]{5,2,1,0,3,4:T(8,128)S(1)}, f32[4,16,16,3,1,64]{5,2,1,0,3,4:T(8,128)}, u32[]{:S(2)}) copy-start(f32[4,16,16,3,1,64]{5,2,1,0,3,4:T(8,128)} %get-tuple-element.317) | copy-start | bytes 2359300
  244.0 8.0 %copy-start.40 = (pred[128]{0:T(512)(128)(4,1)S(1)}, pred[128]{0:T(512)(128)(4,1)}, u32[]{:S(2)}) copy-start(pred[128]{0:T(512)(128)(4,1)} %get-tuple-element.428) | copy-start | bytes 388
  246.5 11.4 %collective-permute-start.6 = (f32[6,16,1,3,128]{4,2,1,0,3:T(1,128)S(1)}, f32[6,16,1,3,128]{4,2,1,0,3:T(1,128)S(1)}, u32[]{:S(2)}, u32[]{:S(2)}) collective-permute-start(f32[6,16,1,3,128]{4,2,1,0,3:T(1,128)S(1)} %get-tuple-element.296), channel_id=1, source_target_pairs={{1,0},{2,1},{3,2},{5,4},{6,5},{7,6},{9,8},{10,9},{11,10},{13,12},{... | collective-permute-start | bytes 442376 | tf_op jit(solution)/shard_map/ppermute | solution.py:15
  248.0 9.9 %collective-permute-start.7 = (f32[6,16,1,3,128]{4,2,1,0,3:T(1,128)S(1)}, f32[6,16,1,3,128]{4,2,1,0,3:T(1,128)S(1)}, u32[]{:S(2)}, u32[]{:S(2)}) collective-permute-start(f32[6,16,1,3,128]{4,2,1,0,3:T(1,128)S(1)} %get-tuple-element.295), channel_id=1, source_target_pairs={{0,1},{1,2},{2,3},{4,5},{5,6},{6,7},{8,9},{9,10},{10,11},{12,13},{... | collective-permute-start | bytes 442376 | tf_op jit(solution)/shard_map/ppermute | solution.py:14
  288.9 18.0 %copy-start.7 = (f32[4,16,16,3,1,128]{5,2,1,0,4,3:T(8,128)S(1)}, f32[4,16,16,3,1,128]{5,2,1,0,4,3:T(8,128)}, u32[]{:S(2)}) copy-start(f32[4,16,16,3,1,128]{5,2,1,0,4,3:T(8,128)} %fusion.221) | copy-start | bytes 4718596
  324.8 51.0 %all-to-all-start.2 = ((f32[128,4,9,128]{3,1,2,0:T(4,128)}), f32[128,4,9,128]{3,1,2,0:T(4,128)}, u32[]{:S(2)}, u32[]{:S(2)}) async-start(f32[128,4,9,128]{3,1,2,0:T(4,128)} %copy.369), calls=%async_computation.2 | async-start | bytes 4718592 | tf_op jit(solution)/shard_map/all_to_all | solution.py:149
  (35 other events, 188.0 us)
where the time goes:
time: 450 us; the launch traced here: 442 us
  other arithmetic  154 us (34%)
  local copies, waits for them, and re-layouts  118 us (26%)
  matrix products  105 us (23%)
  starting transfers between devices  54.3 us (12%)
  waiting for transfers between devices  8.23 us (2%)
    dot_general x4, matrix products, interpolate_block_step(): jnp.einsum('bkc,bpc->bkp', block_grads, kernel_table(block_coords), preci...  53.7 us
    dot_general x4, matrix products, deposit_block_step(): jnp.einsum('bip,bpc->bic', block_vortex, kernel_table(block_coords), prec...  51.4 us
    div x3, other arithmetic, sixth_order(): (45.0 * (getter(1) - getter(-1)) - 9.0 * (getter(2) - getter(-2)) + (gett...  45.9 us
    concatenate x18, other arithmetic, cell_offset(): behind = jnp.roll(before, -(offset + per) * stride, axis=-1)  39.4 us
    concatenate x16, local copies, waits for them, and re-layouts, cell_offset(): same = jnp.roll(center, -offset * stride, axis=-1)  36.4 us
    scatter-add x1, other arithmetic, assemble(): summed = jax.ops.segment_sum(patches, slot_index, num_segments=slot_count)  34.7 us
    concatenate x8, other arithmetic, cell_offset(): ahead = jnp.roll(after, -(offset - per) * stride, axis=-1)  17.6 us
    scatter x1, local copies, waits for them, and re-layouts, on_device(): jnp.zeros((buffer_rows, 3, 128), jnp.float32).at[targets].set(patches)  16.3 us
  transfers between devices with their start and end apart: 11, of which 1 were waited for; matrix products, arithmetic and copies ran while one was open for 69% of the time, Pallas kernels for 0%

commit v1 on v0

v1 whole, which is shorter than its diff:
```python
import jax
import jax.numpy as jnp
from jax import lax
from jax.experimental import pallas as pl
from jax.experimental.pallas import tpu as pltpu
from jax.sharding import PartitionSpec as P

AXES = ("gx", "gz")
F32 = jnp.float32
BF16 = jnp.bfloat16
VMEM = pl.BlockSpec(memory_space=pltpu.VMEM)
SMEM = pl.BlockSpec(memory_space=pltpu.SMEM)
PARAMS = pltpu.CompilerParams(vmem_limit_bytes=40 * 1024 * 1024)
GRAD_ROWS = 64 * 9 * 16
GRAD_PAD = 128


def sds(shape, dtype=F32):
    return jax.ShapeDtypeStruct(shape, dtype)


def cost(flops, read):
    return pl.CostEstimate(flops=flops, bytes_accessed=read, transcendentals=0)


def depart_kernel(vort, pos, counts, *outs):
    place = lax.broadcasted_iota(jnp.int32, (32, 128), 0)
    for heading in range(4):
        leaves = place < counts[heading : heading + 1, :]
        rows = slice(heading * 32, heading * 32 + 32)
        for i in range(3):
            outs[heading][i] = jnp.where(leaves, vort[i, rows, :], 0.0)
            outs[heading][3 + i] = jnp.where(leaves, pos[i, rows, :], 0.0)


def depart(vort, pos, counts):
    return pl.pallas_call(
        depart_kernel,
        out_shape=[sds((6, 32, 128))] * 4,
        in_specs=[VMEM] * 3,
        out_specs=[VMEM] * 4,
        compiler_params=PARAMS,
        cost_estimate=cost(400_000, 1_600_000),
    )(vort, pos, counts)


def plan_kernel(owners, slots, places, marks, tally):
    def clear(i, carry):
        tally[i] = 0
        for k in range(4):
            marks[4 * i + k] = 0
        return carry

    lax.fori_loop(0, 128, clear, 0)

    def step(r, carry):
        owner = owners[r]
        rank = tally[owner]
        tally[owner] = rank + 1
        places[r] = owner * 4 + rank
        marks[owner * 4 + rank] = slots[r]
        return carry

    lax.fori_loop(0, 256, step, 0, unroll=4)


def plan(owners, slots):
    return pl.pallas_call(
        plan_kernel,
        out_shape=[sds((256,), jnp.int32), sds((512,), jnp.int32)],
        in_specs=[SMEM] * 2,
        out_specs=[SMEM] * 2,
        scratch_shapes=[pltpu.SMEM((128,), jnp.int32)],
        cost_estimate=cost(4_000, 6_000),
    )(owners, slots)


ORDER = (3, 4, 0, 1, 2, 5)


def route_kernel(places, vort, pos, counts, a0, a1, a2, a3, ship, turned):
    arrivals = (a0, a1, a2, a3)

    def clear(i, carry):
        ship[pl.ds(pl.multiple_of(i * 64, 64), 64), :] = jnp.zeros((64, 128), F32)
        return carry

    lax.fori_loop(0, 48, clear, 0)
    place = lax.broadcasted_iota(jnp.int32, (32, 128), 0)
    leaves = [place < counts[heading : heading + 1, :] for heading in range(4)]
    for at, comp in enumerate(ORDER):
        if comp < 3:
            kept = jnp.concatenate(
                [
                    jnp.where(leaves[h], 0.0, vort[comp, 32 * h : 32 * h + 32, :])
                    for h in range(4)
                ],
                axis=0,
            )
        else:
            kept = pos[comp - 3]
        turned[at * 256 : at * 256 + 128, :] = kept.T
        came = jnp.concatenate([a[comp] for a in arrivals], axis=0)
        turned[at * 256 + 128 : at * 256 + 256, :] = came.T

    def move(r, carry):
        place = places[r]
        base = (place >> 2) * 24 + (place & 3)
        ship[pl.ds(base, 6, stride=4), :] = turned[pl.ds(r, 6, stride=256), :]
        return carry

    lax.fori_loop(0, 256, move, 0, unroll=8)


def route(places, vort, pos, counts, arrivals):
    return pl.pallas_call(
        route_kernel,
        out_shape=sds((3072, 128)),
        in_specs=[SMEM] + [VMEM] * 7,
        out_specs=VMEM,
        scratch_shapes=[pltpu.VMEM((1536, 128), F32)],
        compiler_params=PARAMS,
        cost_estimate=cost(1_000_000, 4_000_000),
    )(places, vort, pos, counts, *arrivals)


def gradient_kernel(vel, xb, xa, zb, za, out):
    lane = lax.broadcasted_iota(jnp.int32, (16, 128), 1)
    digit_y = (lane // 8) % 4
    digit_z = lane % 8

    def shift(value, by):
        return pltpu.roll(value, by % 128, 1)

    def derive(sx, sy, i):
        c = vel[sx, sy, i]
        before = vel[sx - 1, sy, i] if sx > 0 else xb[sy, i]
        after = vel[sx + 1, sy, i] if sx < 3 else xa[sy, i]
        plus = [shift(jnp.where(lane < 32 * o, after, c), -32 * o) for o in (1, 2, 3)]
        minus = [shift(jnp.where(lane >= 128 - 32 * o, before, c), 32 * o) for o in (1, 2, 3)]
        along_x = combine(plus, minus)

        before = vel[sx, (sy + 15) & 15, i]
        after = vel[sx, (sy + 1) & 15, i]
        plus = [
            jnp.where(digit_y >= 4 - o, shift(after, 32 - 8 * o), shift(c, -8 * o))
            for o in (1, 2, 3)
        ]
        minus = [
            jnp.where(digit_y < o, shift(before, 8 * o - 32), shift(c, 8 * o)) for o in (1, 2, 3)
        ]
        along_y = combine(plus, minus)

        before = jnp.concatenate([zb[sx, sy, i], c[:15]], axis=0)
        after = jnp.concatenate([c[1:], za[sx, sy, i]], axis=0)
        plus = [
            jnp.where(digit_z >= 8 - o, shift(after, 8 - o), shift(c, -o)) for o in (1, 2, 3)
        ]
        minus = [jnp.where(digit_z < o, shift(before, o - 8), shift(c, o)) for o in (1, 2, 3)]
        along_z = combine(plus, minus)
        return along_x, along_y, along_z

    def combine(plus, minus):
        return (
            (45.0 / 60.0) * (plus[0] - minus[0])
            - (9.0 / 60.0) * (plus[1] - minus[1])
            + (1.0 / 60.0) * (plus[2] - minus[2])
        )

    for sx in range(4):

        def per_y(sy, carry, sx=sx):
            base = (sx * 16 + sy) * 144
            for i in range(3):
                for j, value in enumerate(derive(sx, sy, i)):
                    row = pl.multiple_of(base + (j * 3 + i) * 16, 16)
                    out[pl.ds(row, 16), :] = value
            return carry

        lax.fori_loop(0, 16, per_y, 0)
    out[GRAD_ROWS:, :] = jnp.zeros((GRAD_PAD, 128), F32)


def gradient(vel, xb, xa, zb, za):
    return pl.pallas_call(
        gradient_kernel,
        out_shape=sds((GRAD_ROWS + GRAD_PAD, 128)),
        in_specs=[VMEM] * 5,
        out_specs=VMEM,
        compiler_params=PARAMS,
        cost_estimate=cost(20_000_000, 8_000_000),
    )(vel, xb, xa, zb, za)


def split(value):
    high = value.astype(BF16)
    return high, (value - high.astype(F32)).astype(BF16)


def owner_kernel(marks, rows, grads, mesh, back):
    def clear(i, carry):
        mesh[pl.ds(pl.multiple_of(i * 64, 64), 64), :] = jnp.zeros((64, 128), F32)
        return carry

    lax.fori_loop(0, 48, clear, 0)
    cell_z = lax.broadcasted_iota(jnp.int32, (8, 128), 0).astype(F32)

    def wide(row):
        return jnp.broadcast_to(row, (8, 128))

    def per_source(s, carry):
        base = pl.multiple_of(s * 24, 8)
        f = rows[pl.ds(base, 8), :] - 1.0
        g = 1.0 - f
        weights = (
            -0.5 * f * g * g,
            1.0 + f * f * (1.5 * f - 2.5),
            1.0 + g * g * (1.5 * g - 2.5),
            -0.5 * g * f * f,
        )
        for k in range(4):
            slot = marks[s * 4 + k]
            column = slot >> 4
            level = slot & 15
            z = wide(rows[pl.ds(base + 20 + k, 1), :])
            radius = jnp.abs(cell_z - z)
            rest = jnp.maximum(2.0 - radius, 0.0)
            along_z = jnp.where(
                radius < 1.0,
                1.0 + radius * radius * (1.5 * radius - 2.5),
                0.5 * rest * rest * (1.0 - radius),
            )
            yz = [wide(weights[b][4 + k : 5 + k]) * along_z for b in range(4)]
            xs = [wide(weights[a][k : k + 1]) for a in range(4)]
            table = jnp.concatenate([xs[a] * yz[b] for a in range(4) for b in range(4)], axis=0)
            high, low = split(table)

            vortex = [rows[pl.ds(base + 8 + 4 * j + k, 1), :] for j in range(3)]
            grad = jnp.concatenate(
                [
                    grads[pl.ds(column * 144 + j * 48 + level, 8, stride=16), :]
                    for j in range(3)
                ],
                axis=0,
            )
            g_high, g_low = split(grad)
            left = jnp.concatenate([g_high, g_low], axis=0)
            left = jnp.concatenate([left, left], axis=1)
            sampled = jnp.dot(
                left, jnp.concatenate([high, low], axis=0), preferred_element_type=F32
            )
            sampled = sampled[:24] + sampled[24:]
            stretch = (
                sampled[0:8] * wide(vortex[0])
                + sampled[8:16] * wide(vortex[1])
                + sampled[16:24] * wide(vortex[2])
            )
            back[pl.ds(s * 12 + k, 3, stride=4), :] = stretch[:3]

            v = rows[pl.ds(base + 8 + k, 3, stride=4), :]
            v = jnp.concatenate([v, jnp.zeros((5, 128), F32)], axis=0)
            v_high, v_low = split(v)
            left = jnp.concatenate([v_high, v_low], axis=0)
            left = jnp.concatenate([left, left], axis=1)
            patch = lax.dot_general(
                left,
                jnp.concatenate([high, low], axis=1),
                (((1,), (1,)), ((), ())),
                preferred_element_type=F32,
            )
            patch = patch[:3] + patch[8:11]
            at = pl.ds(column * 48 + level, 3, stride=16)
            mesh[at, :] = mesh[at, :] + patch
        return carry

    lax.fori_loop(0, 128, per_source, 0)


def owner_work(marks, rows, grads):
    return pl.pallas_call(
        owner_kernel,
        out_shape=[sds((3072, 128)), sds((1536, 128))],
        in_specs=[SMEM, VMEM, VMEM],
        out_specs=[VMEM] * 2,
        compiler_params=PARAMS,
        cost_estimate=cost(300_000_000, 9_000_000),
    )(marks, rows, grads)


def unpack_kernel(places, back, out, turned):
    def move(r, carry):
        place = places[r]
        base = (place >> 2) * 12 + (place & 3)
        turned[pl.ds(r, 3, stride=256), :] = back[pl.ds(base, 3, stride=4), :]
        return carry

    lax.fori_loop(0, 256, move, 0, unroll=8)
    for h in range(2):
        for i in range(3):
            at = i * 256 + h * 128
            out[h, i] = turned[at : at + 128, :].T


def unpack(places, back):
    return pl.pallas_call(
        unpack_kernel,
        out_shape=sds((2, 3, 128, 128)),
        in_specs=[SMEM, VMEM],
        out_specs=VMEM,
        scratch_shapes=[pltpu.VMEM((768, 128), F32)],
        compiler_params=PARAMS,
        cost_estimate=cost(1_000_000, 2_000_000),
    )(places, back)


def stepped(value, axis, step):
    count = lax.axis_size(axis)
    first, last = (max(0, -step), min(count, count - step))
    return lax.ppermute(value, axis, [(source, source + step) for source in range(first, last)])


def exchange(value):
    return lax.all_to_all(value, AXES, split_axis=0, concat_axis=0, tiled=True)


def on_device(vorticity, position, counts, owner_ids, slot_ids, velocity):
    leaving = depart(vorticity, position, counts)
    arrivals = [
        stepped(leaving[0], "gx", 1),
        stepped(leaving[1], "gx", -1),
        stepped(leaving[2], "gz", 1),
        stepped(leaving[3], "gz", -1),
    ]
    places, marks = plan(owner_ids[:, 0], slot_ids)
    marks = exchange(marks.reshape(128, 1, 4)).reshape(512)
    ship = route(places, vorticity, position, counts, arrivals)
    rows = exchange(ship.reshape(128, 24, 128)).reshape(3072, 128)

    vel = jnp.transpose(velocity, (0, 1, 3, 2, 4))
    xb = stepped(vel[3], "gx", 1)
    xa = stepped(vel[0], "gx", -1)
    zb = stepped(vel[:, :, :, 15:], "gz", 1)
    za = stepped(vel[:, :, :, :1], "gz", -1)
    grads = gradient(vel, xb, xa, zb, za)

    mesh, back = owner_work(marks, rows, grads)
    back = exchange(back.reshape(128, 3, 4, 128)).reshape(1536, 128)
    stretching = unpack(places, back)
    mesh = jnp.transpose(mesh.reshape(4, 16, 3, 16, 128), (0, 1, 3, 2, 4))
    return mesh, stretching


def solution(mesh):
    placed = (
        P(None, None, AXES),
        P(None, None, AXES),
        P(None, AXES),
        P(AXES, None),
        P(AXES),
        P("gx", None, "gz", None, None),
    )
    return jax.shard_map(
        on_device,
        mesh=mesh,
        in_specs=placed,
        out_specs=(P("gx", None, "gz", None, None), P(None, None, None, AXES)),
        check_vma=False,
    )
```

time: 450 us -> 159 us (0.35); the launches traced: 442 us -> 158 us
  other arithmetic: 154 us -> 2.17 us
  matrix products: 105 us -> 0 us
  local copies, waits for them, and re-layouts: 118 us -> 15.5 us
  Pallas kernels: 0 us -> 62.9 us
  blocking collectives: 0 us -> 25 us
  starting transfers between devices: 54.3 us -> 40.6 us
    dot_general x8 -> x0, matrix products: 105 us -> none  [the longest x4 53.7 us: interpolate_block_step(): jnp.einsum('bkc,bpc->bkp', block_grads, kernel_table(block_coords), preci...]
    pallas_call x0 -> x6, Pallas kernels: none -> 62.9 us  [the longest x1 36 us: owner_work(): pl.pallas_call(owner_kernel, out_shape=[sds((3072, 128)), sds((1536, 128)...]
    concatenate x32 -> x0, other arithmetic: 59 us -> none  [the longest x18 39.4 us: cell_offset(): behind = jnp.roll(before, -(offset + per) * stride, axis=-1)]
    concatenate x28 -> x0, local copies, waits for them, and re-layouts: 48.1 us -> none  [the longest x16 36.4 us: cell_offset(): same = jnp.roll(center, -offset * stride, axis=-1)]
    div x3 -> x0, other arithmetic: 45.9 us -> none  [sixth_order(): (45.0 * (getter(1) - getter(-1)) - 9.0 * (getter(2) - getter(-2)) + (gett...]
    scatter-add x1 -> x0, other arithmetic: 34.7 us -> none  [assemble(): summed = jax.ops.segment_sum(patches, slot_index, num_segments=slot_count)]
    all_to_all x0 -> x1, blocking collectives: none -> 25 us  [exchange(): return lax.all_to_all(value, AXES, split_axis=0, concat_axis=0, tiled=True)]
    scatter x2 -> x0, local copies, waits for them, and re-layouts: 17.7 us -> none  [the longest x1 16.3 us: on_device(): jnp.zeros((buffer_rows, 3, 128), jnp.float32).at[targets].set(patches)]
  transfers between devices with their start and end apart: 11 -> 10, of which waited for: 1 -> 3; matrix products, arithmetic and copies ran while one was open for 69% -> 4% of each run, Pallas kernels for 0% -> 16%
where the time goes in v1:
time: 159 us; the launch traced here: 158 us
  Pallas kernels  62.9 us (40%)
  starting transfers between devices  40.6 us (26%)
  blocking collectives  25 us (16%)
  local copies, waits for them, and re-layouts  15.5 us (10%)
  waiting for transfers between devices  11.1 us (7%)
  other arithmetic  2.17 us (1%)
    pallas_call x1, Pallas kernels, owner_work(): pl.pallas_call(owner_kernel, out_shape=[sds((3072, 128)), sds((1536, 128)...  36 us
    all_to_all x1, blocking collectives, exchange(): return lax.all_to_all(value, AXES, split_axis=0, concat_axis=0, tiled=True)  25 us
    ppermute x8, starting transfers between devices, stepped(): lax.ppermute(value, axis, [(source, source + step) for source in range(fi...  22.9 us
    pallas_call x1, Pallas kernels, gradient(): pl.pallas_call(gradient_kernel, out_shape=sds((GRAD_ROWS + GRAD_PAD, 128)...  17.9 us
    all_to_all x2, starting transfers between devices, exchange(): return lax.all_to_all(value, AXES, split_axis=0, concat_axis=0, tiled=True)  17.8 us
    unnamed x24, local copies, waits for them, and re-layouts  10.9 us
    ppermute x8, waiting for transfers between devices, stepped(): lax.ppermute(value, axis, [(source, source + step) for source in range(fi...  7.56 us
    pallas_call x1, Pallas kernels, plan(): pl.pallas_call(plan_kernel, out_shape=[sds((256,), jnp.int32), sds((512,)...  3.83 us
  transfers between devices with their start and end apart: 10, of which 3 were waited for; matrix products, arithmetic and copies ran while one was open for 4% of the time, Pallas kernels for 16%

profile of v1, /device:TPU:1, one launch (start us, length us, event | category | flops | bytes accessed | tf_op | source)
XLA Modules:
  0.0 158.0 jit_solution(18191098657119469257)
XLA Ops:
  3.2 4.9 %collective-permute-start = (f32[6,32,128]{2,1,0:T(8,128)S(1)}, f32[6,32,128]{2,1,0:T(8,128)S(1)}, u32[]{:S(2)}, u32[]{:S(2)}) collective-permute-start(f32[6,32,128]{2,1,0:T(8,128)S(1)} %get-tuple-element.12), channel_id=1, source_target_pairs={{0,4},{4,8},{8,12},{12,16},{16,20},{20,24},{24,28},{28,32},{32,36}... | collective-permute-start | bytes 294920 | tf_op jit(solution)/shard_map/ppermute | solution.py:319
  8.1 1.9 %collective-permute-start.1 = (f32[6,32,128]{2,1,0:T(8,128)S(1)}, f32[6,32,128]{2,1,0:T(8,128)S(1)}, u32[]{:S(2)}, u32[]{:S(2)}) collective-permute-start(f32[6,32,128]{2,1,0:T(8,128)S(1)} %get-tuple-element.13), channel_id=1, source_target_pairs={{4,0},{8,4},{12,8},{16,12},{20,16},{24,20},{28,24},{32,28},{36,32}... | collective-permute-start | bytes 294920 | tf_op jit(solution)/shard_map/ppermute | solution.py:319
  10.1 3.2 %collective-permute-start.2 = (f32[6,32,128]{2,1,0:T(8,128)S(1)}, f32[6,32,128]{2,1,0:T(8,128)S(1)}, u32[]{:S(2)}, u32[]{:S(2)}) collective-permute-start(f32[6,32,128]{2,1,0:T(8,128)S(1)} %get-tuple-element.14), channel_id=1, source_target_pairs={{0,1},{1,2},{2,3},{4,5},{5,6},{6,7},{8,9},{9,10},{10,11},{12,13},{... | collective-permute-start | bytes 294920 | tf_op jit(solution)/shard_map/ppermute | solution.py:319
  13.3 1.3 collective-permute-start.3
  14.6 3.8 %shard_map.77 = (s32[256]{0:T(256)}, s32[512]{0:T(512)}) custom-call(s32[256]{0:T(256)} %bitcast.20, s32[256]{0:T(256)} %slots.1), custom_call_target="tpu_custom_call" | custom-call | flops 4000 | bytes 6000 | tf_op jit(solution)/shard_map/pallas_call | solution.py:68
  18.4 1.4 reshape.25
  19.8 11.5 %all-to-all-start = ((s32[128,1,4]{2,1,0:T(1,128)}), s32[128,1,4]{2,1,0:T(1,128)S(1)}, u32[]{:S(2)}, u32[]{:S(2)}) async-start(s32[128,1,4]{2,1,0:T(1,128)} %bitcast.1), calls=%async_computation | async-start | bytes 131072 | tf_op jit(solution)/shard_map/all_to_all | solution.py:323
  34.6 3.0 %shard_map.79 = f32[3072,128]{1,0:T(8,128)} custom-call(s32[256]{0:T(256)S(1)} %copy-done.9, f32[3,128,128]{2,1,0:T(8,128)S(1)} %copy-done.4, f32[3,128,128]{2,1,0:T(8,128)S(1)} %copy-done.6, s32[4,128]{1,0:T(4,128)S(1)} %copy-done.8, f32[6,32,128]{2,1,0:T(8,128)S(1)} %collective-permute-done.a0, f32[6,32,128]{2,1,0:T(8,128)S(1)} %collective-permute-done.1.a1, ...), custom_call_target="tpu_custom_call" | custom-call | flops 1000000 | bytes 4000000 | tf_op jit(solution)/shard_map/pallas_call | solution.py:116
  37.7 3.5 %all-to-all-done = s32[128,1,4]{2,1,0:T(1,128)S(1)} async-done(((s32[128,1,4]{2,1,0:T(1,128)}), s32[128,1,4]{2,1,0:T(1,128)S(1)}, u32[]{:S(2)}, u32[]{:S(2)}) %all-to-all-start) | async-done | bytes 2080 | tf_op jit(solution)/shard_map/all_to_all | solution.py:323
  41.8 6.2 %all-to-all-start.1 = ((f32[128,24,128]{2,1,0:T(8,128)}), f32[128,24,128]{2,1,0:T(8,128)S(1)}, u32[]{:S(2)}, u32[]{:S(2)}) async-start(f32[128,24,128]{2,1,0:T(8,128)} %bitcast.2), calls=%async_computation.1 | async-start | bytes 3145728 | tf_op jit(solution)/shard_map/all_to_all | solution.py:323
  49.0 3.0 %collective-permute-start.5 = (f32[16,3,16,128]{3,2,1,0:T(8,128)}, f32[16,3,16,128]{3,2,1,0:T(8,128)S(1)}, u32[]{:S(2)}, u32[]{:S(2)}) collective-permute-start(f32[16,3,16,128]{3,2,1,0:T(8,128)} %get-tuple-element.20), channel_id=1, source_target_pairs={{4,0},{8,4},{12,8},{16,12},{20,16},{24,20},{28,24},{32,28},{36,32}... | collective-permute-start | bytes 1179656 | tf_op jit(solution)/shard_map/ppermute | solution.py:319
  52.0 2.6 %collective-permute-start.4 = (f32[16,3,16,128]{3,2,1,0:T(8,128)}, f32[16,3,16,128]{3,2,1,0:T(8,128)}, u32[]{:S(2)}, u32[]{:S(2)}) collective-permute-start(f32[16,3,16,128]{3,2,1,0:T(8,128)} %get-tuple-element.21), channel_id=1, source_target_pairs={{0,4},{4,8},{8,12},{12,16},{16,20},{20,24},{24,28},{28,32},{32,36}... | collective-permute-start | bytes 1179656 | tf_op jit(solution)/shard_map/ppermute | solution.py:319
  55.4 1.3 collective-permute-start.7
  56.7 4.6 %collective-permute-start.6 = (f32[4,16,3,1,128]{4,3,2,1,0:T(1,128)}, f32[4,16,3,1,128]{4,3,2,1,0:T(1,128)}, u32[]{:S(2)}, u32[]{:S(2)}) collective-permute-start(f32[4,16,3,1,128]{4,3,2,1,0:T(1,128)} %get-tuple-element.19), channel_id=1, source_target_pairs={{0,1},{1,2},{2,3},{4,5},{5,6},{6,7},{8,9},{9,10},{10,11},{12,13},{... | collective-permute-start | bytes 294920 | tf_op jit(solution)/shard_map/ppermute | solution.py:319
  61.8 2.2 %reduce.3 = s32[128,4]{1,0:T(8,128)} reduce(s32[128,1,4]{2,1,0:T(1,128)} %copy-done.11, s32[]{:T(128)} %broadcast.3), dimensions={1}, to_apply=%all_to_all.9.reduce_sub_computation.3 | reduce | bytes 4100 | tf_op jit(solution)/shard_map/all_to_all | solution.py:323
  64.0 0.9 reshape.26.marks
  64.9 3.6 %collective-permute-done.7.za = f32[4,16,3,1,128]{4,3,2,1,0:T(1,128)} collective-permute-done((f32[4,16,3,1,128]{4,3,2,1,0:T(1,128)}, f32[4,16,3,1,128]{4,3,2,1,0:T(1,128)}, u32[]{:S(2)}, u32[]{:S(2)}) %collective-permute-start.7) | collective-permute-done | bytes 98336 | tf_op jit(solution)/shard_map/ppermute | solution.py:319
  68.5 4.0 %collective-permute-done.5.xa = f32[16,3,16,128]{3,2,1,0:T(8,128)S(1)} collective-permute-done((f32[16,3,16,128]{3,2,1,0:T(8,128)}, f32[16,3,16,128]{3,2,1,0:T(8,128)S(1)}, u32[]{:S(2)}, u32[]{:S(2)}) %collective-permute-start.5) | collective-permute-done | bytes 393248 | tf_op jit(solution)/shard_map/ppermute | solution.py:319
  72.5 17.9 %shard_map.80.grads = f32[9344,128]{1,0:T(8,128)S(1)} custom-call(f32[4,16,3,16,128]{4,3,2,1,0:T(8,128)S(1)} %bitcast.17, f32[16,3,16,128]{3,2,1,0:T(8,128)} %collective-permute-done.4.xb, f32[16,3,16,128]{3,2,1,0:T(8,128)S(1)} %collective-permute-done.5.xa, f32[4,16,3,1,128]{4,3,2,1,0:T(1,128)} %collective-permute-done.6.zb, ...), custom_call_target="tpu_custom_call" | custom-call | flops 20000000 | bytes 8000000 | tf_op jit(solution)/shard_map/pallas_call | solution.py:185
  90.4 2.2 %copy-done = f32[9344,128]{1,0:T(8,128)} copy-done((f32[9344,128]{1,0:T(8,128)}, f32[9344,128]{1,0:T(8,128)S(1)}, u32[]{:S(2)}) %copy-start) | copy-done | bytes 4784152
  92.5 2.4 %copy-done.1 = f32[9344,128]{1,0:T(8,128)S(1)} copy-done((f32[9344,128]{1,0:T(8,128)S(1)}, f32[9344,128]{1,0:T(8,128)}, u32[]{:S(2)}) %copy-start.1) | copy-done | bytes 4784152
  94.9 36.0 %shard_map.81 = (f32[3072,128]{1,0:T(8,128)}, f32[1536,128]{1,0:T(8,128)S(1)}) custom-call(s32[512]{0:T(512)S(1)} %reshape.26.marks, f32[3072,128]{1,0:T(8,128)S(1)} %bitcast.14, f32[9344,128]{1,0:T(8,128)S(1)} %copy-done.1), custom_call_target="tpu_custom_call" | custom-call | flops 300000000 | bytes 9000000 | tf_op jit(solution)/shard_map/pallas_call | solution.py:280
  130.9 25.0 %all_to_all.15 = f32[128,3,4,128]{3,2,1,0:T(4,128)S(1)} all-to-all(f32[128,3,4,128]{3,2,1,0:T(4,128)S(1)} %bitcast.19), channel_id=1, replica_groups=mesh['gx'=32,'gz'=4] {'gx','gz'}, dimensions={0} | all-to-all | bytes 1572864 | tf_op jit(solution)/shard_map/all_to_all | solution.py:323
  155.9 2.1 %shard_map.82 = f32[2,3,128,128]{3,2,1,0:T(8,128)} custom-call(s32[256]{0:T(256)S(1)} %copy-done.10, f32[1536,128]{1,0:T(8,128)S(1)} %bitcast.18), custom_call_target="tpu_custom_call" | custom-call | flops 1000000 | bytes 2000000 | tf_op jit(solution)/shard_map/pallas_call | solution.py:305
  (33 shorter events, 8.6 us)
Async XLA Ops:
  0.6 0.9 copy-start.3
  1.6 0.9 copy-start.5
  2.5 0.7 copy-start.7
  3.2 28.2 %collective-permute-start = (f32[6,32,128]{2,1,0:T(8,128)S(1)}, f32[6,32,128]{2,1,0:T(8,128)S(1)}, u32[]{:S(2)}, u32[]{:S(2)}) collective-permute-start(f32[6,32,128]{2,1,0:T(8,128)S(1)} %get-tuple-element.12), channel_id=1, source_target_pairs={{0,4},{4,8},{8,12},{12,16},{16,20},{20,24},{24,28},{28,32},{32,36}... | collective-permute-start | bytes 294920 | tf_op jit(solution)/shard_map/ppermute | solution.py:319
  8.1 23.3 %collective-permute-start.1 = (f32[6,32,128]{2,1,0:T(8,128)S(1)}, f32[6,32,128]{2,1,0:T(8,128)S(1)}, u32[]{:S(2)}, u32[]{:S(2)}) collective-permute-start(f32[6,32,128]{2,1,0:T(8,128)S(1)} %get-tuple-element.13), channel_id=1, source_target_pairs={{4,0},{8,4},{12,8},{16,12},{20,16},{24,20},{28,24},{32,28},{36,32}... | collective-permute-start | bytes 294920 | tf_op jit(solution)/shard_map/ppermute | solution.py:319
  10.1 21.4 %collective-permute-start.2 = (f32[6,32,128]{2,1,0:T(8,128)S(1)}, f32[6,32,128]{2,1,0:T(8,128)S(1)}, u32[]{:S(2)}, u32[]{:S(2)}) collective-permute-start(f32[6,32,128]{2,1,0:T(8,128)S(1)} %get-tuple-element.14), channel_id=1, source_target_pairs={{0,1},{1,2},{2,3},{4,5},{5,6},{6,7},{8,9},{9,10},{10,11},{12,13},{... | collective-permute-start | bytes 294920 | tf_op jit(solution)/shard_map/ppermute | solution.py:319
  13.3 18.1 %collective-permute-start.3 = (f32[6,32,128]{2,1,0:T(8,128)S(1)}, f32[6,32,128]{2,1,0:T(8,128)S(1)}, u32[]{:S(2)}, u32[]{:S(2)}) collective-permute-start(f32[6,32,128]{2,1,0:T(8,128)S(1)} %get-tuple-element.15), channel_id=1, source_target_pairs={{1,0},{2,1},{3,2},{5,4},{6,5},{7,6},{9,8},{10,9},{11,10},{13,12},{... | collective-permute-start | bytes 294920 | tf_op jit(solution)/shard_map/ppermute | solution.py:319
  19.8 21.4 %all-to-all-start = ((s32[128,1,4]{2,1,0:T(1,128)}), s32[128,1,4]{2,1,0:T(1,128)S(1)}, u32[]{:S(2)}, u32[]{:S(2)}) async-start(s32[128,1,4]{2,1,0:T(1,128)} %bitcast.1), calls=%async_computation | async-start | bytes 131072 | tf_op jit(solution)/shard_map/all_to_all | solution.py:323
  31.4 0.9 copy-start.4
  32.4 0.9 copy-start.6
  33.3 0.7 copy-start.8
  34.0 0.7 copy-start.9
  41.2 0.6 copy-start.11
  41.2 6.9 %copy-start.2 = (f32[4,16,16,3,128]{4,2,3,1,0:T(8,128)S(1)}, f32[4,16,16,3,128]{4,2,3,1,0:T(8,128)}, u32[]{:S(2)}) copy-start(f32[4,16,16,3,128]{4,2,3,1,0:T(8,128)} %param.11) | copy-start | bytes 4718596
  41.8 50.7 %all-to-all-start.1 = ((f32[128,24,128]{2,1,0:T(8,128)}), f32[128,24,128]{2,1,0:T(8,128)S(1)}, u32[]{:S(2)}, u32[]{:S(2)}) async-start(f32[128,24,128]{2,1,0:T(8,128)} %bitcast.2), calls=%async_computation.1 | async-start | bytes 3145728 | tf_op jit(solution)/shard_map/all_to_all | solution.py:323
  49.0 23.5 %collective-permute-start.5 = (f32[16,3,16,128]{3,2,1,0:T(8,128)}, f32[16,3,16,128]{3,2,1,0:T(8,128)S(1)}, u32[]{:S(2)}, u32[]{:S(2)}) collective-permute-start(f32[16,3,16,128]{3,2,1,0:T(8,128)} %get-tuple-element.20), channel_id=1, source_target_pairs={{4,0},{8,4},{12,8},{16,12},{20,16},{24,20},{28,24},{32,28},{36,32}... | collective-permute-start | bytes 1179656 | tf_op jit(solution)/shard_map/ppermute | solution.py:319
  52.0 20.5 %collective-permute-start.4 = (f32[16,3,16,128]{3,2,1,0:T(8,128)}, f32[16,3,16,128]{3,2,1,0:T(8,128)}, u32[]{:S(2)}, u32[]{:S(2)}) collective-permute-start(f32[16,3,16,128]{3,2,1,0:T(8,128)} %get-tuple-element.21), channel_id=1, source_target_pairs={{0,4},{4,8},{8,12},{12,16},{16,20},{20,24},{24,28},{28,32},{32,36}... | collective-permute-start | bytes 1179656 | tf_op jit(solution)/shard_map/ppermute | solution.py:319
  55.4 13.1 %collective-permute-start.7 = (f32[4,16,3,1,128]{4,3,2,1,0:T(1,128)}, f32[4,16,3,1,128]{4,3,2,1,0:T(1,128)}, u32[]{:S(2)}, u32[]{:S(2)}) collective-permute-start(f32[4,16,3,1,128]{4,3,2,1,0:T(1,128)} %get-tuple-element.18), channel_id=1, source_target_pairs={{1,0},{2,1},{3,2},{5,4},{6,5},{7,6},{9,8},{10,9},{11,10},{13,12},{... | collective-permute-start | bytes 294920 | tf_op jit(solution)/shard_map/ppermute | solution.py:319
  56.7 11.8 %collective-permute-start.6 = (f32[4,16,3,1,128]{4,3,2,1,0:T(1,128)}, f32[4,16,3,1,128]{4,3,2,1,0:T(1,128)}, u32[]{:S(2)}, u32[]{:S(2)}) collective-permute-start(f32[4,16,3,1,128]{4,3,2,1,0:T(1,128)} %get-tuple-element.19), channel_id=1, source_target_pairs={{0,1},{1,2},{2,3},{4,5},{5,6},{6,7},{8,9},{9,10},{10,11},{12,13},{... | collective-permute-start | bytes 294920 | tf_op jit(solution)/shard_map/ppermute | solution.py:319
  90.4 2.2 %copy-start = (f32[9344,128]{1,0:T(8,128)}, f32[9344,128]{1,0:T(8,128)S(1)}, u32[]{:S(2)}) copy-start(f32[9344,128]{1,0:T(8,128)S(1)} %shard_map.80.grads) | copy-start | bytes 14352388
  92.5 2.4 %copy-start.1 = (f32[9344,128]{1,0:T(8,128)S(1)}, f32[9344,128]{1,0:T(8,128)}, u32[]{:S(2)}) copy-start(f32[9344,128]{1,0:T(8,128)} %copy-done) | copy-start | bytes 14352388
  130.9 25.0 %copy-start.10 = (s32[256]{0:T(256)S(1)}, s32[256]{0:T(256)}, u32[]{:S(2)}) copy-start(s32[256]{0:T(256)} %get-tuple-element.11.places) | copy-start | bytes 3076

commit v2 on v1

v2 whole, which is shorter than its diff:
```python
import jax
import jax.numpy as jnp
import numpy as np
from jax import lax
from jax.experimental import pallas as pl
from jax.experimental.pallas import tpu as pltpu
from jax.sharding import PartitionSpec as P

AXES = ("gx", "gz")
F32 = jnp.float32
BF16 = jnp.bfloat16
VMEM = pl.BlockSpec(memory_space=pltpu.VMEM)
SMEM = pl.BlockSpec(memory_space=pltpu.SMEM)
ANY = pl.BlockSpec(memory_space=pl.ANY)
PARAMS = pltpu.CompilerParams(vmem_limit_bytes=16 * 1024 * 1024)
GRAD_ROWS = 64 * 9 * 16
GRAD_PAD = 128
GROUP = 8


def sds(shape, dtype=F32):
    return jax.ShapeDtypeStruct(shape, dtype)


def cost(flops, read):
    return pl.CostEstimate(flops=flops, bytes_accessed=read, transcendentals=0)


def depart_kernel(vort, pos, counts, d0, d1, d2, d3, v_here, p_here, c_here, sems):
    copies = [
        pltpu.make_async_copy(source, target, sems.at[n])
        for n, (source, target) in enumerate(((counts, c_here), (vort, v_here), (pos, p_here)))
    ]
    for copy in copies:
        copy.start()
    for copy in copies:
        copy.wait()
    place = lax.broadcasted_iota(jnp.int32, (32, 128), 0)
    for heading, out in enumerate((d0, d1, d2, d3)):
        leaves = place < c_here[heading : heading + 1, :]
        rows = slice(heading * 32, heading * 32 + 32)
        for i in range(3):
            out[i] = jnp.where(leaves, v_here[i, rows, :], 0.0)
            out[3 + i] = jnp.where(leaves, p_here[i, rows, :], 0.0)


def depart(vort, pos, counts):
    return pl.pallas_call(
        depart_kernel,
        out_shape=[sds((6, 32, 128))] * 4,
        in_specs=[ANY] * 3,
        out_specs=[VMEM] * 4,
        scratch_shapes=[
            pltpu.VMEM((3, 128, 128), F32),
            pltpu.VMEM((3, 128, 128), F32),
            pltpu.VMEM((4, 128), jnp.int32),
            pltpu.SemaphoreType.DMA((3,)),
        ],
        compiler_params=PARAMS,
        cost_estimate=cost(400_000, 1_600_000),
        name="depart",
    )(vort, pos, counts)


ORDER = (3, 4, 0, 1, 2, 5)


def send_rows(places, turned, ship, first):
    def move(r, carry):
        place = places[first + r]
        base = (place >> 2) * 28 + (place & 3)
        ship[pl.ds(base, 7, stride=4), :] = turned[pl.ds(r, 7, stride=128), :]
        return carry

    lax.fori_loop(0, 128, move, 0, unroll=8)


def slot_rows(slots, half, turned):
    row = slots[half : half + 1, :].astype(F32)
    turned[768:896, :] = jnp.broadcast_to(row, (128, 128)).T


def keep_kernel(owners, vort, pos, counts, slots, places, turned, tally):
    for i in range(128):
        tally[i] = 0

    def rank_of(r, carry):
        owner = owners[r]
        rank = tally[owner]
        tally[owner] = rank + 1
        places[r] = owner * 4 + rank
        return carry

    lax.fori_loop(0, 256, rank_of, 0, unroll=8)
    place = lax.broadcasted_iota(jnp.int32, (32, 128), 0)
    leaves = [place < counts[heading : heading + 1, :] for heading in range(4)]
    for at, comp in enumerate(ORDER):
        if comp < 3:
            kept = jnp.concatenate(
                [
                    jnp.where(leaves[h], 0.0, vort[comp, 32 * h : 32 * h + 32, :])
                    for h in range(4)
                ],
                axis=0,
            )
        else:
            kept = pos[comp - 3]
        turned[at * 128 : at * 128 + 128, :] = kept.T
    slot_rows(slots, 0, turned)


def keep(owners, vort, pos, counts, slots):
    return pl.pallas_call(
        keep_kernel,
        out_shape=[sds((256,), jnp.int32), sds((896, 128))],
        in_specs=[SMEM] + [VMEM] * 4,
        out_specs=[SMEM, VMEM],
        scratch_shapes=[pltpu.SMEM((128,), jnp.int32)],
        compiler_params=PARAMS,
        cost_estimate=cost(1_000_000, 4_000_000),
        name="keep",
    )(owners, vort, pos, counts, slots)


def route_kernel(places, slots, a0, a1, a2, a3, kept, ship, turned):
    def clear(i, carry):
        ship[pl.ds(pl.multiple_of(i * 64, 64), 64), :] = jnp.zeros((64, 128), F32)
        return carry

    lax.fori_loop(0, 56, clear, 0)
    send_rows(places, kept, ship, 0)
    for at, comp in enumerate(ORDER):
        came = jnp.concatenate([a[comp] for a in (a0, a1, a2, a3)], axis=0)
        turned[at * 128 : at * 128 + 128, :] = came.T
    slot_rows(slots, 1, turned)
    send_rows(places, turned, ship, 128)


def route(places, slots, arrivals, kept):
    return pl.pallas_call(
        route_kernel,
        out_shape=sds((3584, 128)),
        in_specs=[SMEM] + [VMEM] * 6,
        out_specs=VMEM,
        scratch_shapes=[pltpu.VMEM((896, 128), F32)],
        compiler_params=PARAMS,
        cost_estimate=cost(1_000_000, 4_000_000),
        name="route",
    )(places, slots, *arrivals, kept)


def stencil(stride, per):
    here, before, after = (np.zeros((128, 128), np.float32) for _ in range(3))
    factors = {1: 45.0, -1: -45.0, 2: -9.0, -2: 9.0, 3: 1.0, -3: -1.0}
    for lane in range(128):
        digit = lane // stride % per
        for offset, factor in factors.items():
            at = lane + offset * stride
            if digit + offset >= per:
                after[at - per * stride, lane] = factor
            elif digit + offset < 0:
                before[at + per * stride, lane] = factor
            else:
                here[at, lane] = factor
    return here, before, after


def matrices():
    along_x = np.concatenate(stencil(32, 4) * 2)
    along_y = np.concatenate(stencil(8, 4) * 2)
    here, before, after = stencil(1, 8)
    along_z = np.concatenate((here, before + after) * 2)
    return [jnp.asarray(m, BF16) for m in (along_x, along_y, along_z)]


def split(value):
    high = value.astype(BF16)
    return high, (value - high.astype(F32)).astype(BF16)


def gradient_kernel(vel, xb, xa, zb, za, mx, my, mz, out, high, low, z_high, z_low):
    late = lax.broadcasted_iota(jnp.int32, (16, 128), 1) % 8 >= 5

    def put(sx, sy, value):
        at = pl.ds(pl.multiple_of((sx * 18 + sy) * 48, 16), 48)
        high[at, :], low[at, :] = split(value)

    def fill(sy, carry):
        rows = pl.ds(pl.multiple_of(sy * 48, 16), 48)
        put(0, sy + 1, xb[rows, :])
        put(5, sy + 1, xa[rows, :])
        for sx in range(4):
            row = (sx * 16 + sy) * 48
            value = vel[pl.ds(pl.multiple_of(row, 16), 48), :]
            put(sx + 1, sy + 1, value)
            for i in range(3):
                c = value[16 * i : 16 * i + 16]
                edge = pl.ds((sx * 16 + sy) * 3 + i, 1)
                before = jnp.concatenate([zb[edge, :], c[:15]], axis=0)
                after = jnp.concatenate([c[1:], za[edge, :]], axis=0)
                at = pl.ds(pl.multiple_of(row + 16 * i, 16), 16)
                z_high[at, :], z_low[at, :] = split(jnp.where(late, before, after))
        return carry

    lax.fori_loop(0, 16, fill, 0)
    for sx in range(4):
        put(sx + 1, 0, vel[(sx * 16 + 15) * 48 : (sx * 16 + 16) * 48, :])
        put(sx + 1, 17, vel[sx * 16 * 48 : (sx * 16 + 1) * 48, :])

    def per_x(sx, carry):
        def part(ref, dx, dy):
            at = pl.multiple_of(((sx + 1 + dx) * 18 + 1 + dy) * 48, 16)
            return ref[pl.ds(at, 768), :]

        both = (high, low)
        own = pl.ds(pl.multiple_of(sx * 768, 16), 768)
        along_x = [part(ref, dx, 0) for ref in both for dx in (0, -1, 1)]
        along_y = [part(ref, 0, dy) for ref in both for dy in (0, -1, 1)]
        along_z = [part(high, 0, 0), z_high[own, :], part(low, 0, 0), z_low[own, :]]
        for j, (parts, matrix) in enumerate(((along_x, mx), (along_y, my), (along_z, mz))):
            value = jnp.dot(
                jnp.concatenate(parts, axis=1), matrix[...], preferred_element_type=F32
            ) * (1.0 / 60.0)
            for sy in range(16):
                at = pl.multiple_of(((sx * 16 + sy) * 9 + 3 * j) * 16, 16)
                out[pl.ds(at, 48), :] = value[48 * sy : 48 * sy + 48]
        return carry

    lax.fori_loop(0, 4, per_x, 0)
    out[GRAD_ROWS:, :] = jnp.zeros((GRAD_PAD, 128), F32)


def gradient(vel, xb, xa, zb, za):
    return pl.pallas_call(
        gradient_kernel,
        out_shape=sds((GRAD_ROWS + GRAD_PAD, 128)),
        in_specs=[VMEM] * 8,
        out_specs=VMEM,
        scratch_shapes=[pltpu.VMEM((6 * 18 * 48, 128), BF16)] * 2
        + [pltpu.VMEM((3072, 128), BF16)] * 2,
        compiler_params=PARAMS,
        cost_estimate=cost(20_000_000, 8_000_000),
        name="gradient",
    )(vel, xb, xa, zb, za, *matrices())


def owner_kernel(rows, grads, mesh, back):
    def clear(i, carry):
        mesh[pl.ds(pl.multiple_of(i * 64, 64), 64), :] = jnp.zeros((64, 128), F32)
        return carry

    lax.fori_loop(0, 48, clear, 0)
    cell_z = lax.broadcasted_iota(jnp.int32, (8, 128), 0).astype(F32)

    def wide(row):
        return jnp.broadcast_to(row, (8, 128))

    def per_source(s, base):
        f = rows[pl.ds(base, 8), :] - 1.0
        g = 1.0 - f
        weights = (
            -0.5 * f * g * g,
            1.0 + f * f * (1.5 * f - 2.5),
            1.0 + g * g * (1.5 * g - 2.5),
            -0.5 * g * f * f,
        )
        slots = rows[pl.ds(base + 24, 4), :].astype(jnp.int32)
        for k in range(4):
            slot = slots[k, 0]
            column = slot >> 4
            level = slot & 15
            z = wide(rows[pl.ds(base + 20 + k, 1), :])
            radius = jnp.abs(cell_z - z)
            rest = jnp.maximum(2.0 - radius, 0.0)
            along_z = jnp.where(
                radius < 1.0,
                1.0 + radius * radius * (1.5 * radius - 2.5),
                0.5 * rest * rest * (1.0 - radius),
            )
            yz = [wide(weights[b][4 + k : 5 + k]) * along_z for b in range(4)]
            xs = [wide(weights[a][k : k + 1]) for a in range(4)]
            table = jnp.concatenate([xs[a] * yz[b] for a in range(4) for b in range(4)], axis=0)
            high, low = split(table)

            vortex = [rows[pl.ds(base + 8 + 4 * j + k, 1), :] for j in range(3)]
            grad = jnp.concatenate(
                [
                    grads[pl.ds(column * 144 + j * 48 + level, 8, stride=16), :]
                    for j in range(3)
                ],
                axis=0,
            )
            left = jnp.concatenate(split(grad), axis=0)
            left = jnp.concatenate([left, left], axis=1)
            sampled = jnp.dot(
                left, jnp.concatenate([high, low], axis=0), preferred_element_type=F32
            )
            sampled = sampled[:24] + sampled[24:]
            stretch = (
                sampled[0:8] * wide(vortex[0])
                + sampled[8:16] * wide(vortex[1])
                + sampled[16:24] * wide(vortex[2])
            )
            back[pl.ds(s * 12 + k, 3, stride=4), :] = stretch[:3]

            v = jnp.concatenate(vortex + [jnp.zeros((5, 128), F32)], axis=0)
            left = jnp.concatenate(split(v), axis=0)
            left = jnp.concatenate([left, left], axis=1)
            patch = lax.dot_general(
                left,
                jnp.concatenate([high, low], axis=1),
                (((1,), (1,)), ((), ())),
                preferred_element_type=F32,
            )
            patch = patch[:3] + patch[8:11]
            at = pl.ds(column * 48 + level, 3, stride=16)
            mesh[at, :] = mesh[at, :] + patch

    def per_group(q, carry):
        base = pl.multiple_of(q * (28 * GROUP), 8)
        for u in range(GROUP):
            per_source(q * GROUP + u, base + 28 * u)
        return carry

    lax.fori_loop(0, 128 // GROUP, per_group, 0)


def owner_work(rows, grads):
    return pl.pallas_call(
        owner_kernel,
        out_shape=[sds((3072, 128)), sds((1536, 128))],
        in_specs=[VMEM, VMEM],
        out_specs=[VMEM] * 2,
        compiler_params=PARAMS,
        cost_estimate=cost(300_000_000, 9_000_000),
        name="owner",
    )(rows, grads)


def unpack_kernel(places, back, out, turned):
    def move(r, carry):
        place = places[r]
        base = (place >> 2) * 12 + (place & 3)
        turned[pl.ds(r, 3, stride=256), :] = back[pl.ds(base, 3, stride=4), :]
        return carry

    lax.fori_loop(0, 256, move, 0, unroll=8)
    for h in range(2):
        for i in range(3):
            at = i * 256 + h * 128
            out[h, i] = turned[at : at + 128, :].T


def unpack(places, back):
    return pl.pallas_call(
        unpack_kernel,
        out_shape=sds((2, 3, 128, 128)),
        in_specs=[SMEM, VMEM],
        out_specs=VMEM,
        scratch_shapes=[pltpu.VMEM((768, 128), F32)],
        compiler_params=PARAMS,
        cost_estimate=cost(1_000_000, 2_000_000),
        name="unpack",
    )(places, back)


def stepped(value, axis, step):
    count = lax.axis_size(axis)
    first, last = (max(0, -step), min(count, count - step))
    return lax.ppermute(value, axis, [(source, source + step) for source in range(first, last)])


def exchange(value):
    return lax.all_to_all(value, AXES, split_axis=0, concat_axis=0, tiled=True)


def on_device(vorticity, position, counts, owner_ids, slot_ids, velocity):
    slots = slot_ids.reshape(2, 128)
    leaving = depart(vorticity, position, counts)
    arrivals = [
        stepped(leaving[0], "gx", 1),
        stepped(leaving[1], "gx", -1),
        stepped(leaving[2], "gz", 1),
        stepped(leaving[3], "gz", -1),
    ]
    places, kept = keep(owner_ids[:, 0], vorticity, position, counts, slots)
    ship = route(places, slots, arrivals, kept)
    rows = exchange(ship.reshape(128, 7, 4, 128)).reshape(3584, 128)

    vel = jnp.transpose(velocity, (0, 1, 3, 2, 4))
    xb = stepped(vel[3].reshape(768, 128), "gx", 1)
    xa = stepped(vel[0].reshape(768, 128), "gx", -1)
    zb = stepped(vel[:, :, :, 15].reshape(192, 128), "gz", 1)
    za = stepped(vel[:, :, :, 0].reshape(192, 128), "gz", -1)
    grads = gradient(vel.reshape(3072, 128), xb, xa, zb, za)

    mesh, back = owner_work(rows, grads)
    back = exchange(back.reshape(128, 3, 4, 128)).reshape(1536, 128)
    stretching = unpack(places, back)
    mesh = jnp.transpose(mesh.reshape(4, 16, 3, 16, 128), (0, 1, 3, 2, 4))
    return mesh, stretching


def solution(mesh):
    placed = (
        P(None, None, AXES),
        P(None, None, AXES),
        P(None, AXES),
        P(AXES, None),
        P(AXES),
        P("gx", None, "gz", None, None),
    )
    return jax.shard_map(
        on_device,
        mesh=mesh,
        in_specs=placed,
        out_specs=(P("gx", None, "gz", None, None), P(None, None, None, AXES)),
        check_vma=False,
    )
```

time: 159 us -> 120 us (0.75)
  Pallas kernels: 62.9 us -> 32.7 us
  starting transfers between devices: 40.6 us -> 33.1 us
  waiting for transfers between devices: 11.1 us -> 16.8 us
  local copies, waits for them, and re-layouts: 15.5 us -> 11.2 us
  other arithmetic: 2.17 us -> 0 us
    pallas_call x1, Pallas kernels: 36 us -> 19.5 us  [owner_work(): pl.pallas_call(owner_kernel, out_shape=[sds((3072, 128)), sds((1536, 128)...]
    pallas_call x1, Pallas kernels: 17.9 us -> 4.8 us  [gradient(): pl.pallas_call(gradient_kernel, out_shape=sds((GRAD_ROWS + GRAD_PAD, 128)...]
    ppermute x8, waiting for transfers between devices: 7.56 us -> 16.8 us  [stepped(): lax.ppermute(value, axis, [(source, source + step) for source in range(fi...]
    all_to_all x2 -> x1, starting transfers between devices: 17.8 us -> 11.5 us  [exchange(): return lax.all_to_all(value, AXES, split_axis=0, concat_axis=0, tiled=True)]
    all_to_all x2 -> x1, waiting for transfers between devices: 3.54 us -> 0.01 us  [exchange(): return lax.all_to_all(value, AXES, split_axis=0, concat_axis=0, tiled=True)]
    reshape x2 -> x0, local copies, waits for them, and re-layouts: 2.36 us -> none  [on_device(): marks = exchange(marks.reshape(128, 1, 4)).reshape(512)]
    all_to_all x1 -> x0, other arithmetic: 2.17 us -> none  [exchange(): return lax.all_to_all(value, AXES, split_axis=0, concat_axis=0, tiled=True)]
    unnamed x24 -> x28, local copies, waits for them, and re-layouts: 10.9 us -> 11 us
  transfers between devices with their start and end apart: 10 -> 9, of which waited for: 3 -> 4; matrix products, arithmetic and copies ran while one was open for 4% -> 0% of each run, Pallas kernels for 16% -> 6%
where the time goes in v2:
time: 120 us
  starting transfers between devices  33.1 us (28%)
  Pallas kernels  32.7 us (27%)
  blocking collectives  25 us (21%)
  waiting for transfers between devices  16.8 us (14%)
  local copies, waits for them, and re-layouts  11.2 us (9%)
    all_to_all x1, blocking collectives, exchange(): return lax.all_to_all(value, AXES, split_axis=0, concat_axis=0, tiled=True)  25 us
    ppermute x8, starting transfers between devices, stepped(): lax.ppermute(value, axis, [(source, source + step) for source in range(fi...  21.5 us
    pallas_call x1, Pallas kernels, owner_work(): pl.pallas_call(owner_kernel, out_shape=[sds((3072, 128)), sds((1536, 128)...  19.5 us
    ppermute x8, waiting for transfers between devices, stepped(): lax.ppermute(value, axis, [(source, source + step) for source in range(fi...  16.8 us
    all_to_all x1, starting transfers between devices, exchange(): return lax.all_to_all(value, AXES, split_axis=0, concat_axis=0, tiled=True)  11.5 us
    unnamed x28, local copies, waits for them, and re-layouts  11 us
    pallas_call x1, Pallas kernels, gradient(): pl.pallas_call(gradient_kernel, out_shape=sds((GRAD_ROWS + GRAD_PAD, 128)...  4.8 us
    pallas_call x1, Pallas kernels, route(): pl.pallas_call(route_kernel, out_shape=sds((3584, 128)), in_specs=[SMEM]...  3.27 us
  transfers between devices with their start and end apart: 9, of which 4 were waited for; matrix products, arithmetic and copies ran while one was open for 0% of the time, Pallas kernels for 6%

profile of v2, /device:TPU:1, one launch (start us, length us, event | category | flops | bytes accessed | tf_op | source)
XLA Modules:
  0.0 119.6 jit_solution(533491814933055191)
XLA Ops:
  0.6 0.9 copy-done.3
  1.6 0.9 copy-done.5
  3.7 4.9 %collective-permute-start = (f32[6,32,128]{2,1,0:T(8,128)S(1)}, f32[6,32,128]{2,1,0:T(8,128)S(1)}, u32[]{:S(2)}, u32[]{:S(2)}) collective-permute-start(f32[6,32,128]{2,1,0:T(8,128)S(1)} %get-tuple-element.11), channel_id=1, source_target_pairs={{0,4},{4,8},{8,12},{12,16},{16,20},{20,24},{24,28},{28,32},{32,36}... | collective-permute-start | bytes 294920 | tf_op jit(solution)/shard_map/ppermute | solution.py:370
  8.7 1.9 %collective-permute-start.1 = (f32[6,32,128]{2,1,0:T(8,128)S(1)}, f32[6,32,128]{2,1,0:T(8,128)S(1)}, u32[]{:S(2)}, u32[]{:S(2)}) collective-permute-start(f32[6,32,128]{2,1,0:T(8,128)S(1)} %get-tuple-element.12), channel_id=1, source_target_pairs={{4,0},{8,4},{12,8},{16,12},{20,16},{24,20},{28,24},{32,28},{36,32}... | collective-permute-start | bytes 294920 | tf_op jit(solution)/shard_map/ppermute | solution.py:370
  10.6 3.2 %collective-permute-start.2 = (f32[6,32,128]{2,1,0:T(8,128)S(1)}, f32[6,32,128]{2,1,0:T(8,128)S(1)}, u32[]{:S(2)}, u32[]{:S(2)}) collective-permute-start(f32[6,32,128]{2,1,0:T(8,128)S(1)} %get-tuple-element.13), channel_id=1, source_target_pairs={{0,1},{1,2},{2,3},{4,5},{5,6},{6,7},{8,9},{9,10},{10,11},{12,13},{... | collective-permute-start | bytes 294920 | tf_op jit(solution)/shard_map/ppermute | solution.py:370
  13.8 1.3 %collective-permute-start.3 = (f32[6,32,128]{2,1,0:T(8,128)S(1)}, f32[6,32,128]{2,1,0:T(8,128)S(1)}, u32[]{:S(2)}, u32[]{:S(2)}) collective-permute-start(f32[6,32,128]{2,1,0:T(8,128)S(1)} %get-tuple-element.14), channel_id=1, source_target_pairs={{1,0},{2,1},{3,2},{5,4},{6,5},{7,6},{9,8},{10,9},{11,10},{13,12},{... | collective-permute-start | bytes 294920 | tf_op jit(solution)/shard_map/ppermute | solution.py:370
  16.0 0.9 copy-done.6
  19.0 2.5 %keep.1 = (s32[256]{0:T(256)S(1)}, f32[896,128]{1,0:T(8,128)S(1)}) custom-call(s32[256]{0:T(256)S(1)} %bitcast.24, f32[3,128,128]{2,1,0:T(8,128)S(1)} %copy-done.4, f32[3,128,128]{2,1,0:T(8,128)S(1)} %copy-done.6, s32[4,128]{1,0:T(4,128)S(1)} %copy-done.11, s32[2,128]{1,0:T(2,128)S(1)} %bitcast.22), custom_call_target="tpu_custom_call" | custom-call | flops 1000000 | bytes 4000000 | tf_op jit(solution)/shard_map/keep/pallas_call | solution.py:113
  21.6 3.3 %route.1 = f32[3584,128]{1,0:T(8,128)} custom-call(s32[256]{0:T(256)S(1)} %get-tuple-element.10.places, s32[2,128]{1,0:T(2,128)S(1)} %bitcast.23, f32[6,32,128]{2,1,0:T(8,128)S(1)} %collective-permute-done.a0, f32[6,32,128]{2,1,0:T(8,128)S(1)} %collective-permute-done.1.a1, f32[6,32,128]{2,1,0:T(8,128)S(1)} %collective-permute-done.2.a2, ...), custom_call_target="tpu_custom_call" | custom-call | flops 1000000 | bytes 4000000 | tf_op jit(solution)/shard_map/route/pallas_call | solution.py:140
  24.9 11.5 %all-to-all-start = ((f32[128,7,4,128]{3,2,1,0:T(4,128)}), f32[128,7,4,128]{3,2,1,0:T(4,128)S(1)}, u32[]{:S(2)}, u32[]{:S(2)}) async-start(f32[128,7,4,128]{3,2,1,0:T(4,128)} %bitcast.2), calls=%async_computation | async-start | bytes 3670016 | tf_op jit(solution)/shard_map/all_to_all | solution.py:374
  36.5 3.8 %collective-permute-start.4 = (f32[768,128]{1,0:T(8,128)S(1)}, f32[768,128]{1,0:T(8,128)S(1)}, u32[]{:S(2)}, u32[]{:S(2)}) collective-permute-start(f32[768,128]{1,0:T(8,128)S(1)} %bitcast.26), channel_id=1, source_target_pairs={{0,4},{4,8},{8,12},{12,16},{16,20},{20,24},{24,28},{28,32},{32,36}... | collective-permute-start | bytes 1179656 | tf_op jit(solution)/shard_map/ppermute | solution.py:370
  40.3 1.9 %collective-permute-start.5 = (f32[768,128]{1,0:T(8,128)S(1)}, f32[768,128]{1,0:T(8,128)S(1)}, u32[]{:S(2)}, u32[]{:S(2)}) collective-permute-start(f32[768,128]{1,0:T(8,128)S(1)} %bitcast.25), channel_id=1, source_target_pairs={{4,0},{8,4},{12,8},{16,12},{20,16},{24,20},{28,24},{32,28},{36,32}... | collective-permute-start | bytes 1179656 | tf_op jit(solution)/shard_map/ppermute | solution.py:370
  42.4 3.2 %collective-permute-start.6 = (f32[192,128]{1,0:T(8,128)S(1)}, f32[192,128]{1,0:T(8,128)S(1)}, u32[]{:S(2)}, u32[]{:S(2)}) collective-permute-start(f32[192,128]{1,0:T(8,128)S(1)} %bitcast.28), channel_id=1, source_target_pairs={{0,1},{1,2},{2,3},{4,5},{5,6},{6,7},{8,9},{9,10},{10,11},{12,13},{... | collective-permute-start | bytes 294920 | tf_op jit(solution)/shard_map/ppermute | solution.py:370
  45.6 1.3 %collective-permute-start.7 = (f32[192,128]{1,0:T(8,128)S(1)}, f32[192,128]{1,0:T(8,128)S(1)}, u32[]{:S(2)}, u32[]{:S(2)}) collective-permute-start(f32[192,128]{1,0:T(8,128)S(1)} %bitcast.27), channel_id=1, source_target_pairs={{1,0},{2,1},{3,2},{5,4},{6,5},{7,6},{9,8},{10,9},{11,10},{13,12},{... | collective-permute-start | bytes 294920 | tf_op jit(solution)/shard_map/ppermute | solution.py:370
  46.9 5.8 %collective-permute-done.6.zb = f32[192,128]{1,0:T(8,128)S(1)} collective-permute-done((f32[192,128]{1,0:T(8,128)S(1)}, f32[192,128]{1,0:T(8,128)S(1)}, u32[]{:S(2)}, u32[]{:S(2)}) %collective-permute-start.6) | collective-permute-done | bytes 98336 | tf_op jit(solution)/shard_map/ppermute | solution.py:370
  52.7 6.5 %collective-permute-done.7.za = f32[192,128]{1,0:T(8,128)S(1)} collective-permute-done((f32[192,128]{1,0:T(8,128)S(1)}, f32[192,128]{1,0:T(8,128)S(1)}, u32[]{:S(2)}, u32[]{:S(2)}) %collective-permute-start.7) | collective-permute-done | bytes 98336 | tf_op jit(solution)/shard_map/ppermute | solution.py:370
  59.2 2.5 %collective-permute-done.4.xb = f32[768,128]{1,0:T(8,128)S(1)} collective-permute-done((f32[768,128]{1,0:T(8,128)S(1)}, f32[768,128]{1,0:T(8,128)S(1)}, u32[]{:S(2)}, u32[]{:S(2)}) %collective-permute-start.4) | collective-permute-done | bytes 393248 | tf_op jit(solution)/shard_map/ppermute | solution.py:370
  61.7 2.0 %collective-permute-done.5.xa = f32[768,128]{1,0:T(8,128)S(1)} collective-permute-done((f32[768,128]{1,0:T(8,128)S(1)}, f32[768,128]{1,0:T(8,128)S(1)}, u32[]{:S(2)}, u32[]{:S(2)}) %collective-permute-start.5) | collective-permute-done | bytes 393248 | tf_op jit(solution)/shard_map/ppermute | solution.py:370
  63.7 4.8 %gradient.1.grads = f32[9344,128]{1,0:T(8,128)S(1)} custom-call(f32[3072,128]{1,0:T(8,128)S(1)} %bitcast.19, f32[768,128]{1,0:T(8,128)S(1)} %collective-permute-done.4.xb, f32[768,128]{1,0:T(8,128)S(1)} %collective-permute-done.5.xa, f32[192,128]{1,0:T(8,128)S(1)} %collective-permute-done.6.zb, f32[192,128]{1,0:T(8,128)S(1)} %collective-permute-done.7.za, ...), custom_call_target="tpu_custom_call" | custom-call | flops 20000000 | bytes 8000000 | tf_op jit(solution)/shard_map/gradient/pallas_call | solution.py:234
  68.5 2.2 %copy-done = f32[9344,128]{1,0:T(8,128)} copy-done((f32[9344,128]{1,0:T(8,128)}, f32[9344,128]{1,0:T(8,128)S(1)}, u32[]{:S(2)}) %copy-start) | copy-done | bytes 4784152
  70.7 2.4 %copy-done.1 = f32[9344,128]{1,0:T(8,128)S(1)} copy-done((f32[9344,128]{1,0:T(8,128)S(1)}, f32[9344,128]{1,0:T(8,128)}, u32[]{:S(2)}) %copy-start.1) | copy-done | bytes 4784152
  73.0 19.5 %owner.1 = (f32[3072,128]{1,0:T(8,128)}, f32[1536,128]{1,0:T(8,128)S(1)}) custom-call(f32[3584,128]{1,0:T(8,128)S(1)} %bitcast.16, f32[9344,128]{1,0:T(8,128)S(1)} %copy-done.1), custom_call_target="tpu_custom_call" | custom-call | flops 300000000 | bytes 9000000 | tf_op jit(solution)/shard_map/owner/pallas_call | solution.py:329
  92.5 25.0 %all_to_all.10 = f32[128,3,4,128]{3,2,1,0:T(4,128)S(1)} all-to-all(f32[128,3,4,128]{3,2,1,0:T(4,128)S(1)} %bitcast.21), channel_id=1, replica_groups=mesh['gx'=32,'gz'=4] {'gx','gz'}, dimensions={0} | all-to-all | bytes 1572864 | tf_op jit(solution)/shard_map/all_to_all | solution.py:374
  117.5 2.1 %unpack.1 = f32[2,3,128,128]{3,2,1,0:T(8,128)} custom-call(s32[256]{0:T(256)S(1)} %get-tuple-element.10.places, f32[1536,128]{1,0:T(8,128)S(1)} %bitcast.20), custom_call_target="tpu_custom_call" | custom-call | flops 1000000 | bytes 2000000 | tf_op jit(solution)/shard_map/unpack/pallas_call | solution.py:355
  (31 shorter events, 4.4 us)
Async XLA Ops:
  0.6 0.9 copy-start.3
  1.6 0.9 copy-start.5
  2.5 0.7 copy-start.10
  3.7 17.8 %collective-permute-start = (f32[6,32,128]{2,1,0:T(8,128)S(1)}, f32[6,32,128]{2,1,0:T(8,128)S(1)}, u32[]{:S(2)}, u32[]{:S(2)}) collective-permute-start(f32[6,32,128]{2,1,0:T(8,128)S(1)} %get-tuple-element.11), channel_id=1, source_target_pairs={{0,4},{4,8},{8,12},{12,16},{16,20},{20,24},{24,28},{28,32},{32,36}... | collective-permute-start | bytes 294920 | tf_op jit(solution)/shard_map/ppermute | solution.py:370
  8.7 12.9 %collective-permute-start.1 = (f32[6,32,128]{2,1,0:T(8,128)S(1)}, f32[6,32,128]{2,1,0:T(8,128)S(1)}, u32[]{:S(2)}, u32[]{:S(2)}) collective-permute-start(f32[6,32,128]{2,1,0:T(8,128)S(1)} %get-tuple-element.12), channel_id=1, source_target_pairs={{4,0},{8,4},{12,8},{16,12},{20,16},{24,20},{28,24},{32,28},{36,32}... | collective-permute-start | bytes 294920 | tf_op jit(solution)/shard_map/ppermute | solution.py:370
  10.6 11.0 %collective-permute-start.2 = (f32[6,32,128]{2,1,0:T(8,128)S(1)}, f32[6,32,128]{2,1,0:T(8,128)S(1)}, u32[]{:S(2)}, u32[]{:S(2)}) collective-permute-start(f32[6,32,128]{2,1,0:T(8,128)S(1)} %get-tuple-element.13), channel_id=1, source_target_pairs={{0,1},{1,2},{2,3},{4,5},{5,6},{6,7},{8,9},{9,10},{10,11},{12,13},{... | collective-permute-start | bytes 294920 | tf_op jit(solution)/shard_map/ppermute | solution.py:370
  13.8 7.8 %collective-permute-start.3 = (f32[6,32,128]{2,1,0:T(8,128)S(1)}, f32[6,32,128]{2,1,0:T(8,128)S(1)}, u32[]{:S(2)}, u32[]{:S(2)}) collective-permute-start(f32[6,32,128]{2,1,0:T(8,128)S(1)} %get-tuple-element.14), channel_id=1, source_target_pairs={{1,0},{2,1},{3,2},{5,4},{6,5},{7,6},{9,8},{10,9},{11,10},{13,12},{... | collective-permute-start | bytes 294920 | tf_op jit(solution)/shard_map/ppermute | solution.py:370
  15.1 0.9 copy-start.4
  16.0 0.9 copy-start.6
  17.0 0.7 copy-start.11
  17.6 0.7 copy-start.12
  18.3 0.7 copy-start.13
  24.8 11.6 %copy-start.2 = (f32[4,16,16,3,128]{4,2,3,1,0:T(8,128)S(1)}, f32[4,16,16,3,128]{4,2,3,1,0:T(8,128)}, u32[]{:S(2)}) copy-start(f32[4,16,16,3,128]{4,2,3,1,0:T(8,128)} %param.14) | copy-start | bytes 4718596
  24.9 45.8 %all-to-all-start = ((f32[128,7,4,128]{3,2,1,0:T(4,128)}), f32[128,7,4,128]{3,2,1,0:T(4,128)S(1)}, u32[]{:S(2)}, u32[]{:S(2)}) async-start(f32[128,7,4,128]{3,2,1,0:T(4,128)} %bitcast.2), calls=%async_computation | async-start | bytes 3670016 | tf_op jit(solution)/shard_map/all_to_all | solution.py:374
  36.4 27.3 %copy-start.7 = (bf16[768,128]{1,0:T(8,128)(2,1)S(1)}, bf16[768,128]{1,0:T(8,128)(2,1)}, u32[]{:S(2)}) copy-start(bf16[768,128]{1,0:T(8,128)(2,1)} %constant.7.clone.my) | copy-start | bytes 589828
  36.4 27.3 %copy-start.8 = (bf16[768,128]{1,0:T(8,128)(2,1)S(1)}, bf16[768,128]{1,0:T(8,128)(2,1)}, u32[]{:S(2)}) copy-start(bf16[768,128]{1,0:T(8,128)(2,1)} %constant.6.clone.mx) | copy-start | bytes 589828
  36.4 27.3 %copy-start.9 = (bf16[512,128]{1,0:T(8,128)(2,1)S(1)}, bf16[512,128]{1,0:T(8,128)(2,1)}, u32[]{:S(2)}) copy-start(bf16[512,128]{1,0:T(8,128)(2,1)} %constant.8.clone.mz) | copy-start | bytes 393220
  36.5 25.2 %collective-permute-start.4 = (f32[768,128]{1,0:T(8,128)S(1)}, f32[768,128]{1,0:T(8,128)S(1)}, u32[]{:S(2)}, u32[]{:S(2)}) collective-permute-start(f32[768,128]{1,0:T(8,128)S(1)} %bitcast.26), channel_id=1, source_target_pairs={{0,4},{4,8},{8,12},{12,16},{16,20},{20,24},{24,28},{28,32},{32,36}... | collective-permute-start | bytes 1179656 | tf_op jit(solution)/shard_map/ppermute | solution.py:370
  40.3 23.4 %collective-permute-start.5 = (f32[768,128]{1,0:T(8,128)S(1)}, f32[768,128]{1,0:T(8,128)S(1)}, u32[]{:S(2)}, u32[]{:S(2)}) collective-permute-start(f32[768,128]{1,0:T(8,128)S(1)} %bitcast.25), channel_id=1, source_target_pairs={{4,0},{8,4},{12,8},{16,12},{20,16},{24,20},{28,24},{32,28},{36,32}... | collective-permute-start | bytes 1179656 | tf_op jit(solution)/shard_map/ppermute | solution.py:370
  42.4 10.3 %collective-permute-start.6 = (f32[192,128]{1,0:T(8,128)S(1)}, f32[192,128]{1,0:T(8,128)S(1)}, u32[]{:S(2)}, u32[]{:S(2)}) collective-permute-start(f32[192,128]{1,0:T(8,128)S(1)} %bitcast.28), channel_id=1, source_target_pairs={{0,1},{1,2},{2,3},{4,5},{5,6},{6,7},{8,9},{9,10},{10,11},{12,13},{... | collective-permute-start | bytes 294920 | tf_op jit(solution)/shard_map/ppermute | solution.py:370
  45.6 13.7 %collective-permute-start.7 = (f32[192,128]{1,0:T(8,128)S(1)}, f32[192,128]{1,0:T(8,128)S(1)}, u32[]{:S(2)}, u32[]{:S(2)}) collective-permute-start(f32[192,128]{1,0:T(8,128)S(1)} %bitcast.27), channel_id=1, source_target_pairs={{1,0},{2,1},{3,2},{5,4},{6,5},{7,6},{9,8},{10,9},{11,10},{13,12},{... | collective-permute-start | bytes 294920 | tf_op jit(solution)/shard_map/ppermute | solution.py:370
  68.5 2.2 %copy-start = (f32[9344,128]{1,0:T(8,128)}, f32[9344,128]{1,0:T(8,128)S(1)}, u32[]{:S(2)}) copy-start(f32[9344,128]{1,0:T(8,128)S(1)} %gradient.1.grads) | copy-start | bytes 14352388
  70.7 2.4 %copy-start.1 = (f32[9344,128]{1,0:T(8,128)S(1)}, f32[9344,128]{1,0:T(8,128)}, u32[]{:S(2)}) copy-start(f32[9344,128]{1,0:T(8,128)} %copy-done) | copy-start | bytes 14352388

commit v3 on v2

--- a/solution.py
+++ b/solution.py
@@ -13,6 +13,7 @@
 SMEM = pl.BlockSpec(memory_space=pltpu.SMEM)
 ANY = pl.BlockSpec(memory_space=pl.ANY)
 PARAMS = pltpu.CompilerParams(vmem_limit_bytes=16 * 1024 * 1024)
+LARGE = pltpu.CompilerParams(vmem_limit_bytes=60 * 1024 * 1024)
 GRAD_ROWS = 64 * 9 * 16
 GRAD_PAD = 128
 GROUP = 8
@@ -26,40 +27,68 @@
     return pl.CostEstimate(flops=flops, bytes_accessed=read, transcendentals=0)
 
 
-def depart_kernel(vort, pos, counts, d0, d1, d2, d3, v_here, p_here, c_here, sems):
-    copies = [
+def depart_kernel(vort, pos, counts, vel, d0, d1, d2, d3, v_here, p_here, c_here, u_here, out, sems):
+    layer = pl.ds(192, 768)
+    fetches = [
         pltpu.make_async_copy(source, target, sems.at[n])
-        for n, (source, target) in enumerate(((counts, c_here), (vort, v_here), (pos, p_here)))
+        for n, (source, target) in enumerate(
+            ((counts, c_here), (vort, v_here), (pos, p_here), (vel, u_here))
+        )
     ]
-    for copy in copies:
+    sides = [
+        pltpu.make_async_copy(u_here.at[pl.ds(3 * 768, 768), :], d0.at[layer, :], sems.at[4]),
+        pltpu.make_async_copy(u_here.at[pl.ds(0, 768), :], d1.at[layer, :], sems.at[5]),
+    ]
+    for copy in fetches:
         copy.start()
-    for copy in copies:
+    for copy in fetches[:3]:
         copy.wait()
     place = lax.broadcasted_iota(jnp.int32, (32, 128), 0)
-    for heading, out in enumerate((d0, d1, d2, d3)):
+    sends = []
+    for heading in range(4):
         leaves = place < c_here[heading : heading + 1, :]
         rows = slice(heading * 32, heading * 32 + 32)
         for i in range(3):
-            out[i] = jnp.where(leaves, v_here[i, rows, :], 0.0)
-            out[3 + i] = jnp.where(leaves, p_here[i, rows, :], 0.0)
-
-
-def depart(vort, pos, counts):
+            out[heading, 32 * i : 32 * i + 32, :] = jnp.where(leaves, v_here[i, rows, :], 0.0)
+            out[heading, 96 + 32 * i : 128 + 32 * i, :] = jnp.where(leaves, p_here[i, rows, :], 0.0)
+        if heading < 2:
+            target = (d0, d1)[heading].at[pl.ds(0, 192), :]
+            sends.append(
+                pltpu.make_async_copy(
+                    out.at[heading, pl.ds(0, 192), :], target, sems.at[6 + heading]
+                )
+            )
+            sends[-1].start()
+    fetches[3].wait()
+    for copy in sides:
+        copy.start()
+    for heading, level in ((2, 15), (3, 0)):
+        out[heading, 192:384, :] = u_here[pl.ds(level, 192, stride=16), :]
+        target = (d2, d3)[heading - 2]
+        sends.append(pltpu.make_async_copy(out.at[heading], target, sems.at[6 + heading]))
+        sends[-1].start()
+    for copy in sides + sends:
+        copy.wait()
+
+
+def depart(vort, pos, counts, vel):
     return pl.pallas_call(
         depart_kernel,
-        out_shape=[sds((6, 32, 128))] * 4,
-        in_specs=[ANY] * 3,
-        out_specs=[VMEM] * 4,
+        out_shape=[sds((960, 128))] * 2 + [sds((384, 128))] * 2,
+        in_specs=[ANY] * 4,
+        out_specs=[ANY] * 4,
         scratch_shapes=[
             pltpu.VMEM((3, 128, 128), F32),
             pltpu.VMEM((3, 128, 128), F32),
             pltpu.VMEM((4, 128), jnp.int32),
-            pltpu.SemaphoreType.DMA((3,)),
+            pltpu.VMEM((3072, 128), F32),
+            pltpu.VMEM((4, 384, 128), F32),
+            pltpu.SemaphoreType.DMA((10,)),
         ],
-        compiler_params=PARAMS,
-        cost_estimate=cost(400_000, 1_600_000),
+        compiler_params=LARGE,
+        cost_estimate=cost(400_000, 3_000_000),
         name="depart",
-    )(vort, pos, counts)
+    )(vort, pos, counts, vel)
 
 
 ORDER = (3, 4, 0, 1, 2, 5)
@@ -80,7 +109,17 @@
     turned[768:896, :] = jnp.broadcast_to(row, (128, 128)).T
 
 
-def keep_kernel(owners, vort, pos, counts, slots, places, turned, tally):
+def keep_kernel(
+    owners, vort, pos, counts, slots, places, turned, tally, v_here, p_here, c_here, s_here, sems
+):
+    fetches = [
+        pltpu.make_async_copy(source, target, sems.at[n])
+        for n, (source, target) in enumerate(
+            ((counts, c_here), (vort, v_here), (pos, p_here), (slots, s_here))
+        )
+    ]
+    for copy in fetches:
+        copy.start()
     for i in range(128):
         tally[i] = 0
 
@@ -92,31 +131,40 @@
         return carry
 
     lax.fori_loop(0, 256, rank_of, 0, unroll=8)
+    for copy in fetches:
+        copy.wait()
     place = lax.broadcasted_iota(jnp.int32, (32, 128), 0)
-    leaves = [place < counts[heading : heading + 1, :] for heading in range(4)]
+    leaves = [place < c_here[heading : heading + 1, :] for heading in range(4)]
     for at, comp in enumerate(ORDER):
         if comp < 3:
             kept = jnp.concatenate(
                 [
-                    jnp.where(leaves[h], 0.0, vort[comp, 32 * h : 32 * h + 32, :])
+                    jnp.where(leaves[h], 0.0, v_here[comp, 32 * h : 32 * h + 32, :])
                     for h in range(4)
                 ],
                 axis=0,
             )
         else:
-            kept = pos[comp - 3]
+            kept = p_here[comp - 3]
         turned[at * 128 : at * 128 + 128, :] = kept.T
-    slot_rows(slots, 0, turned)
+    slot_rows(s_here, 0, turned)
 
 
 def keep(owners, vort, pos, counts, slots):
     return pl.pallas_call(
         keep_kernel,
         out_shape=[sds((256,), jnp.int32), sds((896, 128))],
-        in_specs=[SMEM] + [VMEM] * 4,
+        in_specs=[SMEM] + [ANY] * 4,
         out_specs=[SMEM, VMEM],
-        scratch_shapes=[pltpu.SMEM((128,), jnp.int32)],
-        compiler_params=PARAMS,
+        scratch_shapes=[
+            pltpu.SMEM((128,), jnp.int32),
+            pltpu.VMEM((3, 128, 128), F32),
+            pltpu.VMEM((3, 128, 128), F32),
+            pltpu.VMEM((4, 128), jnp.int32),
+            pltpu.VMEM((2, 128), jnp.int32),
+            pltpu.SemaphoreType.DMA((4,)),
+        ],
+        compiler_params=LARGE,
         cost_estimate=cost(1_000_000, 4_000_000),
         name="keep",
     )(owners, vort, pos, counts, slots)
@@ -130,7 +178,9 @@
     lax.fori_loop(0, 56, clear, 0)
     send_rows(places, kept, ship, 0)
     for at, comp in enumerate(ORDER):
-        came = jnp.concatenate([a[comp] for a in (a0, a1, a2, a3)], axis=0)
+        came = jnp.concatenate(
+            [a[32 * comp : 32 * comp + 32, :] for a in (a0, a1, a2, a3)], axis=0
+        )
         turned[at * 128 : at * 128 + 128, :] = came.T
     slot_rows(slots, 1, turned)
     send_rows(places, turned, ship, 128)
@@ -186,7 +236,7 @@
         high[at, :], low[at, :] = split(value)
 
     def fill(sy, carry):
-        rows = pl.ds(pl.multiple_of(sy * 48, 16), 48)
+        rows = pl.ds(pl.multiple_of(192 + sy * 48, 16), 48)
         put(0, sy + 1, xb[rows, :])
         put(5, sy + 1, xa[rows, :])
         for sx in range(4):
@@ -195,7 +245,7 @@
             put(sx + 1, sy + 1, value)
             for i in range(3):
                 c = value[16 * i : 16 * i + 16]
-                edge = pl.ds((sx * 16 + sy) * 3 + i, 1)
+                edge = pl.ds(192 + (sx * 16 + sy) * 3 + i, 1)
                 before = jnp.concatenate([zb[edge, :], c[:15]], axis=0)
                 after = jnp.concatenate([c[1:], za[edge, :]], axis=0)
                 at = pl.ds(pl.multiple_of(row + 16 * i, 16), 16)
@@ -376,7 +426,8 @@
 
 def on_device(vorticity, position, counts, owner_ids, slot_ids, velocity):
     slots = slot_ids.reshape(2, 128)
-    leaving = depart(vorticity, position, counts)
+    vel = jnp.transpose(velocity, (0, 1, 3, 2, 4)).reshape(3072, 128)
+    leaving = depart(vorticity, position, counts, vel)
     arrivals = [
         stepped(leaving[0], "gx", 1),
         stepped(leaving[1], "gx", -1),
@@ -387,12 +438,7 @@
     ship = route(places, slots, arrivals, kept)
     rows = exchange(ship.reshape(128, 7, 4, 128)).reshape(3584, 128)
 
-    vel = jnp.transpose(velocity, (0, 1, 3, 2, 4))
-    xb = stepped(vel[3].reshape(768, 128), "gx", 1)
-    xa = stepped(vel[0].reshape(768, 128), "gx", -1)
-    zb = stepped(vel[:, :, :, 15].reshape(192, 128), "gz", 1)
-    za = stepped(vel[:, :, :, 0].reshape(192, 128), "gz", -1)
-    grads = gradient(vel.reshape(3072, 128), xb, xa, zb, za)
+    grads = gradient(vel, *arrivals)
 
     mesh, back = owner_work(rows, grads)
     back = exchange(back.reshape(128, 3, 4, 128)).reshape(1536, 128)

time: 120 us -> 110 us (0.917)
  starting transfers between devices: 33.1 us -> 22.8 us
  blocking collectives: 25 us -> 20.1 us
  Pallas kernels: 32.7 us -> 35.6 us
  waiting for transfers between devices: 16.8 us -> 18.2 us
  local copies, waits for them, and re-layouts: 11.2 us -> 12.4 us
    all_to_all x1, waiting for transfers between devices: 0.01 us -> 15.4 us  [exchange(): return lax.all_to_all(value, AXES, split_axis=0, concat_axis=0, tiled=True)]
    ppermute x8 -> x4, waiting for transfers between devices: 16.8 us -> 2.76 us  [stepped(): lax.ppermute(value, axis, [(source, source + step) for source in range(fi...]
    ppermute x8 -> x4, starting transfers between devices: 21.5 us -> 11.4 us  [stepped(): lax.ppermute(value, axis, [(source, source + step) for source in range(fi...]
    all_to_all x1, blocking collectives: 25 us -> 20.1 us  [exchange(): return lax.all_to_all(value, AXES, split_axis=0, concat_axis=0, tiled=True)]
    pallas_call x1, Pallas kernels: 0.54 us -> 2.75 us  [depart(): pl.pallas_call(depart_kernel, out_shape=[sds((960, 128))] * 2 + [sds((384...]
    unnamed x28 -> x36, local copies, waits for them, and re-layouts: 11 us -> 12.4 us
  transfers between devices with their start and end apart: 9 -> 5, of which waited for: 4 -> 2; matrix products, arithmetic and copies ran while one was open for 0% -> 0% of each run, Pallas kernels for 6% -> 7%
where the time goes in v3:
time: 110 us
  Pallas kernels  35.6 us (32%)
  starting transfers between devices  22.8 us (21%)
  blocking collectives  20.1 us (18%)
  waiting for transfers between devices  18.2 us (17%)
  local copies, waits for them, and re-layouts  12.4 us (11%)
    all_to_all x1, blocking collectives, exchange(): return lax.all_to_all(value, AXES, split_axis=0, concat_axis=0, tiled=True)  20.1 us
    pallas_call x1, Pallas kernels, owner_work(): pl.pallas_call(owner_kernel, out_shape=[sds((3072, 128)), sds((1536, 128)...  19.5 us
    all_to_all x1, waiting for transfers between devices, exchange(): return lax.all_to_all(value, AXES, split_axis=0, concat_axis=0, tiled=True)  15.4 us
    unnamed x36, local copies, waits for them, and re-layouts  12.4 us
    all_to_all x1, starting transfers between devices, exchange(): return lax.all_to_all(value, AXES, split_axis=0, concat_axis=0, tiled=True)  11.5 us
    ppermute x4, starting transfers between devices, stepped(): lax.ppermute(value, axis, [(source, source + step) for source in range(fi...  11.4 us
    pallas_call x1, Pallas kernels, gradient(): pl.pallas_call(gradient_kernel, out_shape=sds((GRAD_ROWS + GRAD_PAD, 128)...  4.79 us
    pallas_call x1, Pallas kernels, route(): pl.pallas_call(route_kernel, out_shape=sds((3584, 128)), in_specs=[SMEM]...  3.28 us
  transfers between devices with their start and end apart: 5, of which 2 were waited for; matrix products, arithmetic and copies ran while one was open for 0% of the time, Pallas kernels for 7%

profile of v3, /device:TPU:1, one launch (start us, length us, event | category | flops | bytes accessed | tf_op | source)
XLA Modules:
  0.0 109.8 jit_solution(10181390777634296179)
XLA Ops:
  0.6 2.8 %depart.1 = (f32[960,128]{1,0:T(8,128)}, f32[960,128]{1,0:T(8,128)}, f32[384,128]{1,0:T(8,128)}, f32[384,128]{1,0:T(8,128)}) custom-call(f32[3,128,128]{2,1,0:T(8,128)} %vort.3, f32[3,128,128]{2,1,0:T(8,128)} %pos.3, s32[4,128]{1,0:T(4,128)} %counts.3, f32[3072,128]{1,0:T(8,128)} %bitcast.13), custom_call_target="tpu_custom_call" | custom-call | flops 400000 | bytes 3000000 | tf_op jit(solution)/shard_map/depart/pallas_call | solution.py:75
  3.4 4.9 %collective-permute-start = (f32[960,128]{1,0:T(8,128)}, f32[960,128]{1,0:T(8,128)S(1)}, u32[]{:S(2)}, u32[]{:S(2)}) collective-permute-start(f32[960,128]{1,0:T(8,128)} %get-tuple-element.11), channel_id=1, source_target_pairs={{0,4},{4,8},{8,12},{12,16},{16,20},{20,24},{24,28},{28,32},{32,36}... | collective-permute-start | bytes 1474568 | tf_op jit(solution)/shard_map/ppermute | solution.py:420
  8.3 1.9 %collective-permute-start.1 = (f32[960,128]{1,0:T(8,128)}, f32[960,128]{1,0:T(8,128)S(1)}, u32[]{:S(2)}, u32[]{:S(2)}) collective-permute-start(f32[960,128]{1,0:T(8,128)} %get-tuple-element.12), channel_id=1, source_target_pairs={{4,0},{8,4},{12,8},{16,12},{20,16},{24,20},{28,24},{32,28},{36,32}... | collective-permute-start | bytes 1474568 | tf_op jit(solution)/shard_map/ppermute | solution.py:420
  10.3 3.2 %collective-permute-start.2 = (f32[384,128]{1,0:T(8,128)}, f32[384,128]{1,0:T(8,128)S(1)}, u32[]{:S(2)}, u32[]{:S(2)}) collective-permute-start(f32[384,128]{1,0:T(8,128)} %get-tuple-element.13), channel_id=1, source_target_pairs={{0,1},{1,2},{2,3},{4,5},{5,6},{6,7},{8,9},{9,10},{10,11},{12,13},{... | collective-permute-start | bytes 589832 | tf_op jit(solution)/shard_map/ppermute | solution.py:420
  13.5 1.3 %collective-permute-start.3 = (f32[384,128]{1,0:T(8,128)}, f32[384,128]{1,0:T(8,128)S(1)}, u32[]{:S(2)}, u32[]{:S(2)}) collective-permute-start(f32[384,128]{1,0:T(8,128)} %get-tuple-element.14), channel_id=1, source_target_pairs={{1,0},{2,1},{3,2},{5,4},{6,5},{7,6},{9,8},{10,9},{11,10},{13,12},{... | collective-permute-start | bytes 589832 | tf_op jit(solution)/shard_map/ppermute | solution.py:420
  14.8 3.1 %keep.1 = (s32[256]{0:T(256)}, f32[896,128]{1,0:T(8,128)}) custom-call(s32[256]{0:T(256)} %bitcast.19, f32[3,128,128]{2,1,0:T(8,128)} %vort.3, f32[3,128,128]{2,1,0:T(8,128)} %pos.3, s32[4,128]{1,0:T(4,128)} %counts.3, s32[2,128]{1,0:T(2,128)} %bitcast.17), custom_call_target="tpu_custom_call" | custom-call | flops 1000000 | bytes 4000000 | tf_op jit(solution)/shard_map/keep/pallas_call | solution.py:154
  17.9 2.8 %collective-permute-done.3.a3.za = f32[384,128]{1,0:T(8,128)S(1)} collective-permute-done((f32[384,128]{1,0:T(8,128)}, f32[384,128]{1,0:T(8,128)S(1)}, u32[]{:S(2)}, u32[]{:S(2)}) %collective-permute-start.3) | collective-permute-done | bytes 196640 | tf_op jit(solution)/shard_map/ppermute | solution.py:420
  20.7 1.4 %copy-done.11 = f32[896,128]{1,0:T(8,128)S(1)} copy-done((f32[896,128]{1,0:T(8,128)S(1)}, f32[896,128]{1,0:T(8,128)}, u32[]{:S(2)}) %copy-start.11) | copy-done | bytes 458776
  22.1 0.7 copy-done.16
  22.7 3.3 %route.1 = f32[3584,128]{1,0:T(8,128)} custom-call(s32[256]{0:T(256)S(1)} %copy-done.16, s32[2,128]{1,0:T(2,128)S(1)} %bitcast.18, f32[960,128]{1,0:T(8,128)S(1)} %collective-permute-done.a0.xb, f32[960,128]{1,0:T(8,128)S(1)} %collective-permute-done.1.a1.xa, f32[384,128]{1,0:T(8,128)S(1)} %collective-permute-done.2.a2.zb, ...), custom_call_target="tpu_custom_call" | custom-call | flops 1000000 | bytes 4000000 | tf_op jit(solution)/shard_map/route/pallas_call | solution.py:190
  26.1 11.5 %all-to-all-start = ((f32[128,7,4,128]{3,2,1,0:T(4,128)}), f32[128,7,4,128]{3,2,1,0:T(4,128)S(1)}, u32[]{:S(2)}, u32[]{:S(2)}) async-start(f32[128,7,4,128]{3,2,1,0:T(4,128)} %bitcast.4), calls=%async_computation | async-start | bytes 3670016 | tf_op jit(solution)/shard_map/all_to_all | solution.py:424
  37.6 1.0 copy-done.4
  38.6 1.0 copy-done.6
  39.6 0.9 copy-done.8
  40.6 0.9 copy-done.10
  41.5 0.9 copy-done.12
  42.4 0.9 copy-done.13
  43.4 4.8 %gradient.1.grads = f32[9344,128]{1,0:T(8,128)S(1)} custom-call(f32[3072,128]{1,0:T(8,128)S(1)} %bitcast.14, f32[960,128]{1,0:T(8,128)S(1)} %copy-done.4, f32[960,128]{1,0:T(8,128)S(1)} %copy-done.6, f32[384,128]{1,0:T(8,128)S(1)} %copy-done.8, f32[384,128]{1,0:T(8,128)S(1)} %copy-done.10, bf16[768,128]{1,0:T(8,128)(2,1)S(1)} %copy-done.13, ...), custom_call_target="tpu_custom_call" | custom-call | flops 20000000 | bytes 8000000 | tf_op jit(solution)/shard_map/gradient/pallas_call | solution.py:284
  48.2 2.2 %copy-done = f32[9344,128]{1,0:T(8,128)} copy-done((f32[9344,128]{1,0:T(8,128)}, f32[9344,128]{1,0:T(8,128)S(1)}, u32[]{:S(2)}) %copy-start) | copy-done | bytes 4784152
  50.3 15.4 %all-to-all-done = f32[128,7,4,128]{3,2,1,0:T(4,128)S(1)} async-done(((f32[128,7,4,128]{3,2,1,0:T(4,128)}), f32[128,7,4,128]{3,2,1,0:T(4,128)S(1)}, u32[]{:S(2)}, u32[]{:S(2)}) %all-to-all-start) | async-done | bytes 1835040 | tf_op jit(solution)/shard_map/all_to_all | solution.py:424
  65.7 2.4 %copy-done.1 = f32[9344,128]{1,0:T(8,128)S(1)} copy-done((f32[9344,128]{1,0:T(8,128)S(1)}, f32[9344,128]{1,0:T(8,128)}, u32[]{:S(2)}) %copy-start.1) | copy-done | bytes 4784152
  68.1 19.5 %owner.1 = (f32[3072,128]{1,0:T(8,128)}, f32[1536,128]{1,0:T(8,128)S(1)}) custom-call(f32[3584,128]{1,0:T(8,128)S(1)} %bitcast.12, f32[9344,128]{1,0:T(8,128)S(1)} %copy-done.1), custom_call_target="tpu_custom_call" | custom-call | flops 300000000 | bytes 9000000 | tf_op jit(solution)/shard_map/owner/pallas_call | solution.py:379
  87.6 20.1 %all_to_all.10 = f32[128,3,4,128]{3,2,1,0:T(4,128)S(1)} all-to-all(f32[128,3,4,128]{3,2,1,0:T(4,128)S(1)} %bitcast.16), channel_id=1, replica_groups=mesh['gx'=32,'gz'=4] {'gx','gz'}, dimensions={0} | all-to-all | bytes 1572864 | tf_op jit(solution)/shard_map/all_to_all | solution.py:424
  107.7 2.1 %unpack.1 = f32[2,3,128,128]{3,2,1,0:T(8,128)} custom-call(s32[256]{0:T(256)S(1)} %copy-done.17, f32[1536,128]{1,0:T(8,128)S(1)} %bitcast.15), custom_call_target="tpu_custom_call" | custom-call | flops 1000000 | bytes 2000000 | tf_op jit(solution)/shard_map/unpack/pallas_call | solution.py:405
  (29 shorter events, 0.1 us)
Async XLA Ops:
  0.6 20.1 %copy-start.15 = (s32[256]{0:T(256)S(1)}, s32[256]{0:T(256)}, u32[]{:S(2)}) copy-start(s32[256]{0:T(256)} %param.13) | copy-start | bytes 3076
  3.4 17.3 %collective-permute-start = (f32[960,128]{1,0:T(8,128)}, f32[960,128]{1,0:T(8,128)S(1)}, u32[]{:S(2)}, u32[]{:S(2)}) collective-permute-start(f32[960,128]{1,0:T(8,128)} %get-tuple-element.11), channel_id=1, source_target_pairs={{0,4},{4,8},{8,12},{12,16},{16,20},{20,24},{24,28},{28,32},{32,36}... | collective-permute-start | bytes 1474568 | tf_op jit(solution)/shard_map/ppermute | solution.py:420
  8.3 12.3 %collective-permute-start.1 = (f32[960,128]{1,0:T(8,128)}, f32[960,128]{1,0:T(8,128)S(1)}, u32[]{:S(2)}, u32[]{:S(2)}) collective-permute-start(f32[960,128]{1,0:T(8,128)} %get-tuple-element.12), channel_id=1, source_target_pairs={{4,0},{8,4},{12,8},{16,12},{20,16},{24,20},{28,24},{32,28},{36,32}... | collective-permute-start | bytes 1474568 | tf_op jit(solution)/shard_map/ppermute | solution.py:420
  10.3 7.6 %collective-permute-start.2 = (f32[384,128]{1,0:T(8,128)}, f32[384,128]{1,0:T(8,128)S(1)}, u32[]{:S(2)}, u32[]{:S(2)}) collective-permute-start(f32[384,128]{1,0:T(8,128)} %get-tuple-element.13), channel_id=1, source_target_pairs={{0,1},{1,2},{2,3},{4,5},{5,6},{6,7},{8,9},{9,10},{10,11},{12,13},{... | collective-permute-start | bytes 589832 | tf_op jit(solution)/shard_map/ppermute | solution.py:420
  13.5 7.2 %collective-permute-start.3 = (f32[384,128]{1,0:T(8,128)}, f32[384,128]{1,0:T(8,128)S(1)}, u32[]{:S(2)}, u32[]{:S(2)}) collective-permute-start(f32[384,128]{1,0:T(8,128)} %get-tuple-element.14), channel_id=1, source_target_pairs={{1,0},{2,1},{3,2},{5,4},{6,5},{7,6},{9,8},{10,9},{11,10},{13,12},{... | collective-permute-start | bytes 589832 | tf_op jit(solution)/shard_map/ppermute | solution.py:420
  17.9 8.1 %copy-start.7 = (f32[384,128]{1,0:T(8,128)}, f32[384,128]{1,0:T(8,128)S(1)}, u32[]{:S(2)}) copy-start(f32[384,128]{1,0:T(8,128)S(1)} %collective-permute-done.2.a2.zb) | copy-start | bytes 589828
  20.7 5.4 %copy-start.9 = (f32[384,128]{1,0:T(8,128)}, f32[384,128]{1,0:T(8,128)S(1)}, u32[]{:S(2)}) copy-start(f32[384,128]{1,0:T(8,128)S(1)} %collective-permute-done.3.a3.za) | copy-start | bytes 589828
  20.7 5.4 %copy-start.3 = (f32[960,128]{1,0:T(8,128)}, f32[960,128]{1,0:T(8,128)S(1)}, u32[]{:S(2)}) copy-start(f32[960,128]{1,0:T(8,128)S(1)} %collective-permute-done.a0.xb) | copy-start | bytes 1474564
  20.7 5.4 %copy-start.5 = (f32[960,128]{1,0:T(8,128)}, f32[960,128]{1,0:T(8,128)S(1)}, u32[]{:S(2)}) copy-start(f32[960,128]{1,0:T(8,128)S(1)} %collective-permute-done.1.a1.xa) | copy-start | bytes 1474564
  20.7 1.4 %copy-start.11 = (f32[896,128]{1,0:T(8,128)S(1)}, f32[896,128]{1,0:T(8,128)}, u32[]{:S(2)}) copy-start(f32[896,128]{1,0:T(8,128)} %get-tuple-element.15.kept) | copy-start | bytes 1376260
  22.1 0.7 copy-start.16
  26.0 11.5 %copy-start.2 = (f32[4,16,16,3,128]{4,2,3,1,0:T(8,128)S(1)}, f32[4,16,16,3,128]{4,2,3,1,0:T(8,128)}, u32[]{:S(2)}) copy-start(f32[4,16,16,3,128]{4,2,3,1,0:T(8,128)} %param.14) | copy-start | bytes 4718596
  26.1 11.5 %copy-start.14 = (bf16[512,128]{1,0:T(8,128)(2,1)S(1)}, bf16[512,128]{1,0:T(8,128)(2,1)}, u32[]{:S(2)}) copy-start(bf16[512,128]{1,0:T(8,128)(2,1)} %constant.8.clone.mz) | copy-start | bytes 393220
  26.1 39.7 %all-to-all-start = ((f32[128,7,4,128]{3,2,1,0:T(4,128)}), f32[128,7,4,128]{3,2,1,0:T(4,128)S(1)}, u32[]{:S(2)}, u32[]{:S(2)}) async-start(f32[128,7,4,128]{3,2,1,0:T(4,128)} %bitcast.4), calls=%async_computation | async-start | bytes 3670016 | tf_op jit(solution)/shard_map/all_to_all | solution.py:424
  37.6 1.0 copy-start.4
  38.6 1.0 copy-start.6
  39.6 0.9 copy-start.8
  40.6 0.9 copy-start.10
  41.5 0.9 copy-start.12
  42.4 0.9 copy-start.13
  48.2 2.2 %copy-start = (f32[9344,128]{1,0:T(8,128)}, f32[9344,128]{1,0:T(8,128)S(1)}, u32[]{:S(2)}) copy-start(f32[9344,128]{1,0:T(8,128)S(1)} %gradient.1.grads) | copy-start | bytes 14352388
  65.7 2.4 %copy-start.1 = (f32[9344,128]{1,0:T(8,128)S(1)}, f32[9344,128]{1,0:T(8,128)}, u32[]{:S(2)}) copy-start(f32[9344,128]{1,0:T(8,128)} %copy-done) | copy-start | bytes 14352388
  68.1 39.6 %copy-start.17 = (s32[256]{0:T(256)S(1)}, s32[256]{0:T(256)}, u32[]{:S(2)}) copy-start(s32[256]{0:T(256)} %get-tuple-element.10.places) | copy-start | bytes 3076

commit v4 on v3

--- a/solution.py
+++ b/solution.py
@@ -17,6 +17,7 @@
 GRAD_ROWS = 64 * 9 * 16
 GRAD_PAD = 128
 GROUP = 8
+EARLY = 2
 
 
 def sds(shape, dtype=F32):
@@ -95,10 +96,16 @@
 
 
 def send_rows(places, turned, ship, first):
+    lane = lax.broadcasted_iota(jnp.int32, (1, 128), 1)
+
     def move(r, carry):
         place = places[first + r]
-        base = (place >> 2) * 28 + (place & 3)
-        ship[pl.ds(base, 7, stride=4), :] = turned[pl.ds(r, 7, stride=128), :]
+        base = (place >> 2) * 25
+        rank = place & 3
+        ship[pl.ds(base + rank, 6, stride=4), :] = turned[pl.ds(r, 6, stride=128), :]
+        marks = pl.ds(base + 24, 1)
+        slot = turned[pl.ds(768 + r, 1), :]
+        ship[marks, :] = jnp.where(lane == rank, slot, ship[marks, :])
         return carry
 
     lax.fori_loop(0, 128, move, 0, unroll=8)
@@ -170,30 +177,50 @@
     )(owners, vort, pos, counts, slots)
 
 
-def route_kernel(places, slots, a0, a1, a2, a3, kept, ship, turned):
+def route_kernel(
+    places, slots, a0, a1, a2, a3, kept, ship, turned, kept_here, came_here, s_here, sems
+):
+    fetches = [
+        pltpu.make_async_copy(source.at[pl.ds(0, 192), :], came_here.at[n], sems.at[n])
+        for n, source in enumerate((a0, a1, a2, a3))
+    ]
+    fetches.append(pltpu.make_async_copy(slots, s_here, sems.at[4]))
+    fetches.append(pltpu.make_async_copy(kept, kept_here, sems.at[5]))
+    for copy in fetches:
+        copy.start()
+
     def clear(i, carry):
         ship[pl.ds(pl.multiple_of(i * 64, 64), 64), :] = jnp.zeros((64, 128), F32)
         return carry
 
-    lax.fori_loop(0, 56, clear, 0)
-    send_rows(places, kept, ship, 0)
+    lax.fori_loop(0, 50, clear, 0)
+    fetches[5].wait()
+    send_rows(places, kept_here, ship, 0)
+    for copy in fetches[:5]:
+        copy.wait()
     for at, comp in enumerate(ORDER):
         came = jnp.concatenate(
-            [a[32 * comp : 32 * comp + 32, :] for a in (a0, a1, a2, a3)], axis=0
+            [came_here[n, 32 * comp : 32 * comp + 32, :] for n in range(4)], axis=0
         )
         turned[at * 128 : at * 128 + 128, :] = came.T
-    slot_rows(slots, 1, turned)
+    slot_rows(s_here, 1, turned)
     send_rows(places, turned, ship, 128)
 
 
 def route(places, slots, arrivals, kept):
     return pl.pallas_call(
         route_kernel,
-        out_shape=sds((3584, 128)),
-        in_specs=[SMEM] + [VMEM] * 6,
+        out_shape=sds((3200, 128)),
+        in_specs=[SMEM] + [ANY] * 6,
         out_specs=VMEM,
-        scratch_shapes=[pltpu.VMEM((896, 128), F32)],
-        compiler_params=PARAMS,
+        scratch_shapes=[
+            pltpu.VMEM((896, 128), F32),
+            pltpu.VMEM((896, 128), F32),
+            pltpu.VMEM((4, 192, 128), F32),
+            pltpu.VMEM((2, 128), jnp.int32),
+            pltpu.SemaphoreType.DMA((6,)),
+        ],
+        compiler_params=LARGE,
         cost_estimate=cost(1_000_000, 4_000_000),
         name="route",
     )(places, slots, *arrivals, kept)
@@ -294,16 +321,12 @@
     )(vel, xb, xa, zb, za, *matrices())
 
 
-def owner_kernel(rows, grads, mesh, back):
-    def clear(i, carry):
-        mesh[pl.ds(pl.multiple_of(i * 64, 64), 64), :] = jnp.zeros((64, 128), F32)
-        return carry
-
-    lax.fori_loop(0, 48, clear, 0)
+def wide(row):
+    return jnp.broadcast_to(row, (8, 128))
+
+
+def each_row(rows, work, first, last):
     cell_z = lax.broadcasted_iota(jnp.int32, (8, 128), 0).astype(F32)
-
-    def wide(row):
-        return jnp.broadcast_to(row, (8, 128))
 
     def per_source(s, base):
         f = rows[pl.ds(base, 8), :] - 1.0
@@ -314,11 +337,8 @@
             1.0 + g * g * (1.5 * g - 2.5),
             -0.5 * g * f * f,
         )
-        slots = rows[pl.ds(base + 24, 4), :].astype(jnp.int32)
+        slots = rows[pl.ds(base + 24, 1), :].astype(jnp.int32)
         for k in range(4):
-            slot = slots[k, 0]
-            column = slot >> 4
-            level = slot & 15
             z = wide(rows[pl.ds(base + 20 + k, 1), :])
             radius = jnp.abs(cell_z - z)
             rest = jnp.maximum(2.0 - radius, 0.0)
@@ -330,61 +350,130 @@
             yz = [wide(weights[b][4 + k : 5 + k]) * along_z for b in range(4)]
             xs = [wide(weights[a][k : k + 1]) for a in range(4)]
             table = jnp.concatenate([xs[a] * yz[b] for a in range(4) for b in range(4)], axis=0)
-            high, low = split(table)
-
             vortex = [rows[pl.ds(base + 8 + 4 * j + k, 1), :] for j in range(3)]
-            grad = jnp.concatenate(
-                [
-                    grads[pl.ds(column * 144 + j * 48 + level, 8, stride=16), :]
-                    for j in range(3)
-                ],
-                axis=0,
-            )
-            left = jnp.concatenate(split(grad), axis=0)
-            left = jnp.concatenate([left, left], axis=1)
-            sampled = jnp.dot(
-                left, jnp.concatenate([high, low], axis=0), preferred_element_type=F32
-            )
-            sampled = sampled[:24] + sampled[24:]
-            stretch = (
-                sampled[0:8] * wide(vortex[0])
-                + sampled[8:16] * wide(vortex[1])
-                + sampled[16:24] * wide(vortex[2])
-            )
-            back[pl.ds(s * 12 + k, 3, stride=4), :] = stretch[:3]
-
-            v = jnp.concatenate(vortex + [jnp.zeros((5, 128), F32)], axis=0)
-            left = jnp.concatenate(split(v), axis=0)
-            left = jnp.concatenate([left, left], axis=1)
-            patch = lax.dot_general(
-                left,
-                jnp.concatenate([high, low], axis=1),
-                (((1,), (1,)), ((), ())),
-                preferred_element_type=F32,
-            )
-            patch = patch[:3] + patch[8:11]
-            at = pl.ds(column * 48 + level, 3, stride=16)
-            mesh[at, :] = mesh[at, :] + patch
+            slot = slots[0, k]
+            work(s, k, slot >> 4, slot & 15, vortex, *split(table))
 
     def per_group(q, carry):
-        base = pl.multiple_of(q * (28 * GROUP), 8)
+        base = pl.multiple_of(q * (25 * GROUP), 8)
         for u in range(GROUP):
-            per_source(q * GROUP + u, base + 28 * u)
-        return carry
-
-    lax.fori_loop(0, 128 // GROUP, per_group, 0)
-
-
-def owner_work(rows, grads):
-    return pl.pallas_call(
-        owner_kernel,
-        out_shape=[sds((3072, 128)), sds((1536, 128))],
-        in_specs=[VMEM, VMEM],
-        out_specs=[VMEM] * 2,
-        compiler_params=PARAMS,
+            per_source(q * GROUP + u, base + 25 * u)
+        return carry
+
+    lax.fori_loop(first, last, per_group, 0)
+
+
+def sampled_row(grads, column, level, vortex, high, low):
+    grad = jnp.concatenate(
+        [grads[pl.ds(column * 144 + j * 48 + level, 8, stride=16), :] for j in range(3)],
+        axis=0,
+    )
+    left = jnp.concatenate(split(grad), axis=0)
+    left = jnp.concatenate([left, left], axis=1)
+    value = jnp.dot(left, jnp.concatenate([high, low], axis=0), preferred_element_type=F32)
+    value = value[:24] + value[24:]
+    stretch = (
+        value[0:8] * wide(vortex[0])
+        + value[8:16] * wide(vortex[1])
+        + value[16:24] * wide(vortex[2])
+    )
+    return stretch[:3]
+
+
+def add_patch(mesh, column, level, vortex, high, low):
+    v = jnp.concatenate(vortex + [jnp.zeros((5, 128), F32)], axis=0)
+    left = jnp.concatenate(split(v), axis=0)
+    left = jnp.concatenate([left, left], axis=1)
+    patch = lax.dot_general(
+        left,
+        jnp.concatenate([high, low], axis=1),
+        (((1,), (1,)), ((), ())),
+        preferred_element_type=F32,
+    )
+    patch = patch[:3] + patch[8:11]
+    at = pl.ds(column * 48 + level, 3, stride=16)
+    mesh[at, :] = mesh[at, :] + patch
+
+
+def sample_kernel(rows, grads, back, mesh, rows_here, grads_here, back_here, mesh_here, sems):
+    ahead = EARLY * GROUP * 25
+    parts = (pl.ds(0, ahead), pl.ds(ahead, 3200 - ahead))
+    fetches = [
+        pltpu.make_async_copy(rows.at[part, :], rows_here.at[part, :], sems.at[n])
+        for n, part in enumerate(parts)
+    ]
+    fetches.append(pltpu.make_async_copy(grads, grads_here, sems.at[2]))
+    for copy in fetches:
+        copy.start()
+
+    def clear(i, carry):
+        mesh_here[pl.ds(pl.multiple_of(i * 64, 64), 64), :] = jnp.zeros((64, 128), F32)
+        return carry
+
+    lax.fori_loop(0, 48, clear, 0)
+    fetches[0].wait()
+    each_row(rows_here, lambda s, k, *row: add_patch(mesh_here, *row), 0, EARLY)
+    stores = [pltpu.make_async_copy(mesh_here, mesh, sems.at[3])]
+    stores[0].start()
+    for copy in fetches[1:]:
+        copy.wait()
+
+    def work(s, k, *row):
+        back_here[pl.ds(s * 12 + k, 3, stride=4), :] = sampled_row(grads_here, *row)
+
+    for n in range(2):
+        each_row(rows_here, work, n * 64 // GROUP, (n + 1) * 64 // GROUP)
+        half = pl.ds(768 * n, 768)
+        stores.append(pltpu.make_async_copy(back_here.at[half, :], back.at[half, :], sems.at[4 + n]))
+        stores[-1].start()
+    for copy in stores:
+        copy.wait()
+
+
+def sample(rows, grads):
+    return pl.pallas_call(
+        sample_kernel,
+        out_shape=[sds((1536, 128)), sds((3072, 128))],
+        in_specs=[ANY] * 2,
+        out_specs=[ANY] * 2,
+        scratch_shapes=[
+            pltpu.VMEM((3200, 128), F32),
+            pltpu.VMEM((GRAD_ROWS + GRAD_PAD, 128), F32),
+            pltpu.VMEM((1536, 128), F32),
+            pltpu.VMEM((3072, 128), F32),
+            pltpu.SemaphoreType.DMA((6,)),
+        ],
+        compiler_params=LARGE,
         cost_estimate=cost(300_000_000, 9_000_000),
-        name="owner",
+        name="sample",
     )(rows, grads)
+
+
+def deposit_kernel(rows, before, mesh, rows_here, sems):
+    ahead = EARLY * GROUP * 25
+    part = pl.ds(ahead, 3200 - ahead)
+    fetches = [
+        pltpu.make_async_copy(rows.at[part, :], rows_here.at[part, :], sems.at[0]),
+        pltpu.make_async_copy(before, mesh, sems.at[1]),
+    ]
+    for copy in fetches:
+        copy.start()
+    for copy in fetches:
+        copy.wait()
+    each_row(rows_here, lambda s, k, *row: add_patch(mesh, *row), EARLY, 128 // GROUP)
+
+
+def deposit(rows, before):
+    return pl.pallas_call(
+        deposit_kernel,
+        out_shape=sds((3072, 128)),
+        in_specs=[ANY] * 2,
+        out_specs=VMEM,
+        scratch_shapes=[pltpu.VMEM((3200, 128), F32), pltpu.SemaphoreType.DMA((2,))],
+        compiler_params=LARGE,
+        cost_estimate=cost(300_000_000, 40_000_000),
+        name="deposit",
+    )(rows, before)
 
 
 def unpack_kernel(places, back, out, turned):
@@ -436,12 +525,13 @@
     ]
     places, kept = keep(owner_ids[:, 0], vorticity, position, counts, slots)
     ship = route(places, slots, arrivals, kept)
-    rows = exchange(ship.reshape(128, 7, 4, 128)).reshape(3584, 128)
+    rows = exchange(ship.reshape(128, 25, 1, 128)).reshape(3200, 128)
 
     grads = gradient(vel, *arrivals)
 
-    mesh, back = owner_work(rows, grads)
+    back, mesh = sample(rows, grads)
     back = exchange(back.reshape(128, 3, 4, 128)).reshape(1536, 128)
+    mesh = deposit(rows, mesh)
     stretching = unpack(places, back)
     mesh = jnp.transpose(mesh.reshape(4, 16, 3, 16, 128), (0, 1, 3, 2, 4))
     return mesh, stretching

time: 110 us -> 104 us (0.945)
  blocking collectives: 20.1 us -> 0 us
  Pallas kernels: 35.6 us -> 47.1 us
  local copies, waits for them, and re-layouts: 12.4 us -> 3.21 us
  waiting for transfers between devices: 18.2 us -> 25.2 us
  starting transfers between devices: 22.8 us -> 26.9 us
    all_to_all x1 -> x0, blocking collectives: 20.1 us -> none  [exchange(): return lax.all_to_all(value, AXES, split_axis=0, concat_axis=0, tiled=True)]
    pallas_call x2 -> x3, Pallas kernels: 22.8 us -> 34.3 us  [the longest x1 16.3 us: sample(): pl.pallas_call(sample_kernel, out_shape=[sds((1536, 128)), sds((3072, 128...]
    unnamed x36 -> x28, local copies, waits for them, and re-layouts: 12.4 us -> 3.21 us
    all_to_all x1 -> x2, waiting for transfers between devices: 15.4 us -> 22.5 us  [exchange(): return lax.all_to_all(value, AXES, split_axis=0, concat_axis=0, tiled=True)]
    all_to_all x1 -> x2, starting transfers between devices: 11.5 us -> 15.6 us  [exchange(): return lax.all_to_all(value, AXES, split_axis=0, concat_axis=0, tiled=True)]
  transfers between devices with their start and end apart: 5 -> 6, of which waited for: 2 -> 3; matrix products, arithmetic and copies ran while one was open for 0% -> 0% of each run, Pallas kernels for 7% -> 21%
where the time goes in v4:
time: 104 us; the launch traced here: 103 us
  Pallas kernels  47.1 us (45%)
  starting transfers between devices  26.9 us (26%)
  waiting for transfers between devices  25.2 us (24%)
  local copies, waits for them, and re-layouts  3.21 us (3%)
    all_to_all x2, waiting for transfers between devices, exchange(): return lax.all_to_all(value, AXES, split_axis=0, concat_axis=0, tiled=True)  22.5 us
    pallas_call x1, Pallas kernels, sample(): pl.pallas_call(sample_kernel, out_shape=[sds((1536, 128)), sds((3072, 128...  16.3 us
    all_to_all x2, starting transfers between devices, exchange(): return lax.all_to_all(value, AXES, split_axis=0, concat_axis=0, tiled=True)  15.6 us
    pallas_call x1, Pallas kernels, deposit(): pl.pallas_call(deposit_kernel, out_shape=sds((3072, 128)), in_specs=[ANY]...  13.3 us
    ppermute x4, starting transfers between devices, stepped(): lax.ppermute(value, axis, [(source, source + step) for source in range(fi...  11.4 us
    pallas_call x1, Pallas kernels, gradient(): pl.pallas_call(gradient_kernel, out_shape=sds((GRAD_ROWS + GRAD_PAD, 128)...  4.8 us
    pallas_call x1, Pallas kernels, route(): pl.pallas_call(route_kernel, out_shape=sds((3200, 128)), in_specs=[SMEM]...  4.68 us
    unnamed x28, local copies, waits for them, and re-layouts  3.21 us
  transfers between devices with their start and end apart: 6, of which 3 were waited for; matrix products, arithmetic and copies ran while one was open for 0% of the time, Pallas kernels for 21%

profile of v4, /device:TPU:1, one launch (start us, length us, event | category | flops | bytes accessed | tf_op | source)
XLA Modules:
  0.0 103.3 jit_solution(16678083907765889163)
XLA Ops:
  0.6 2.7 %depart.1 = (f32[960,128]{1,0:T(8,128)}, f32[960,128]{1,0:T(8,128)}, f32[384,128]{1,0:T(8,128)}, f32[384,128]{1,0:T(8,128)}) custom-call(f32[3,128,128]{2,1,0:T(8,128)} %vort.3, f32[3,128,128]{2,1,0:T(8,128)} %pos.3, s32[4,128]{1,0:T(4,128)} %counts.3, f32[3072,128]{1,0:T(8,128)} %bitcast.12), custom_call_target="tpu_custom_call" | custom-call | flops 400000 | bytes 3000000 | tf_op jit(solution)/shard_map/depart/pallas_call | solution.py:76
  3.4 4.9 %collective-permute-start = (f32[960,128]{1,0:T(8,128)}, f32[960,128]{1,0:T(8,128)S(1)}, u32[]{:S(2)}, u32[]{:S(2)}) collective-permute-start(f32[960,128]{1,0:T(8,128)} %get-tuple-element.11), channel_id=1, source_target_pairs={{0,4},{4,8},{8,12},{12,16},{16,20},{20,24},{24,28},{28,32},{32,36}... | collective-permute-start | bytes 1474568 | tf_op jit(solution)/shard_map/ppermute | solution.py:509
  8.3 1.9 %collective-permute-start.1 = (f32[960,128]{1,0:T(8,128)}, f32[960,128]{1,0:T(8,128)S(1)}, u32[]{:S(2)}, u32[]{:S(2)}) collective-permute-start(f32[960,128]{1,0:T(8,128)} %get-tuple-element.12), channel_id=1, source_target_pairs={{4,0},{8,4},{12,8},{16,12},{20,16},{24,20},{28,24},{32,28},{36,32}... | collective-permute-start | bytes 1474568 | tf_op jit(solution)/shard_map/ppermute | solution.py:509
  10.2 3.2 %collective-permute-start.2 = (f32[384,128]{1,0:T(8,128)}, f32[384,128]{1,0:T(8,128)S(1)}, u32[]{:S(2)}, u32[]{:S(2)}) collective-permute-start(f32[384,128]{1,0:T(8,128)} %get-tuple-element.13), channel_id=1, source_target_pairs={{0,1},{1,2},{2,3},{4,5},{5,6},{6,7},{8,9},{9,10},{10,11},{12,13},{... | collective-permute-start | bytes 589832 | tf_op jit(solution)/shard_map/ppermute | solution.py:509
  13.5 1.3 %collective-permute-start.3 = (f32[384,128]{1,0:T(8,128)}, f32[384,128]{1,0:T(8,128)S(1)}, u32[]{:S(2)}, u32[]{:S(2)}) collective-permute-start(f32[384,128]{1,0:T(8,128)} %get-tuple-element.14), channel_id=1, source_target_pairs={{1,0},{2,1},{3,2},{5,4},{6,5},{7,6},{9,8},{10,9},{11,10},{13,12},{... | collective-permute-start | bytes 589832 | tf_op jit(solution)/shard_map/ppermute | solution.py:509
  14.8 3.1 %keep.1 = (s32[256]{0:T(256)}, f32[896,128]{1,0:T(8,128)}) custom-call(s32[256]{0:T(256)} %bitcast.20, f32[3,128,128]{2,1,0:T(8,128)} %vort.3, f32[3,128,128]{2,1,0:T(8,128)} %pos.3, s32[4,128]{1,0:T(4,128)} %counts.3, s32[2,128]{1,0:T(2,128)} %bitcast.18), custom_call_target="tpu_custom_call" | custom-call | flops 1000000 | bytes 4000000 | tf_op jit(solution)/shard_map/keep/pallas_call | solution.py:161
  17.9 0.0 copy-start.6
  17.9 2.7 %collective-permute-done.3.a3.za = f32[384,128]{1,0:T(8,128)S(1)} collective-permute-done((f32[384,128]{1,0:T(8,128)}, f32[384,128]{1,0:T(8,128)S(1)}, u32[]{:S(2)}, u32[]{:S(2)}) %collective-permute-start.3) | collective-permute-done | bytes 196640 | tf_op jit(solution)/shard_map/ppermute | solution.py:509
  20.7 0.7 copy-done.8
  21.3 0.2 copy-done.2
  21.5 0.2 copy-done.4
  21.7 4.7 %route.1 = f32[3200,128]{1,0:T(8,128)} custom-call(s32[256]{0:T(256)} %get-tuple-element.10.places, s32[2,128]{1,0:T(2,128)} %bitcast.19, f32[960,128]{1,0:T(8,128)} %copy-done.2, f32[960,128]{1,0:T(8,128)} %copy-done.4, f32[384,128]{1,0:T(8,128)} %copy-done.6, f32[384,128]{1,0:T(8,128)} %copy-done.8, f32[896,128]{1,0:T(8,128)} %get-tuple-element.15.kept), custom_call_target="tpu_custom_call" | custom-call | flops 1000000 | bytes 4000000 | tf_op jit(solution)/shard_map/route/pallas_call | solution.py:211
  26.4 0.0 copy-start.7
  26.4 0.0 copy-start.10
  26.4 0.0 copy-start.12
  26.4 11.9 %all-to-all-start = ((f32[128,25,1,128]{3,2,1,0:T(1,128)}), f32[128,25,1,128]{3,2,1,0:T(1,128)}, u32[]{:S(2)}, u32[]{:S(2)}) async-start(f32[128,25,1,128]{3,2,1,0:T(1,128)} %bitcast.15), calls=%async_computation | async-start | bytes 3276800 | tf_op jit(solution)/shard_map/all_to_all | solution.py:513
  38.4 4.8 %gradient.1.grads = f32[9344,128]{1,0:T(8,128)S(1)} custom-call(f32[3072,128]{1,0:T(8,128)S(1)} %bitcast.13, f32[960,128]{1,0:T(8,128)S(1)} %copy-done.3, f32[960,128]{1,0:T(8,128)S(1)} %copy-done.5, f32[384,128]{1,0:T(8,128)S(1)} %copy-done.7, f32[384,128]{1,0:T(8,128)S(1)} %copy-done.9, bf16[768,128]{1,0:T(8,128)(2,1)S(1)} %copy-done.11, ...), custom_call_target="tpu_custom_call" | custom-call | flops 20000000 | bytes 8000000 | tf_op jit(solution)/shard_map/gradient/pallas_call | solution.py:311
  43.2 2.2 %copy-done = f32[9344,128]{1,0:T(8,128)} copy-done((f32[9344,128]{1,0:T(8,128)}, f32[9344,128]{1,0:T(8,128)S(1)}, u32[]{:S(2)}) %copy-start) | copy-done | bytes 4784152
  45.4 18.7 %all-to-all-done = f32[128,25,1,128]{3,2,1,0:T(1,128)} async-done(((f32[128,25,1,128]{3,2,1,0:T(1,128)}), f32[128,25,1,128]{3,2,1,0:T(1,128)}, u32[]{:S(2)}, u32[]{:S(2)}) %all-to-all-start) | async-done | bytes 1638432 | tf_op jit(solution)/shard_map/all_to_all | solution.py:513
  64.1 16.3 %sample.1 = (f32[1536,128]{1,0:T(8,128)}, f32[3072,128]{1,0:T(8,128)}) custom-call(f32[3200,128]{1,0:T(8,128)} %bitcast.5.rows, f32[9344,128]{1,0:T(8,128)} %copy-done), custom_call_target="tpu_custom_call" | custom-call | flops 300000000 | bytes 9000000 | tf_op jit(solution)/shard_map/sample/pallas_call | solution.py:434
  80.4 3.7 %all-to-all-start.1 = ((f32[128,3,4,128]{3,2,1,0:T(4,128)}), f32[128,3,4,128]{3,2,1,0:T(4,128)S(1)}, u32[]{:S(2)}, u32[]{:S(2)}) async-start(f32[128,3,4,128]{3,2,1,0:T(4,128)} %bitcast.17), calls=%async_computation.1 | async-start | bytes 1572864 | tf_op jit(solution)/shard_map/all_to_all | solution.py:513
  84.1 13.3 %deposit.1 = f32[3072,128]{1,0:T(8,128)} custom-call(f32[3200,128]{1,0:T(8,128)} %bitcast.5.rows, f32[3072,128]{1,0:T(8,128)} %get-tuple-element.16.before), custom_call_target="tpu_custom_call" | custom-call | flops 300000000 | bytes 40000000 | tf_op jit(solution)/shard_map/deposit/pallas_call | solution.py:467
  97.4 3.7 %all-to-all-done.1 = f32[128,3,4,128]{3,2,1,0:T(4,128)S(1)} async-done(((f32[128,3,4,128]{3,2,1,0:T(4,128)}), f32[128,3,4,128]{3,2,1,0:T(4,128)S(1)}, u32[]{:S(2)}, u32[]{:S(2)}) %all-to-all-start.1) | async-done | bytes 786464 | tf_op jit(solution)/shard_map/all_to_all | solution.py:513
  101.2 2.1 %unpack.1 = f32[2,3,128,128]{3,2,1,0:T(8,128)} custom-call(s32[256]{0:T(256)S(1)} %copy-done.13, f32[1536,128]{1,0:T(8,128)S(1)} %bitcast.14), custom_call_target="tpu_custom_call" | custom-call | flops 1000000 | bytes 2000000 | tf_op jit(solution)/shard_map/unpack/pallas_call | solution.py:494
  (23 shorter events, 0.1 us)
Async XLA Ops:
  3.4 17.3 %collective-permute-start = (f32[960,128]{1,0:T(8,128)}, f32[960,128]{1,0:T(8,128)S(1)}, u32[]{:S(2)}, u32[]{:S(2)}) collective-permute-start(f32[960,128]{1,0:T(8,128)} %get-tuple-element.11), channel_id=1, source_target_pairs={{0,4},{4,8},{8,12},{12,16},{16,20},{20,24},{24,28},{28,32},{32,36}... | collective-permute-start | bytes 1474568 | tf_op jit(solution)/shard_map/ppermute | solution.py:509
  8.3 12.3 %collective-permute-start.1 = (f32[960,128]{1,0:T(8,128)}, f32[960,128]{1,0:T(8,128)S(1)}, u32[]{:S(2)}, u32[]{:S(2)}) collective-permute-start(f32[960,128]{1,0:T(8,128)} %get-tuple-element.12), channel_id=1, source_target_pairs={{4,0},{8,4},{12,8},{16,12},{20,16},{24,20},{28,24},{32,28},{36,32}... | collective-permute-start | bytes 1474568 | tf_op jit(solution)/shard_map/ppermute | solution.py:509
  10.2 7.6 %collective-permute-start.2 = (f32[384,128]{1,0:T(8,128)}, f32[384,128]{1,0:T(8,128)S(1)}, u32[]{:S(2)}, u32[]{:S(2)}) collective-permute-start(f32[384,128]{1,0:T(8,128)} %get-tuple-element.13), channel_id=1, source_target_pairs={{0,1},{1,2},{2,3},{4,5},{5,6},{6,7},{8,9},{9,10},{10,11},{12,13},{... | collective-permute-start | bytes 589832 | tf_op jit(solution)/shard_map/ppermute | solution.py:509
  13.5 7.2 %collective-permute-start.3 = (f32[384,128]{1,0:T(8,128)}, f32[384,128]{1,0:T(8,128)S(1)}, u32[]{:S(2)}, u32[]{:S(2)}) collective-permute-start(f32[384,128]{1,0:T(8,128)} %get-tuple-element.14), channel_id=1, source_target_pairs={{1,0},{2,1},{3,2},{5,4},{6,5},{7,6},{9,8},{10,9},{11,10},{13,12},{... | collective-permute-start | bytes 589832 | tf_op jit(solution)/shard_map/ppermute | solution.py:509
  17.9 2.8 %copy-start.6 = (f32[384,128]{1,0:T(8,128)}, f32[384,128]{1,0:T(8,128)S(1)}, u32[]{:S(2)}) copy-start(f32[384,128]{1,0:T(8,128)S(1)} %collective-permute-done.2.a2.zb) | copy-start | bytes 589828
  20.6 0.7 copy-start.8
  20.6 0.8 copy-start.2
  20.7 1.0 copy-start.4
  21.7 16.7 %copy-start.11 = (bf16[768,128]{1,0:T(8,128)(2,1)S(1)}, bf16[768,128]{1,0:T(8,128)(2,1)}, u32[]{:S(2)}) copy-start(bf16[768,128]{1,0:T(8,128)(2,1)} %constant.6.clone.mx) | copy-start | bytes 589828
  26.4 12.0 %copy-start.1 = (f32[4,16,16,3,128]{4,2,3,1,0:T(8,128)S(1)}, f32[4,16,16,3,128]{4,2,3,1,0:T(8,128)}, u32[]{:S(2)}) copy-start(f32[4,16,16,3,128]{4,2,3,1,0:T(8,128)} %param.14) | copy-start | bytes 4718596
  26.4 12.0 %copy-start.3 = (f32[960,128]{1,0:T(8,128)S(1)}, f32[960,128]{1,0:T(8,128)}, u32[]{:S(2)}) copy-start(f32[960,128]{1,0:T(8,128)} %copy-done.2) | copy-start | bytes 1474564
  26.4 12.0 %copy-start.5 = (f32[960,128]{1,0:T(8,128)S(1)}, f32[960,128]{1,0:T(8,128)}, u32[]{:S(2)}) copy-start(f32[960,128]{1,0:T(8,128)} %copy-done.4) | copy-start | bytes 1474564
  26.4 12.0 %copy-start.7 = (f32[384,128]{1,0:T(8,128)S(1)}, f32[384,128]{1,0:T(8,128)}, u32[]{:S(2)}) copy-start(f32[384,128]{1,0:T(8,128)} %copy-done.6) | copy-start | bytes 589828
  26.4 12.0 %copy-start.9 = (f32[384,128]{1,0:T(8,128)S(1)}, f32[384,128]{1,0:T(8,128)}, u32[]{:S(2)}) copy-start(f32[384,128]{1,0:T(8,128)} %copy-done.8) | copy-start | bytes 589828
  26.4 12.0 %copy-start.10 = (bf16[768,128]{1,0:T(8,128)(2,1)S(1)}, bf16[768,128]{1,0:T(8,128)(2,1)}, u32[]{:S(2)}) copy-start(bf16[768,128]{1,0:T(8,128)(2,1)} %constant.7.clone.my) | copy-start | bytes 589828
  26.4 12.0 %copy-start.12 = (bf16[512,128]{1,0:T(8,128)(2,1)S(1)}, bf16[512,128]{1,0:T(8,128)(2,1)}, u32[]{:S(2)}) copy-start(bf16[512,128]{1,0:T(8,128)(2,1)} %constant.8.clone.mz) | copy-start | bytes 393220
  26.4 37.7 %all-to-all-start = ((f32[128,25,1,128]{3,2,1,0:T(1,128)}), f32[128,25,1,128]{3,2,1,0:T(1,128)}, u32[]{:S(2)}, u32[]{:S(2)}) async-start(f32[128,25,1,128]{3,2,1,0:T(1,128)} %bitcast.15), calls=%async_computation | async-start | bytes 3276800 | tf_op jit(solution)/shard_map/all_to_all | solution.py:513
  43.2 2.2 %copy-start = (f32[9344,128]{1,0:T(8,128)}, f32[9344,128]{1,0:T(8,128)S(1)}, u32[]{:S(2)}) copy-start(f32[9344,128]{1,0:T(8,128)S(1)} %gradient.1.grads) | copy-start | bytes 14352388
  80.4 20.8 %all-to-all-start.1 = ((f32[128,3,4,128]{3,2,1,0:T(4,128)}), f32[128,3,4,128]{3,2,1,0:T(4,128)S(1)}, u32[]{:S(2)}, u32[]{:S(2)}) async-start(f32[128,3,4,128]{3,2,1,0:T(4,128)} %bitcast.17), calls=%async_computation.1 | async-start | bytes 1572864 | tf_op jit(solution)/shard_map/all_to_all | solution.py:513
  84.1 17.1 %copy-start.13 = (s32[256]{0:T(256)S(1)}, s32[256]{0:T(256)}, u32[]{:S(2)}) copy-start(s32[256]{0:T(256)} %get-tuple-element.10.places) | copy-start | bytes 3076

commit v5 on v4

--- a/solution.py
+++ b/solution.py
@@ -16,8 +16,8 @@
 LARGE = pltpu.CompilerParams(vmem_limit_bytes=60 * 1024 * 1024)
 GRAD_ROWS = 64 * 9 * 16
 GRAD_PAD = 128
-GROUP = 8
-EARLY = 2
+GROUP = 16
+EARLY = 1
 
 
 def sds(shape, dtype=F32):
@@ -96,37 +96,28 @@
 
 
 def send_rows(places, turned, ship, first):
-    lane = lax.broadcasted_iota(jnp.int32, (1, 128), 1)
-
     def move(r, carry):
         place = places[first + r]
-        base = (place >> 2) * 25
-        rank = place & 3
-        ship[pl.ds(base + rank, 6, stride=4), :] = turned[pl.ds(r, 6, stride=128), :]
-        marks = pl.ds(base + 24, 1)
-        slot = turned[pl.ds(768 + r, 1), :]
-        ship[marks, :] = jnp.where(lane == rank, slot, ship[marks, :])
+        base = (place >> 2) * 25 + (place & 3)
+        ship[pl.ds(base, 6, stride=4), :] = turned[pl.ds(r, 6, stride=128), :]
         return carry
 
     lax.fori_loop(0, 128, move, 0, unroll=8)
 
 
-def slot_rows(slots, half, turned):
-    row = slots[half : half + 1, :].astype(F32)
-    turned[768:896, :] = jnp.broadcast_to(row, (128, 128)).T
-
-
 def keep_kernel(
-    owners, vort, pos, counts, slots, places, turned, tally, v_here, p_here, c_here, s_here, sems
+    owners, slots, vort, pos, counts, places, marks, turned, tally, v_here, p_here, c_here, sems
 ):
     fetches = [
         pltpu.make_async_copy(source, target, sems.at[n])
         for n, (source, target) in enumerate(
-            ((counts, c_here), (vort, v_here), (pos, p_here), (slots, s_here))
+            ((counts, c_here), (vort, v_here), (pos, p_here))
         )
     ]
     for copy in fetches:
         copy.start()
+    marks[...] = jnp.zeros((128, 128), F32)
+    lane = lax.broadcasted_iota(jnp.int32, (1, 128), 1)
     for i in range(128):
         tally[i] = 0
 
@@ -135,6 +126,8 @@
         rank = tally[owner]
         tally[owner] = rank + 1
         places[r] = owner * 4 + rank
+        row = pl.ds(owner, 1)
+        marks[row, :] = jnp.where(lane == rank, slots[r].astype(F32), marks[row, :])
         return carry
 
     lax.fori_loop(0, 256, rank_of, 0, unroll=8)
@@ -154,37 +147,35 @@
         else:
             kept = p_here[comp - 3]
         turned[at * 128 : at * 128 + 128, :] = kept.T
-    slot_rows(s_here, 0, turned)
-
-
-def keep(owners, vort, pos, counts, slots):
+
+
+def keep(owners, slots, vort, pos, counts):
     return pl.pallas_call(
         keep_kernel,
-        out_shape=[sds((256,), jnp.int32), sds((896, 128))],
-        in_specs=[SMEM] + [ANY] * 4,
-        out_specs=[SMEM, VMEM],
+        out_shape=[sds((256,), jnp.int32), sds((128, 128)), sds((768, 128))],
+        in_specs=[SMEM] * 2 + [ANY] * 3,
+        out_specs=[SMEM, VMEM, VMEM],
         scratch_shapes=[
             pltpu.SMEM((128,), jnp.int32),
             pltpu.VMEM((3, 128, 128), F32),
             pltpu.VMEM((3, 128, 128), F32),
             pltpu.VMEM((4, 128), jnp.int32),
-            pltpu.VMEM((2, 128), jnp.int32),
-            pltpu.SemaphoreType.DMA((4,)),
+            pltpu.SemaphoreType.DMA((3,)),
         ],
         compiler_params=LARGE,
         cost_estimate=cost(1_000_000, 4_000_000),
         name="keep",
-    )(owners, vort, pos, counts, slots)
+    )(owners, slots, vort, pos, counts)
 
 
 def route_kernel(
-    places, slots, a0, a1, a2, a3, kept, ship, turned, kept_here, came_here, s_here, sems
+    places, marks, a0, a1, a2, a3, kept, ship, turned, kept_here, came_here, m_here, sems
 ):
     fetches = [
         pltpu.make_async_copy(source.at[pl.ds(0, 192), :], came_here.at[n], sems.at[n])
         for n, source in enumerate((a0, a1, a2, a3))
     ]
-    fetches.append(pltpu.make_async_copy(slots, s_here, sems.at[4]))
+    fetches.append(pltpu.make_async_copy(marks, m_here, sems.at[4]))
     fetches.append(pltpu.make_async_copy(kept, kept_here, sems.at[5]))
     for copy in fetches:
         copy.start()
@@ -203,27 +194,27 @@
             [came_here[n, 32 * comp : 32 * comp + 32, :] for n in range(4)], axis=0
         )
         turned[at * 128 : at * 128 + 128, :] = came.T
-    slot_rows(s_here, 1, turned)
     send_rows(places, turned, ship, 128)
-
-
-def route(places, slots, arrivals, kept):
+    ship[pl.ds(24, 128, stride=25), :] = m_here[...]
+
+
+def route(places, marks, arrivals, kept):
     return pl.pallas_call(
         route_kernel,
         out_shape=sds((3200, 128)),
         in_specs=[SMEM] + [ANY] * 6,
         out_specs=VMEM,
         scratch_shapes=[
-            pltpu.VMEM((896, 128), F32),
-            pltpu.VMEM((896, 128), F32),
+            pltpu.VMEM((768, 128), F32),
+            pltpu.VMEM((768, 128), F32),
             pltpu.VMEM((4, 192, 128), F32),
-            pltpu.VMEM((2, 128), jnp.int32),
+            pltpu.VMEM((128, 128), F32),
             pltpu.SemaphoreType.DMA((6,)),
         ],
         compiler_params=LARGE,
         cost_estimate=cost(1_000_000, 4_000_000),
         name="route",
-    )(places, slots, *arrivals, kept)
+    )(places, marks, *arrivals, kept)
 
 
 def stencil(stride, per):
@@ -349,10 +340,9 @@
             )
             yz = [wide(weights[b][4 + k : 5 + k]) * along_z for b in range(4)]
             xs = [wide(weights[a][k : k + 1]) for a in range(4)]
-            table = jnp.concatenate([xs[a] * yz[b] for a in range(4) for b in range(4)], axis=0)
             vortex = [rows[pl.ds(base + 8 + 4 * j + k, 1), :] for j in range(3)]
             slot = slots[0, k]
-            work(s, k, slot >> 4, slot & 15, vortex, *split(table))
+            work(s, k, slot >> 4, slot & 15, vortex, xs, yz)
 
     def per_group(q, carry):
         base = pl.multiple_of(q * (25 * GROUP), 8)
@@ -363,7 +353,12 @@
     lax.fori_loop(first, last, per_group, 0)
 
 
-def sampled_row(grads, column, level, vortex, high, low):
+def weight_table(xs, yz):
+    return split(jnp.concatenate([xs[a] * yz[b] for a in range(4) for b in range(4)], axis=0))
+
+
+def sampled_row(grads, column, level, vortex, xs, yz):
+    high, low = weight_table(xs, yz)
     grad = jnp.concatenate(
         [grads[pl.ds(column * 144 + j * 48 + level, 8, stride=16), :] for j in range(3)],
         axis=0,
@@ -380,7 +375,8 @@
     return stretch[:3]
 
 
-def add_patch(mesh, column, level, vortex, high, low):
+def add_patch(mesh, column, level, vortex, xs, yz):
+    high, low = weight_table(xs, yz)
     v = jnp.concatenate(vortex + [jnp.zeros((5, 128), F32)], axis=0)
     left = jnp.concatenate(split(v), axis=0)
     left = jnp.concatenate([left, left], axis=1)
@@ -514,7 +510,6 @@
 
 
 def on_device(vorticity, position, counts, owner_ids, slot_ids, velocity):
-    slots = slot_ids.reshape(2, 128)
     vel = jnp.transpose(velocity, (0, 1, 3, 2, 4)).reshape(3072, 128)
     leaving = depart(vorticity, position, counts, vel)
     arrivals = [
@@ -523,8 +518,8 @@
         stepped(leaving[2], "gz", 1),
         stepped(leaving[3], "gz", -1),
     ]
-    places, kept = keep(owner_ids[:, 0], vorticity, position, counts, slots)
-    ship = route(places, slots, arrivals, kept)
+    places, marks, kept = keep(owner_ids[:, 0], slot_ids, vorticity, position, counts)
+    ship = route(places, marks, arrivals, kept)
     rows = exchange(ship.reshape(128, 25, 1, 128)).reshape(3200, 128)
 
     grads = gradient(vel, *arrivals)

time: 104 us -> 103 us (level)
  Pallas kernels: 47.1 us -> 45.1 us
  transfers between devices with their start and end apart: 6 -> 6, of which waited for: 3 -> 3; matrix products, arithmetic and copies ran while one was open for 0% -> 0% of each run, Pallas kernels for 21% -> 20%
where the time goes in v5:
time: 103 us; the launch traced here: 102 us
  Pallas kernels  45.1 us (44%)
  starting transfers between devices  26.9 us (26%)
  waiting for transfers between devices  26 us (25%)
  local copies, waits for them, and re-layouts  3.21 us (3%)
    all_to_all x2, waiting for transfers between devices, exchange(): return lax.all_to_all(value, AXES, split_axis=0, concat_axis=0, tiled=True)  23.2 us
    all_to_all x2, starting transfers between devices, exchange(): return lax.all_to_all(value, AXES, split_axis=0, concat_axis=0, tiled=True)  15.5 us
    pallas_call x1, Pallas kernels, sample(): pl.pallas_call(sample_kernel, out_shape=[sds((1536, 128)), sds((3072, 128...  15.5 us
    pallas_call x1, Pallas kernels, deposit(): pl.pallas_call(deposit_kernel, out_shape=sds((3072, 128)), in_specs=[ANY]...  12.6 us
    ppermute x4, starting transfers between devices, stepped(): lax.ppermute(value, axis, [(source, source + step) for source in range(fi...  11.4 us
    pallas_call x1, Pallas kernels, gradient(): pl.pallas_call(gradient_kernel, out_shape=sds((GRAD_ROWS + GRAD_PAD, 128)...  4.8 us
    pallas_call x1, Pallas kernels, route(): pl.pallas_call(route_kernel, out_shape=sds((3200, 128)), in_specs=[SMEM]...  4.28 us
    unnamed x28, local copies, waits for them, and re-layouts  3.21 us
  transfers between devices with their start and end apart: 6, of which 3 were waited for; matrix products, arithmetic and copies ran while one was open for 0% of the time, Pallas kernels for 20%

profile of v5, /device:TPU:1, one launch (start us, length us, event | category | flops | bytes accessed | tf_op | source)
XLA Modules:
  0.0 102.1 jit_solution(4185937591243968281)
XLA Ops:
  0.6 2.7 %depart.1 = (f32[960,128]{1,0:T(8,128)}, f32[960,128]{1,0:T(8,128)}, f32[384,128]{1,0:T(8,128)}, f32[384,128]{1,0:T(8,128)}) custom-call(f32[3,128,128]{2,1,0:T(8,128)} %vort.3, f32[3,128,128]{2,1,0:T(8,128)} %pos.3, s32[4,128]{1,0:T(4,128)} %counts.3, f32[3072,128]{1,0:T(8,128)} %bitcast.11), custom_call_target="tpu_custom_call" | custom-call | flops 400000 | bytes 3000000 | tf_op jit(solution)/shard_map/depart/pallas_call | solution.py:76
  3.4 4.9 %collective-permute-start = (f32[960,128]{1,0:T(8,128)}, f32[960,128]{1,0:T(8,128)S(1)}, u32[]{:S(2)}, u32[]{:S(2)}) collective-permute-start(f32[960,128]{1,0:T(8,128)} %get-tuple-element.13), channel_id=1, source_target_pairs={{0,4},{4,8},{8,12},{12,16},{16,20},{20,24},{24,28},{28,32},{32,36}... | collective-permute-start | bytes 1474568 | tf_op jit(solution)/shard_map/ppermute | solution.py:505
  8.3 1.9 %collective-permute-start.1 = (f32[960,128]{1,0:T(8,128)}, f32[960,128]{1,0:T(8,128)S(1)}, u32[]{:S(2)}, u32[]{:S(2)}) collective-permute-start(f32[960,128]{1,0:T(8,128)} %get-tuple-element.14), channel_id=1, source_target_pairs={{4,0},{8,4},{12,8},{16,12},{20,16},{24,20},{28,24},{32,28},{36,32}... | collective-permute-start | bytes 1474568 | tf_op jit(solution)/shard_map/ppermute | solution.py:505
  10.2 3.2 %collective-permute-start.2 = (f32[384,128]{1,0:T(8,128)}, f32[384,128]{1,0:T(8,128)S(1)}, u32[]{:S(2)}, u32[]{:S(2)}) collective-permute-start(f32[384,128]{1,0:T(8,128)} %get-tuple-element.15), channel_id=1, source_target_pairs={{0,1},{1,2},{2,3},{4,5},{5,6},{6,7},{8,9},{9,10},{10,11},{12,13},{... | collective-permute-start | bytes 589832 | tf_op jit(solution)/shard_map/ppermute | solution.py:505
  13.5 1.3 %collective-permute-start.3 = (f32[384,128]{1,0:T(8,128)}, f32[384,128]{1,0:T(8,128)S(1)}, u32[]{:S(2)}, u32[]{:S(2)}) collective-permute-start(f32[384,128]{1,0:T(8,128)} %get-tuple-element.16), channel_id=1, source_target_pairs={{1,0},{2,1},{3,2},{5,4},{6,5},{7,6},{9,8},{10,9},{11,10},{13,12},{... | collective-permute-start | bytes 589832 | tf_op jit(solution)/shard_map/ppermute | solution.py:505
  14.8 3.1 %keep.1 = (s32[256]{0:T(256)}, f32[128,128]{1,0:T(8,128)}, f32[768,128]{1,0:T(8,128)}) custom-call(s32[256]{0:T(256)} %bitcast.17, s32[256]{0:T(256)} %slots.1, f32[3,128,128]{2,1,0:T(8,128)} %vort.3, f32[3,128,128]{2,1,0:T(8,128)} %pos.3, s32[4,128]{1,0:T(4,128)} %counts.3), custom_call_target="tpu_custom_call" | custom-call | flops 1000000 | bytes 4000000 | tf_op jit(solution)/shard_map/keep/pallas_call | solution.py:153
  17.8 2.8 %collective-permute-done.3.a3.za = f32[384,128]{1,0:T(8,128)S(1)} collective-permute-done((f32[384,128]{1,0:T(8,128)}, f32[384,128]{1,0:T(8,128)S(1)}, u32[]{:S(2)}, u32[]{:S(2)}) %collective-permute-start.3) | collective-permute-done | bytes 196640 | tf_op jit(solution)/shard_map/ppermute | solution.py:505
  20.7 0.7 copy-done.8
  21.3 0.2 copy-done.2
  21.5 0.2 copy-done.4
  21.7 4.3 %route.1 = f32[3200,128]{1,0:T(8,128)} custom-call(s32[256]{0:T(256)} %get-tuple-element.11.places, f32[128,128]{1,0:T(8,128)} %get-tuple-element.12.marks, f32[960,128]{1,0:T(8,128)} %copy-done.2, f32[960,128]{1,0:T(8,128)} %copy-done.4, f32[384,128]{1,0:T(8,128)} %copy-done.6, f32[384,128]{1,0:T(8,128)} %copy-done.8, f32[768,128]{1,0:T(8,128)} %get-tuple-element.17.kept), custom_call_target="tpu_custom_call" | custom-call | flops 1000000 | bytes 4000000 | tf_op jit(solution)/shard_map/route/pallas_call | solution.py:202
  26.0 0.0 copy-start.1
  26.0 0.0 copy-start.3
  26.0 0.0 copy-start.10
  26.0 0.0 copy-start.12
  26.0 11.9 %all-to-all-start = ((f32[128,25,1,128]{3,2,1,0:T(1,128)}), f32[128,25,1,128]{3,2,1,0:T(1,128)}, u32[]{:S(2)}, u32[]{:S(2)}) async-start(f32[128,25,1,128]{3,2,1,0:T(1,128)} %bitcast.14), calls=%async_computation | async-start | bytes 3276800 | tf_op jit(solution)/shard_map/all_to_all | solution.py:509
  38.0 4.8 %gradient.1.grads = f32[9344,128]{1,0:T(8,128)S(1)} custom-call(f32[3072,128]{1,0:T(8,128)S(1)} %bitcast.12, f32[960,128]{1,0:T(8,128)S(1)} %copy-done.3, f32[960,128]{1,0:T(8,128)S(1)} %copy-done.5, f32[384,128]{1,0:T(8,128)S(1)} %copy-done.7, f32[384,128]{1,0:T(8,128)S(1)} %copy-done.9, bf16[768,128]{1,0:T(8,128)(2,1)S(1)} %copy-done.11, ...), custom_call_target="tpu_custom_call" | custom-call | flops 20000000 | bytes 8000000 | tf_op jit(solution)/shard_map/gradient/pallas_call | solution.py:302
  42.8 2.2 %copy-done = f32[9344,128]{1,0:T(8,128)} copy-done((f32[9344,128]{1,0:T(8,128)}, f32[9344,128]{1,0:T(8,128)S(1)}, u32[]{:S(2)}) %copy-start) | copy-done | bytes 4784152
  45.0 18.7 %all-to-all-done = f32[128,25,1,128]{3,2,1,0:T(1,128)} async-done(((f32[128,25,1,128]{3,2,1,0:T(1,128)}), f32[128,25,1,128]{3,2,1,0:T(1,128)}, u32[]{:S(2)}, u32[]{:S(2)}) %all-to-all-start) | async-done | bytes 1638432 | tf_op jit(solution)/shard_map/all_to_all | solution.py:509
  63.7 15.5 %sample.1 = (f32[1536,128]{1,0:T(8,128)}, f32[3072,128]{1,0:T(8,128)}) custom-call(f32[3200,128]{1,0:T(8,128)} %bitcast.4.rows, f32[9344,128]{1,0:T(8,128)} %copy-done), custom_call_target="tpu_custom_call" | custom-call | flops 300000000 | bytes 9000000 | tf_op jit(solution)/shard_map/sample/pallas_call | solution.py:430
  79.2 3.7 %all-to-all-start.1 = ((f32[128,3,4,128]{3,2,1,0:T(4,128)}), f32[128,3,4,128]{3,2,1,0:T(4,128)S(1)}, u32[]{:S(2)}, u32[]{:S(2)}) async-start(f32[128,3,4,128]{3,2,1,0:T(4,128)} %bitcast.16), calls=%async_computation.1 | async-start | bytes 1572864 | tf_op jit(solution)/shard_map/all_to_all | solution.py:509
  82.9 12.6 %deposit.1 = f32[3072,128]{1,0:T(8,128)} custom-call(f32[3200,128]{1,0:T(8,128)} %bitcast.4.rows, f32[3072,128]{1,0:T(8,128)} %get-tuple-element.18.before), custom_call_target="tpu_custom_call" | custom-call | flops 300000000 | bytes 40000000 | tf_op jit(solution)/shard_map/deposit/pallas_call | solution.py:463
  95.5 4.5 %all-to-all-done.1 = f32[128,3,4,128]{3,2,1,0:T(4,128)S(1)} async-done(((f32[128,3,4,128]{3,2,1,0:T(4,128)}), f32[128,3,4,128]{3,2,1,0:T(4,128)S(1)}, u32[]{:S(2)}, u32[]{:S(2)}) %all-to-all-start.1) | async-done | bytes 786464 | tf_op jit(solution)/shard_map/all_to_all | solution.py:509
  100.0 2.1 %unpack.1 = f32[2,3,128,128]{3,2,1,0:T(8,128)} custom-call(s32[256]{0:T(256)S(1)} %copy-done.13, f32[1536,128]{1,0:T(8,128)S(1)} %bitcast.13), custom_call_target="tpu_custom_call" | custom-call | flops 1000000 | bytes 2000000 | tf_op jit(solution)/shard_map/unpack/pallas_call | solution.py:490
  (23 shorter events, 0.0 us)
Async XLA Ops:
  3.4 17.3 %collective-permute-start = (f32[960,128]{1,0:T(8,128)}, f32[960,128]{1,0:T(8,128)S(1)}, u32[]{:S(2)}, u32[]{:S(2)}) collective-permute-start(f32[960,128]{1,0:T(8,128)} %get-tuple-element.13), channel_id=1, source_target_pairs={{0,4},{4,8},{8,12},{12,16},{16,20},{20,24},{24,28},{28,32},{32,36}... | collective-permute-start | bytes 1474568 | tf_op jit(solution)/shard_map/ppermute | solution.py:505
  8.3 12.3 %collective-permute-start.1 = (f32[960,128]{1,0:T(8,128)}, f32[960,128]{1,0:T(8,128)S(1)}, u32[]{:S(2)}, u32[]{:S(2)}) collective-permute-start(f32[960,128]{1,0:T(8,128)} %get-tuple-element.14), channel_id=1, source_target_pairs={{4,0},{8,4},{12,8},{16,12},{20,16},{24,20},{28,24},{32,28},{36,32}... | collective-permute-start | bytes 1474568 | tf_op jit(solution)/shard_map/ppermute | solution.py:505
  10.2 7.6 %collective-permute-start.2 = (f32[384,128]{1,0:T(8,128)}, f32[384,128]{1,0:T(8,128)S(1)}, u32[]{:S(2)}, u32[]{:S(2)}) collective-permute-start(f32[384,128]{1,0:T(8,128)} %get-tuple-element.15), channel_id=1, source_target_pairs={{0,1},{1,2},{2,3},{4,5},{5,6},{6,7},{8,9},{9,10},{10,11},{12,13},{... | collective-permute-start | bytes 589832 | tf_op jit(solution)/shard_map/ppermute | solution.py:505
  13.5 7.2 %collective-permute-start.3 = (f32[384,128]{1,0:T(8,128)}, f32[384,128]{1,0:T(8,128)S(1)}, u32[]{:S(2)}, u32[]{:S(2)}) collective-permute-start(f32[384,128]{1,0:T(8,128)} %get-tuple-element.16), channel_id=1, source_target_pairs={{1,0},{2,1},{3,2},{5,4},{6,5},{7,6},{9,8},{10,9},{11,10},{13,12},{... | collective-permute-start | bytes 589832 | tf_op jit(solution)/shard_map/ppermute | solution.py:505
  17.8 2.8 %copy-start.6 = (f32[384,128]{1,0:T(8,128)}, f32[384,128]{1,0:T(8,128)S(1)}, u32[]{:S(2)}) copy-start(f32[384,128]{1,0:T(8,128)S(1)} %collective-permute-done.2.a2.zb) | copy-start | bytes 589828
  20.6 0.7 copy-start.8
  20.6 0.8 copy-start.2
  20.7 1.0 copy-start.4
  21.7 16.3 %copy-start.11 = (bf16[768,128]{1,0:T(8,128)(2,1)S(1)}, bf16[768,128]{1,0:T(8,128)(2,1)}, u32[]{:S(2)}) copy-start(bf16[768,128]{1,0:T(8,128)(2,1)} %constant.6.clone.mx) | copy-start | bytes 589828
  26.0 12.0 %copy-start.1 = (f32[4,16,16,3,128]{4,2,3,1,0:T(8,128)S(1)}, f32[4,16,16,3,128]{4,2,3,1,0:T(8,128)}, u32[]{:S(2)}) copy-start(f32[4,16,16,3,128]{4,2,3,1,0:T(8,128)} %param.14) | copy-start | bytes 4718596
  26.0 12.0 %copy-start.3 = (f32[960,128]{1,0:T(8,128)S(1)}, f32[960,128]{1,0:T(8,128)}, u32[]{:S(2)}) copy-start(f32[960,128]{1,0:T(8,128)} %copy-done.2) | copy-start | bytes 1474564
  26.0 12.0 %copy-start.5 = (f32[960,128]{1,0:T(8,128)S(1)}, f32[960,128]{1,0:T(8,128)}, u32[]{:S(2)}) copy-start(f32[960,128]{1,0:T(8,128)} %copy-done.4) | copy-start | bytes 1474564
  26.0 12.0 %copy-start.7 = (f32[384,128]{1,0:T(8,128)S(1)}, f32[384,128]{1,0:T(8,128)}, u32[]{:S(2)}) copy-start(f32[384,128]{1,0:T(8,128)} %copy-done.6) | copy-start | bytes 589828
  26.0 12.0 %copy-start.9 = (f32[384,128]{1,0:T(8,128)S(1)}, f32[384,128]{1,0:T(8,128)}, u32[]{:S(2)}) copy-start(f32[384,128]{1,0:T(8,128)} %copy-done.8) | copy-start | bytes 589828
  26.0 12.0 %copy-start.10 = (bf16[768,128]{1,0:T(8,128)(2,1)S(1)}, bf16[768,128]{1,0:T(8,128)(2,1)}, u32[]{:S(2)}) copy-start(bf16[768,128]{1,0:T(8,128)(2,1)} %constant.7.clone.my) | copy-start | bytes 589828
  26.0 12.0 %copy-start.12 = (bf16[512,128]{1,0:T(8,128)(2,1)S(1)}, bf16[512,128]{1,0:T(8,128)(2,1)}, u32[]{:S(2)}) copy-start(bf16[512,128]{1,0:T(8,128)(2,1)} %constant.8.clone.mz) | copy-start | bytes 393220
  26.0 37.7 %all-to-all-start = ((f32[128,25,1,128]{3,2,1,0:T(1,128)}), f32[128,25,1,128]{3,2,1,0:T(1,128)}, u32[]{:S(2)}, u32[]{:S(2)}) async-start(f32[128,25,1,128]{3,2,1,0:T(1,128)} %bitcast.14), calls=%async_computation | async-start | bytes 3276800 | tf_op jit(solution)/shard_map/all_to_all | solution.py:509
  42.8 2.2 %copy-start = (f32[9344,128]{1,0:T(8,128)}, f32[9344,128]{1,0:T(8,128)S(1)}, u32[]{:S(2)}) copy-start(f32[9344,128]{1,0:T(8,128)S(1)} %gradient.1.grads) | copy-start | bytes 14352388
  79.2 20.8 %all-to-all-start.1 = ((f32[128,3,4,128]{3,2,1,0:T(4,128)}), f32[128,3,4,128]{3,2,1,0:T(4,128)S(1)}, u32[]{:S(2)}, u32[]{:S(2)}) async-start(f32[128,3,4,128]{3,2,1,0:T(4,128)} %bitcast.16), calls=%async_computation.1 | async-start | bytes 1572864 | tf_op jit(solution)/shard_map/all_to_all | solution.py:509
  82.9 17.1 %copy-start.13 = (s32[256]{0:T(256)S(1)}, s32[256]{0:T(256)}, u32[]{:S(2)}) copy-start(s32[256]{0:T(256)} %get-tuple-element.11.places) | copy-start | bytes 3076

commit v6 on v5

--- a/solution.py
+++ b/solution.py
@@ -169,7 +169,20 @@
 
 
 def route_kernel(
-    places, marks, a0, a1, a2, a3, kept, ship, turned, kept_here, came_here, m_here, sems
+    places,
+    marks,
+    a0,
+    a1,
+    a2,
+    a3,
+    kept,
+    ship,
+    turned,
+    kept_here,
+    came_here,
+    m_here,
+    places_here,
+    sems,
 ):
     fetches = [
         pltpu.make_async_copy(source.at[pl.ds(0, 192), :], came_here.at[n], sems.at[n])
@@ -177,6 +190,7 @@
     ]
     fetches.append(pltpu.make_async_copy(marks, m_here, sems.at[4]))
     fetches.append(pltpu.make_async_copy(kept, kept_here, sems.at[5]))
+    fetches.append(pltpu.make_async_copy(places, places_here, sems.at[6]))
     for copy in fetches:
         copy.start()
 
@@ -185,8 +199,9 @@
         return carry
 
     lax.fori_loop(0, 50, clear, 0)
-    fetches[5].wait()
-    send_rows(places, kept_here, ship, 0)
+    for copy in fetches[5:]:
+        copy.wait()
+    send_rows(places_here, kept_here, ship, 0)
     for copy in fetches[:5]:
         copy.wait()
     for at, comp in enumerate(ORDER):
@@ -194,7 +209,7 @@
             [came_here[n, 32 * comp : 32 * comp + 32, :] for n in range(4)], axis=0
         )
         turned[at * 128 : at * 128 + 128, :] = came.T
-    send_rows(places, turned, ship, 128)
+    send_rows(places_here, turned, ship, 128)
     ship[pl.ds(24, 128, stride=25), :] = m_here[...]
 
 
@@ -202,14 +217,15 @@
     return pl.pallas_call(
         route_kernel,
         out_shape=sds((3200, 128)),
-        in_specs=[SMEM] + [ANY] * 6,
+        in_specs=[ANY] * 7,
         out_specs=VMEM,
         scratch_shapes=[
             pltpu.VMEM((768, 128), F32),
             pltpu.VMEM((768, 128), F32),
             pltpu.VMEM((4, 192, 128), F32),
             pltpu.VMEM((128, 128), F32),
-            pltpu.SemaphoreType.DMA((6,)),
+            pltpu.SMEM((256,), jnp.int32),
+            pltpu.SemaphoreType.DMA((7,)),
         ],
         compiler_params=LARGE,
         cost_estimate=cost(1_000_000, 4_000_000),
@@ -472,18 +488,23 @@
     )(rows, before)
 
 
-def unpack_kernel(places, back, out, turned):
+def unpack_kernel(places, back, out, turned, whole, sems):
     def move(r, carry):
         place = places[r]
         base = (place >> 2) * 12 + (place & 3)
         turned[pl.ds(r, 3, stride=256), :] = back[pl.ds(base, 3, stride=4), :]
         return carry
 
-    lax.fori_loop(0, 256, move, 0, unroll=8)
+    stores = []
     for h in range(2):
+        lax.fori_loop(h * 128, h * 128 + 128, move, 0, unroll=16)
         for i in range(3):
             at = i * 256 + h * 128
-            out[h, i] = turned[at : at + 128, :].T
+            whole[h, i] = turned[at : at + 128, :].T
+        stores.append(pltpu.make_async_copy(whole.at[h], out.at[h], sems.at[h]))
+        stores[-1].start()
+    for copy in stores:
+        copy.wait()
 
 
 def unpack(places, back):
@@ -491,8 +512,12 @@
         unpack_kernel,
         out_shape=sds((2, 3, 128, 128)),
         in_specs=[SMEM, VMEM],
-        out_specs=VMEM,
-        scratch_shapes=[pltpu.VMEM((768, 128), F32)],
+        out_specs=ANY,
+        scratch_shapes=[
+            pltpu.VMEM((768, 128), F32),
+            pltpu.VMEM((2, 3, 128, 128), F32),
+            pltpu.SemaphoreType.DMA((2,)),
+        ],
         compiler_params=PARAMS,
         cost_estimate=cost(1_000_000, 2_000_000),
         name="unpack",

time: 103 us -> 102 us (level)
  no operation moved by 1% of the time
where the time goes in v6:
time: 102 us; the launch traced here: 101 us
  Pallas kernels  44.4 us (44%)
  starting transfers between devices  26.9 us (26%)
  waiting for transfers between devices  26 us (25%)
  local copies, waits for them, and re-layouts  3.21 us (3%)
    all_to_all x2, waiting for transfers between devices, exchange(): return lax.all_to_all(value, AXES, split_axis=0, concat_axis=0, tiled=True)  23.2 us
    all_to_all x2, starting transfers between devices, exchange(): return lax.all_to_all(value, AXES, split_axis=0, concat_axis=0, tiled=True)  15.6 us
    pallas_call x1, Pallas kernels, sample(): pl.pallas_call(sample_kernel, out_shape=[sds((1536, 128)), sds((3072, 128...  15.5 us
    pallas_call x1, Pallas kernels, deposit(): pl.pallas_call(deposit_kernel, out_shape=sds((3072, 128)), in_specs=[ANY]...  12.6 us
    ppermute x4, starting transfers between devices, stepped(): lax.ppermute(value, axis, [(source, source + step) for source in range(fi...  11.4 us
    pallas_call x1, Pallas kernels, gradient(): pl.pallas_call(gradient_kernel, out_shape=sds((GRAD_ROWS + GRAD_PAD, 128)...  4.8 us
    pallas_call x1, Pallas kernels, route(): pl.pallas_call(route_kernel, out_shape=sds((3200, 128)), in_specs=[ANY] *...  3.52 us
    unnamed x28, local copies, waits for them, and re-layouts  3.21 us
  transfers between devices with their start and end apart: 6, of which 3 were waited for; matrix products, arithmetic and copies ran while one was open for 0% of the time, Pallas kernels for 20%

profile of v6, /device:TPU:1, one launch (start us, length us, event | category | flops | bytes accessed | tf_op | source)
XLA Modules:
  0.0 101.4 jit_solution(7519128234221869576)
XLA Ops:
  0.6 2.7 %depart.1 = (f32[960,128]{1,0:T(8,128)}, f32[960,128]{1,0:T(8,128)}, f32[384,128]{1,0:T(8,128)}, f32[384,128]{1,0:T(8,128)}) custom-call(f32[3,128,128]{2,1,0:T(8,128)} %vort.3, f32[3,128,128]{2,1,0:T(8,128)} %pos.3, s32[4,128]{1,0:T(4,128)} %counts.3, f32[3072,128]{1,0:T(8,128)} %bitcast.11), custom_call_target="tpu_custom_call" | custom-call | flops 400000 | bytes 3000000 | tf_op jit(solution)/shard_map/depart/pallas_call | solution.py:76
  3.4 4.9 %collective-permute-start = (f32[960,128]{1,0:T(8,128)}, f32[960,128]{1,0:T(8,128)S(1)}, u32[]{:S(2)}, u32[]{:S(2)}) collective-permute-start(f32[960,128]{1,0:T(8,128)} %get-tuple-element.13), channel_id=1, source_target_pairs={{0,4},{4,8},{8,12},{12,16},{16,20},{20,24},{24,28},{28,32},{32,36}... | collective-permute-start | bytes 1474568 | tf_op jit(solution)/shard_map/ppermute | solution.py:530
  8.3 1.9 %collective-permute-start.1 = (f32[960,128]{1,0:T(8,128)}, f32[960,128]{1,0:T(8,128)S(1)}, u32[]{:S(2)}, u32[]{:S(2)}) collective-permute-start(f32[960,128]{1,0:T(8,128)} %get-tuple-element.14), channel_id=1, source_target_pairs={{4,0},{8,4},{12,8},{16,12},{20,16},{24,20},{28,24},{32,28},{36,32}... | collective-permute-start | bytes 1474568 | tf_op jit(solution)/shard_map/ppermute | solution.py:530
  10.2 3.2 %collective-permute-start.2 = (f32[384,128]{1,0:T(8,128)}, f32[384,128]{1,0:T(8,128)S(1)}, u32[]{:S(2)}, u32[]{:S(2)}) collective-permute-start(f32[384,128]{1,0:T(8,128)} %get-tuple-element.15), channel_id=1, source_target_pairs={{0,1},{1,2},{2,3},{4,5},{5,6},{6,7},{8,9},{9,10},{10,11},{12,13},{... | collective-permute-start | bytes 589832 | tf_op jit(solution)/shard_map/ppermute | solution.py:530
  13.5 1.3 %collective-permute-start.3 = (f32[384,128]{1,0:T(8,128)}, f32[384,128]{1,0:T(8,128)S(1)}, u32[]{:S(2)}, u32[]{:S(2)}) collective-permute-start(f32[384,128]{1,0:T(8,128)} %get-tuple-element.16), channel_id=1, source_target_pairs={{1,0},{2,1},{3,2},{5,4},{6,5},{7,6},{9,8},{10,9},{11,10},{13,12},{... | collective-permute-start | bytes 589832 | tf_op jit(solution)/shard_map/ppermute | solution.py:530
  14.8 3.1 %keep.1 = (s32[256]{0:T(256)}, f32[128,128]{1,0:T(8,128)}, f32[768,128]{1,0:T(8,128)}) custom-call(s32[256]{0:T(256)} %bitcast.17, s32[256]{0:T(256)} %slots.1, f32[3,128,128]{2,1,0:T(8,128)} %vort.3, f32[3,128,128]{2,1,0:T(8,128)} %pos.3, s32[4,128]{1,0:T(4,128)} %counts.3), custom_call_target="tpu_custom_call" | custom-call | flops 1000000 | bytes 4000000 | tf_op jit(solution)/shard_map/keep/pallas_call | solution.py:153
  17.8 2.8 %collective-permute-done.3.a3.za = f32[384,128]{1,0:T(8,128)S(1)} collective-permute-done((f32[384,128]{1,0:T(8,128)}, f32[384,128]{1,0:T(8,128)S(1)}, u32[]{:S(2)}, u32[]{:S(2)}) %collective-permute-start.3) | collective-permute-done | bytes 196640 | tf_op jit(solution)/shard_map/ppermute | solution.py:530
  20.7 0.7 copy-done.8
  21.3 0.2 copy-done.2
  21.5 0.2 copy-done.4
  21.7 3.5 %route.1 = f32[3200,128]{1,0:T(8,128)} custom-call(s32[256]{0:T(256)} %get-tuple-element.11.places, f32[128,128]{1,0:T(8,128)} %get-tuple-element.12.marks, f32[960,128]{1,0:T(8,128)} %copy-done.2, f32[960,128]{1,0:T(8,128)} %copy-done.4, f32[384,128]{1,0:T(8,128)} %copy-done.6, f32[384,128]{1,0:T(8,128)} %copy-done.8, f32[768,128]{1,0:T(8,128)} %get-tuple-element.17.kept), custom_call_target="tpu_custom_call" | custom-call | flops 1000000 | bytes 4000000 | tf_op jit(solution)/shard_map/route/pallas_call | solution.py:217
  25.2 0.0 copy-start.1
  25.2 0.0 copy-start.3
  25.2 0.0 copy-start.10
  25.3 0.0 copy-start.12
  25.3 11.9 %all-to-all-start = ((f32[128,25,1,128]{3,2,1,0:T(1,128)}), f32[128,25,1,128]{3,2,1,0:T(1,128)}, u32[]{:S(2)}, u32[]{:S(2)}) async-start(f32[128,25,1,128]{3,2,1,0:T(1,128)} %bitcast.14), calls=%async_computation | async-start | bytes 3276800 | tf_op jit(solution)/shard_map/all_to_all | solution.py:534
  37.2 4.8 %gradient.1.grads = f32[9344,128]{1,0:T(8,128)S(1)} custom-call(f32[3072,128]{1,0:T(8,128)S(1)} %bitcast.12, f32[960,128]{1,0:T(8,128)S(1)} %copy-done.3, f32[960,128]{1,0:T(8,128)S(1)} %copy-done.5, f32[384,128]{1,0:T(8,128)S(1)} %copy-done.7, f32[384,128]{1,0:T(8,128)S(1)} %copy-done.9, bf16[768,128]{1,0:T(8,128)(2,1)S(1)} %copy-done.11, ...), custom_call_target="tpu_custom_call" | custom-call | flops 20000000 | bytes 8000000 | tf_op jit(solution)/shard_map/gradient/pallas_call | solution.py:318
  42.1 2.2 %copy-done = f32[9344,128]{1,0:T(8,128)} copy-done((f32[9344,128]{1,0:T(8,128)}, f32[9344,128]{1,0:T(8,128)S(1)}, u32[]{:S(2)}) %copy-start) | copy-done | bytes 4784152
  44.2 18.7 %all-to-all-done = f32[128,25,1,128]{3,2,1,0:T(1,128)} async-done(((f32[128,25,1,128]{3,2,1,0:T(1,128)}), f32[128,25,1,128]{3,2,1,0:T(1,128)}, u32[]{:S(2)}, u32[]{:S(2)}) %all-to-all-start) | async-done | bytes 1638432 | tf_op jit(solution)/shard_map/all_to_all | solution.py:534
  62.9 15.5 %sample.1 = (f32[1536,128]{1,0:T(8,128)}, f32[3072,128]{1,0:T(8,128)}) custom-call(f32[3200,128]{1,0:T(8,128)} %bitcast.4.rows, f32[9344,128]{1,0:T(8,128)} %copy-done), custom_call_target="tpu_custom_call" | custom-call | flops 300000000 | bytes 9000000 | tf_op jit(solution)/shard_map/sample/pallas_call | solution.py:446
  78.5 3.7 %all-to-all-start.1 = ((f32[128,3,4,128]{3,2,1,0:T(4,128)}), f32[128,3,4,128]{3,2,1,0:T(4,128)S(1)}, u32[]{:S(2)}, u32[]{:S(2)}) async-start(f32[128,3,4,128]{3,2,1,0:T(4,128)} %bitcast.16), calls=%async_computation.1 | async-start | bytes 1572864 | tf_op jit(solution)/shard_map/all_to_all | solution.py:534
  82.2 12.6 %deposit.1 = f32[3072,128]{1,0:T(8,128)} custom-call(f32[3200,128]{1,0:T(8,128)} %bitcast.4.rows, f32[3072,128]{1,0:T(8,128)} %get-tuple-element.18.before), custom_call_target="tpu_custom_call" | custom-call | flops 300000000 | bytes 40000000 | tf_op jit(solution)/shard_map/deposit/pallas_call | solution.py:479
  94.8 4.5 %all-to-all-done.1 = f32[128,3,4,128]{3,2,1,0:T(4,128)S(1)} async-done(((f32[128,3,4,128]{3,2,1,0:T(4,128)}), f32[128,3,4,128]{3,2,1,0:T(4,128)S(1)}, u32[]{:S(2)}, u32[]{:S(2)}) %all-to-all-start.1) | async-done | bytes 786464 | tf_op jit(solution)/shard_map/all_to_all | solution.py:534
  99.2 2.1 %unpack.1 = f32[2,3,128,128]{3,2,1,0:T(8,128)} custom-call(s32[256]{0:T(256)S(1)} %copy-done.13, f32[1536,128]{1,0:T(8,128)S(1)} %bitcast.13), custom_call_target="tpu_custom_call" | custom-call | flops 1000000 | bytes 2000000 | tf_op jit(solution)/shard_map/unpack/pallas_call | solution.py:511
  (23 shorter events, 0.0 us)
Async XLA Ops:
  3.4 17.3 %collective-permute-start = (f32[960,128]{1,0:T(8,128)}, f32[960,128]{1,0:T(8,128)S(1)}, u32[]{:S(2)}, u32[]{:S(2)}) collective-permute-start(f32[960,128]{1,0:T(8,128)} %get-tuple-element.13), channel_id=1, source_target_pairs={{0,4},{4,8},{8,12},{12,16},{16,20},{20,24},{24,28},{28,32},{32,36}... | collective-permute-start | bytes 1474568 | tf_op jit(solution)/shard_map/ppermute | solution.py:530
  8.3 12.3 %collective-permute-start.1 = (f32[960,128]{1,0:T(8,128)}, f32[960,128]{1,0:T(8,128)S(1)}, u32[]{:S(2)}, u32[]{:S(2)}) collective-permute-start(f32[960,128]{1,0:T(8,128)} %get-tuple-element.14), channel_id=1, source_target_pairs={{4,0},{8,4},{12,8},{16,12},{20,16},{24,20},{28,24},{32,28},{36,32}... | collective-permute-start | bytes 1474568 | tf_op jit(solution)/shard_map/ppermute | solution.py:530
  10.2 7.6 %collective-permute-start.2 = (f32[384,128]{1,0:T(8,128)}, f32[384,128]{1,0:T(8,128)S(1)}, u32[]{:S(2)}, u32[]{:S(2)}) collective-permute-start(f32[384,128]{1,0:T(8,128)} %get-tuple-element.15), channel_id=1, source_target_pairs={{0,1},{1,2},{2,3},{4,5},{5,6},{6,7},{8,9},{9,10},{10,11},{12,13},{... | collective-permute-start | bytes 589832 | tf_op jit(solution)/shard_map/ppermute | solution.py:530
  13.5 7.2 %collective-permute-start.3 = (f32[384,128]{1,0:T(8,128)}, f32[384,128]{1,0:T(8,128)S(1)}, u32[]{:S(2)}, u32[]{:S(2)}) collective-permute-start(f32[384,128]{1,0:T(8,128)} %get-tuple-element.16), channel_id=1, source_target_pairs={{1,0},{2,1},{3,2},{5,4},{6,5},{7,6},{9,8},{10,9},{11,10},{13,12},{... | collective-permute-start | bytes 589832 | tf_op jit(solution)/shard_map/ppermute | solution.py:530
  17.8 2.8 %copy-start.6 = (f32[384,128]{1,0:T(8,128)}, f32[384,128]{1,0:T(8,128)S(1)}, u32[]{:S(2)}) copy-start(f32[384,128]{1,0:T(8,128)S(1)} %collective-permute-done.2.a2.zb) | copy-start | bytes 589828
  20.6 0.7 copy-start.8
  20.6 0.8 copy-start.2
  20.7 1.0 copy-start.4
  21.7 15.5 %copy-start.11 = (bf16[768,128]{1,0:T(8,128)(2,1)S(1)}, bf16[768,128]{1,0:T(8,128)(2,1)}, u32[]{:S(2)}) copy-start(bf16[768,128]{1,0:T(8,128)(2,1)} %constant.6.clone.mx) | copy-start | bytes 589828
  25.2 12.0 %copy-start.1 = (f32[4,16,16,3,128]{4,2,3,1,0:T(8,128)S(1)}, f32[4,16,16,3,128]{4,2,3,1,0:T(8,128)}, u32[]{:S(2)}) copy-start(f32[4,16,16,3,128]{4,2,3,1,0:T(8,128)} %param.14) | copy-start | bytes 4718596
  25.2 12.0 %copy-start.3 = (f32[960,128]{1,0:T(8,128)S(1)}, f32[960,128]{1,0:T(8,128)}, u32[]{:S(2)}) copy-start(f32[960,128]{1,0:T(8,128)} %copy-done.2) | copy-start | bytes 1474564
  25.2 12.0 %copy-start.5 = (f32[960,128]{1,0:T(8,128)S(1)}, f32[960,128]{1,0:T(8,128)}, u32[]{:S(2)}) copy-start(f32[960,128]{1,0:T(8,128)} %copy-done.4) | copy-start | bytes 1474564
  25.2 12.0 %copy-start.7 = (f32[384,128]{1,0:T(8,128)S(1)}, f32[384,128]{1,0:T(8,128)}, u32[]{:S(2)}) copy-start(f32[384,128]{1,0:T(8,128)} %copy-done.6) | copy-start | bytes 589828
  25.2 12.0 %copy-start.9 = (f32[384,128]{1,0:T(8,128)S(1)}, f32[384,128]{1,0:T(8,128)}, u32[]{:S(2)}) copy-start(f32[384,128]{1,0:T(8,128)} %copy-done.8) | copy-start | bytes 589828
  25.2 12.0 %copy-start.10 = (bf16[768,128]{1,0:T(8,128)(2,1)S(1)}, bf16[768,128]{1,0:T(8,128)(2,1)}, u32[]{:S(2)}) copy-start(bf16[768,128]{1,0:T(8,128)(2,1)} %constant.7.clone.my) | copy-start | bytes 589828
  25.3 12.0 %copy-start.12 = (bf16[512,128]{1,0:T(8,128)(2,1)S(1)}, bf16[512,128]{1,0:T(8,128)(2,1)}, u32[]{:S(2)}) copy-start(bf16[512,128]{1,0:T(8,128)(2,1)} %constant.8.clone.mz) | copy-start | bytes 393220
  25.3 37.7 %all-to-all-start = ((f32[128,25,1,128]{3,2,1,0:T(1,128)}), f32[128,25,1,128]{3,2,1,0:T(1,128)}, u32[]{:S(2)}, u32[]{:S(2)}) async-start(f32[128,25,1,128]{3,2,1,0:T(1,128)} %bitcast.14), calls=%async_computation | async-start | bytes 3276800 | tf_op jit(solution)/shard_map/all_to_all | solution.py:534
  42.0 2.2 %copy-start = (f32[9344,128]{1,0:T(8,128)}, f32[9344,128]{1,0:T(8,128)S(1)}, u32[]{:S(2)}) copy-start(f32[9344,128]{1,0:T(8,128)S(1)} %gradient.1.grads) | copy-start | bytes 14352388
  78.5 20.8 %all-to-all-start.1 = ((f32[128,3,4,128]{3,2,1,0:T(4,128)}), f32[128,3,4,128]{3,2,1,0:T(4,128)S(1)}, u32[]{:S(2)}, u32[]{:S(2)}) async-start(f32[128,3,4,128]{3,2,1,0:T(4,128)} %bitcast.16), calls=%async_computation.1 | async-start | bytes 1572864 | tf_op jit(solution)/shard_map/all_to_all | solution.py:534
  82.2 17.1 %copy-start.13 = (s32[256]{0:T(256)S(1)}, s32[256]{0:T(256)}, u32[]{:S(2)}) copy-start(s32[256]{0:T(256)} %get-tuple-element.11.places) | copy-start | bytes 3076
